TPU v7x, 32 devices: a whole 2x2x4 slice. The times are simulated.
32 devices in a mesh: dp: 4 (over z), ctx: 2 (over y), tensor: 4 (over x, core).
Axes of the slice: x: 2, y: 2, z: 4, core: 2. Of those that a mesh axis runs over, the one named last changes fastest.
Arguments:
- tokens: bfloat16 [8, 2048, 768], P('dp', ('ctx', 'tensor')), may hold values from -6 to 6
- cotangent: bfloat16 [8, 2048, 768], P('dp', 'ctx'), may hold values from -6 to 6
- stretch_order: int32 [8, 4], P('dp'), may hold values from 0 to 3, each once within a row
- attn_gain: bfloat16 [768], P(('dp', 'ctx')), may hold values from 0.5 to 1.5
- attn_shift: bfloat16 [768], P(('dp', 'ctx')), may hold values from -2 to 2
- heads_weight: bfloat16 [3, 768, 768], P(None, ('dp', 'ctx'), 'tensor'), may hold values from -0.21875 to 0.21875
- heads_bias: bfloat16 [2, 768], P(None, ('dp', 'ctx')), may hold values from -0.59765625 to 0.59765625
- merge_weight: bfloat16 [768, 768], P('tensor', ('dp', 'ctx')), may hold values from -1.75 to 1.75
- merge_bias: bfloat16 [768], P(('dp', 'ctx')), may hold values from -3 to 3
- feed_gain: bfloat16 [768], P(('dp', 'ctx')), may hold values from 0.5 to 1.5
- feed_shift: bfloat16 [768], P(('dp', 'ctx')), may hold values from -2 to 2
- up_weight: bfloat16 [768, 3072], P(('dp', 'ctx'), 'tensor'), may hold values from -0.21875 to 0.21875
- up_bias: bfloat16 [3072], P(('dp', 'ctx')), may hold values from -2 to 2
- down_weight: bfloat16 [3072, 768], P('tensor', ('dp', 'ctx')), may hold values from -0.109375 to 0.109375
- down_bias: bfloat16 [768], P(('dp', 'ctx')), may hold values from -3 to 3
Outputs:
- block_out: bfloat16 [8, 2048, 768], P('dp', ('ctx', 'tensor'))
- tokens_grad: float32 [8, 2048, 768], P('dp', ('ctx', 'tensor'))
- attn_gain_grad: float32 [768], P(('dp', 'ctx'))
- attn_shift_grad: float32 [768], P(('dp', 'ctx'))
- heads_weight_grad: float32 [3, 768, 768], P(None, ('dp', 'ctx'), 'tensor')
- heads_bias_grad: float32 [2, 768], P(None, ('dp', 'ctx'))
- merge_weight_grad: float32 [768, 768], P('tensor', ('dp', 'ctx'))
- merge_bias_grad: float32 [768], P(('dp', 'ctx'))
- feed_gain_grad: float32 [768], P(('dp', 'ctx'))
- feed_shift_grad: float32 [768], P(('dp', 'ctx'))
- up_weight_grad: float32 [768, 3072], P(('dp', 'ctx'), 'tensor')
- up_bias_grad: float32 [3072], P(('dp', 'ctx'))
- down_weight_grad: float32 [3072, 768], P('tensor', ('dp', 'ctx'))
- down_bias_grad: float32 [768], P(('dp', 'ctx'))
Inputs may be any that keep to these rules, and one draw needn't show every extreme that they name: Each row of stretch_order is a permutation of the 4 stretch numbers; the tokens of stored stretch k of sequence s stand at positions stretch_order[s, k] * 512 and onward.
All inputs are finite; a program needn't handle non-finite values.
Results may differ from a plain program's by a relative error of at most 0.023.
Values may be sent and summed in bfloat16 or wider, within the bound.
No kernel may reach another device: no remote copies, remote signals or barrier semaphores. Data moves between devices by JAX's collectives and lax.ppermute only.
A program may use at most 192 MiB of HBM per device.

v0:
```python
import jax
import jax.numpy as jnp
from jax import lax
from jax.sharding import PartitionSpec as P

HEAD_DIM = 64


EPS = 1e-05
GELU_C = 0.7978845608028654
NEG = -1e30


def shifted(block, axis, distance):
    devices = range(lax.axis_size(axis))
    route = [((i - distance) % len(devices), i) for i in devices]
    return lax.ppermute(block, axis, route)


def layer_stats(rows):
    centred = rows - jnp.mean(rows, axis=-1, keepdims=True)
    inv_std = lax.rsqrt(jnp.mean(centred * centred, axis=-1, keepdims=True) + EPS)
    return (centred * inv_std, inv_std)


def norm_back(grad_out, normed, inv_std, gain):
    scaled = grad_out * gain
    return inv_std * (
        scaled
        - jnp.mean(scaled, axis=-1, keepdims=True)
        - normed * jnp.mean(scaled * normed, axis=-1, keepdims=True)
    )


def smooth_gelu(values):
    return 0.5 * values * (1.0 + jnp.tanh(GELU_C * (values + 0.044715 * values * values * values)))


def smooth_slope(values):
    tangent = jnp.tanh(GELU_C * (values + 0.044715 * values * values * values))
    return 0.5 * (1.0 + tangent) + 0.5 * values * (1.0 - tangent * tangent) * GELU_C * (
        1.0 + 3.0 * 0.044715 * values * values
    )


def key_positions(order_table, first_row, row_count, stretch_len):
    row_index = first_row + jnp.arange(row_count, dtype=jnp.int32)
    stretch_index = row_index // stretch_len
    choose = (
        stretch_index[:, None] == jnp.arange(order_table.shape[1], dtype=jnp.int32)[None, :]
    ).astype(jnp.int32)
    stretch_first = jnp.sum(choose[:, None, :] * order_table[None, :, :], axis=-1)
    return stretch_first * stretch_len + (row_index % stretch_len)[:, None]


def attend_block(carry_state, query_heads, query_pos, keys_blk, values_blk, key_pos):
    maxima, totals, running = carry_state
    key_heads = keys_blk.reshape(keys_blk.shape[:2] + query_heads.shape[2:])
    value_heads = values_blk.reshape(values_blk.shape[:2] + query_heads.shape[2:])
    scores = jnp.einsum(
        "qshe,kshe->shqk", query_heads, key_heads, preferred_element_type=jnp.float32
    ) * HEAD_DIM ** (-0.5)
    allowed = key_pos.T[:, None, None, :] <= query_pos.T[:, None, :, None]
    scores = jnp.where(allowed, scores, NEG)
    new_max = jnp.maximum(maxima, jnp.max(scores, axis=-1))
    factor = jnp.exp(maxima - new_max)
    weights = jnp.where(allowed, jnp.exp(scores - new_max[..., None]), 0.0)
    totals = totals * factor + jnp.sum(weights, axis=-1)
    running = running * factor[..., None] + jnp.einsum(
        "shqk,kshe->shqe",
        weights.astype(jnp.bfloat16),
        value_heads,
        preferred_element_type=jnp.float32,
    )
    return (new_max, totals, running)


def attend_back(
    query_heads, grad_heads, log_total, row_dots, query_pos, keys_blk, values_blk, key_pos
):
    key_heads = keys_blk.reshape(keys_blk.shape[:2] + query_heads.shape[2:])
    value_heads = values_blk.reshape(values_blk.shape[:2] + query_heads.shape[2:])
    scale = HEAD_DIM ** (-0.5)
    scores = (
        jnp.einsum("qshe,kshe->shqk", query_heads, key_heads, preferred_element_type=jnp.float32)
        * scale
    )
    allowed = key_pos.T[:, None, None, :] <= query_pos.T[:, None, :, None]
    probs = jnp.where(allowed, jnp.exp(scores - log_total[..., None]), 0.0)
    grad_values = jnp.einsum(
        "shqk,qshe->kshe",
        probs.astype(jnp.bfloat16),
        grad_heads,
        preferred_element_type=jnp.float32,
    )
    grad_probs = jnp.einsum(
        "qshe,kshe->shqk", grad_heads, value_heads, preferred_element_type=jnp.float32
    )
    grad_scores = (probs * (grad_probs - row_dots[..., None]) * scale).astype(jnp.bfloat16)
    grad_query = jnp.einsum(
        "shqk,kshe->qshe", grad_scores, key_heads, preferred_element_type=jnp.float32
    )
    grad_keys = jnp.einsum(
        "shqk,qshe->kshe", grad_scores, query_heads, preferred_element_type=jnp.float32
    )
    return (grad_query, grad_keys, grad_values)


def over_blocks(carry_state, pieces, block_rows, piece_fn):
    row_count = pieces[0].shape[0]
    blocks = row_count // block_rows
    split_parts = tuple(
        (member.reshape((blocks, block_rows) + member.shape[1:]) for member in pieces)
    )

    def inner_step(state_in, block_item):
        block_index, parts = block_item
        return (piece_fn(state_in, parts, block_index * block_rows), None)

    carry_state, unused = lax.scan(
        inner_step, carry_state, (jnp.arange(blocks, dtype=jnp.int32), split_parts)
    )
    return carry_state


def local(
    tokens,
    cotangent,
    stretch_order,
    attn_gain,
    attn_shift,
    heads_weight,
    heads_bias,
    merge_weight,
    merge_bias,
    feed_gain,
    feed_shift,
    up_weight,
    up_bias,
    down_weight,
    down_bias,
):
    tensor_pos = lax.axis_index("tensor")
    ctx_size = lax.axis_size("ctx")
    ctx_pos = lax.axis_index("ctx")
    (
        gain_one,
        shift_one,
        w_heads,
        b_heads,
        w_merge,
        b_merge,
        gain_two,
        shift_two,
        w_up,
        b_up,
        w_down,
        b_down,
    ) = (
        lax.all_gather(attn_gain, ("dp", "ctx"), axis=0, tiled=True),
        lax.all_gather(attn_shift, ("dp", "ctx"), axis=0, tiled=True),
        lax.all_gather(heads_weight, ("dp", "ctx"), axis=1, tiled=True),
        lax.all_gather(heads_bias, ("dp", "ctx"), axis=1, tiled=True),
        lax.all_gather(merge_weight, ("dp", "ctx"), axis=1, tiled=True),
        lax.all_gather(merge_bias, ("dp", "ctx"), axis=0, tiled=True),
        lax.all_gather(feed_gain, ("dp", "ctx"), axis=0, tiled=True),
        lax.all_gather(feed_shift, ("dp", "ctx"), axis=0, tiled=True),
        lax.all_gather(up_weight, ("dp", "ctx"), axis=0, tiled=True),
        lax.all_gather(up_bias, ("dp", "ctx"), axis=0, tiled=True),
        lax.all_gather(down_weight, ("dp", "ctx"), axis=1, tiled=True),
        lax.all_gather(down_bias, ("dp", "ctx"), axis=0, tiled=True),
    )
    model_width = gain_one.shape[0]
    local_width = w_heads.shape[2]
    head_count = local_width // HEAD_DIM
    hidden_local = w_up.shape[1]
    hidden_all = b_up.shape[0]
    bias_heads = lax.dynamic_slice_in_dim(b_heads, tensor_pos * local_width, local_width, 1).astype(
        jnp.float32
    )
    bias_hidden = lax.dynamic_slice_in_dim(b_up, tensor_pos * hidden_local, hidden_local, 0).astype(
        jnp.float32
    )
    rows_in = jnp.swapaxes(tokens, 0, 1).astype(jnp.float32)
    own_rows = rows_in.shape[0]
    seq_count = rows_in.shape[1]
    normed_one, inv_one = layer_stats(rows_in)
    norm_out_one = (
        normed_one * gain_one.astype(jnp.float32) + shift_one.astype(jnp.float32)
    ).astype(jnp.bfloat16)
    full_one = lax.all_gather(norm_out_one, "tensor", axis=0, tiled=True)
    span_rows = full_one.shape[0]
    stretch_len = span_rows // 2
    projected = jnp.einsum("rsd,jde->jrse", full_one, w_heads, preferred_element_type=jnp.float32)
    queries = (projected[0] + bias_heads[0]).astype(jnp.bfloat16)
    keys_low = projected[1].astype(jnp.bfloat16)
    values_low = (projected[2] + bias_heads[1]).astype(jnp.bfloat16)
    query_heads = queries.reshape(span_rows, seq_count, head_count, HEAD_DIM)
    query_pos = key_positions(stretch_order, ctx_pos * span_rows, span_rows, stretch_len)

    def attend_piece(carry_state, pieces, first_row):
        key_pos = key_positions(stretch_order, first_row, pieces[0].shape[0], stretch_len)
        return attend_block(carry_state, query_heads, query_pos, pieces[0], pieces[1], key_pos)

    stat_shape = (seq_count, head_count, span_rows)
    initial = (
        jnp.full(stat_shape, NEG, jnp.float32),
        jnp.zeros(stat_shape, jnp.float32),
        jnp.zeros(stat_shape + (HEAD_DIM,), jnp.float32),
    )
    maxima, totals, running = over_blocks(
        initial,
        (
            lax.all_gather(keys_low, "ctx", axis=0, tiled=True),
            lax.all_gather(values_low, "ctx", axis=0, tiled=True),
        ),
        span_rows,
        attend_piece,
    )
    attended32 = running / totals[..., None]
    log_total = maxima + jnp.log(totals)
    heads_out = (
        jnp.transpose(attended32, (2, 0, 1, 3))
        .reshape(span_rows, seq_count, local_width)
        .astype(jnp.bfloat16)
    )
    member = heads_out
    merged = lax.psum_scatter(
        jnp.einsum("rsh,hd->rsd", member, w_merge, preferred_element_type=jnp.float32).astype(
            jnp.bfloat16
        ),
        "tensor",
        scatter_dimension=0,
        tiled=True,
    ).astype(jnp.float32)
    resid = rows_in + merged + b_merge.astype(jnp.float32)
    normed_two, inv_two = layer_stats(resid)
    norm_out_two = (
        normed_two * gain_two.astype(jnp.float32) + shift_two.astype(jnp.float32)
    ).astype(jnp.bfloat16)
    full_two = lax.all_gather(norm_out_two, "tensor", axis=0, tiled=True)
    pre_act = (
        jnp.einsum("rsd,df->rsf", full_two, w_up, preferred_element_type=jnp.float32) + bias_hidden
    )
    activ = smooth_gelu(pre_act).astype(jnp.bfloat16)
    member = activ
    mixed = lax.psum_scatter(
        jnp.einsum("rsf,fd->rsd", member, w_down, preferred_element_type=jnp.float32).astype(
            jnp.bfloat16
        ),
        "tensor",
        scatter_dimension=0,
        tiled=True,
    ).astype(jnp.float32)
    block_rows = resid + mixed + b_down.astype(jnp.float32)
    block_out = jnp.swapaxes(block_rows, 0, 1).astype(jnp.bfloat16)
    grad_full = jnp.swapaxes(cotangent, 0, 1)
    grad_down_bias = jnp.sum(grad_full, axis=(0, 1), dtype=jnp.float32)
    grad_down_w = jnp.einsum("rsf,rsd->fd", activ, grad_full, preferred_element_type=jnp.float32)
    grad_pre = jnp.einsum(
        "rsd,fd->rsf", grad_full, w_down, preferred_element_type=jnp.float32
    ) * smooth_slope(pre_act)
    grad_up_bias = jnp.sum(grad_pre, axis=(0, 1))
    grad_pre_low = grad_pre.astype(jnp.bfloat16)
    grad_up_w = jnp.einsum(
        "rsd,rsf->df", full_two, grad_pre_low, preferred_element_type=jnp.float32
    )
    member = grad_pre_low
    grad_norm_two = lax.psum_scatter(
        jnp.einsum("rsf,df->rsd", member, w_up, preferred_element_type=jnp.float32).astype(
            jnp.bfloat16
        ),
        "tensor",
        scatter_dimension=0,
        tiled=True,
    ).astype(jnp.float32)
    gain_two_part = jnp.sum(grad_norm_two * normed_two, axis=(0, 1))
    shift_two_part = jnp.sum(grad_norm_two, axis=(0, 1))
    own_grad = lax.dynamic_slice_in_dim(grad_full, tensor_pos * own_rows, own_rows, 0).astype(
        jnp.float32
    )
    grad_resid = own_grad + norm_back(
        grad_norm_two, normed_two, inv_two, gain_two.astype(jnp.float32)
    )
    merge_bias_part = jnp.sum(grad_resid, axis=(0, 1))
    grad_resid_full = lax.all_gather(grad_resid.astype(jnp.bfloat16), "tensor", axis=0, tiled=True)
    grad_merge_w = jnp.einsum(
        "rsh,rsd->hd", heads_out, grad_resid_full, preferred_element_type=jnp.float32
    )
    grad_joined = jnp.einsum(
        "rsd,hd->rsh", grad_resid_full, w_merge, preferred_element_type=jnp.float32
    ).astype(jnp.bfloat16)
    grad_heads = grad_joined.reshape(span_rows, seq_count, head_count, HEAD_DIM)
    row_dots = jnp.einsum("qshe,shqe->shq", grad_heads.astype(jnp.float32), attended32)

    def back_piece(keys_blk, values_blk, first_row):
        key_pos = key_positions(stretch_order, first_row, keys_blk.shape[0], stretch_len)
        return attend_back(
            query_heads, grad_heads, log_total, row_dots, query_pos, keys_blk, values_blk, key_pos
        )

    zero_query = jnp.zeros((span_rows, seq_count, head_count, HEAD_DIM), jnp.float32)
    zero_rows = jnp.zeros((span_rows, seq_count, local_width), jnp.float32)

    def cycle_turn(turn_index, carry_state):
        grad_query, moving_keys, moving_values, sum_keys, sum_values = carry_state
        source = (ctx_pos - turn_index) % ctx_size
        part_query, part_keys, part_values = back_piece(
            moving_keys, moving_values, source * span_rows
        )
        sum_keys = sum_keys + part_keys.reshape(span_rows, seq_count, local_width)
        sum_values = sum_values + part_values.reshape(span_rows, seq_count, local_width)
        moving_keys, moving_values = shifted((moving_keys, moving_values), "ctx", 1)
        sum_keys, sum_values = (
            shifted(sum_keys.astype(jnp.bfloat16), "ctx", 1).astype(sum_keys.dtype),
            shifted(sum_values.astype(jnp.bfloat16), "ctx", 1).astype(sum_values.dtype),
        )
        return (grad_query + part_query, moving_keys, moving_values, sum_keys, sum_values)

    grad_query, unused_keys, unused_values, grad_keys, grad_values = lax.fori_loop(
        0, ctx_size, cycle_turn, (zero_query, keys_low, values_low, zero_rows, zero_rows)
    )
    grad_query = grad_query.reshape(span_rows, seq_count, local_width)
    bias_pair = jnp.stack([jnp.sum(grad_query, axis=(0, 1)), jnp.sum(grad_values, axis=(0, 1))])
    heads_bias_pad = lax.dynamic_update_slice(
        jnp.zeros((2, model_width), jnp.float32), bias_pair, (0, tensor_pos * local_width)
    )
    grad_stack = jnp.stack([grad_query, grad_keys, grad_values]).astype(jnp.bfloat16)
    grad_heads_w = jnp.einsum(
        "rsd,jrse->jde", full_one, grad_stack, preferred_element_type=jnp.float32
    )
    member = grad_stack
    grad_norm_one = lax.psum_scatter(
        jnp.einsum("jrse,jde->rsd", member, w_heads, preferred_element_type=jnp.float32).astype(
            jnp.bfloat16
        ),
        "tensor",
        scatter_dimension=0,
        tiled=True,
    ).astype(jnp.float32)
    gain_one_part = jnp.sum(grad_norm_one * normed_one, axis=(0, 1))
    shift_one_part = jnp.sum(grad_norm_one, axis=(0, 1))
    tokens_rows = grad_resid + norm_back(
        grad_norm_one, normed_one, inv_one, gain_one.astype(jnp.float32)
    )
    up_bias_pad = lax.dynamic_update_slice(
        jnp.zeros((hidden_all,), jnp.float32), grad_up_bias, (tensor_pos * hidden_local,)
    )
    summed = (
        lax.psum(gain_one_part.astype(jnp.bfloat16), "tensor").astype(jnp.float32),
        lax.psum(shift_one_part.astype(jnp.bfloat16), "tensor").astype(jnp.float32),
        lax.psum(heads_bias_pad.astype(jnp.bfloat16), "tensor").astype(jnp.float32),
        lax.psum(merge_bias_part.astype(jnp.bfloat16), "tensor").astype(jnp.float32),
        lax.psum(gain_two_part.astype(jnp.bfloat16), "tensor").astype(jnp.float32),
        lax.psum(shift_two_part.astype(jnp.bfloat16), "tensor").astype(jnp.float32),
        lax.psum(up_bias_pad.astype(jnp.bfloat16), "tensor").astype(jnp.float32),
    )
    grads = (
        lax.psum_scatter(summed[0], ("dp", "ctx"), scatter_dimension=0, tiled=True),
        lax.psum_scatter(summed[1], ("dp", "ctx"), scatter_dimension=0, tiled=True),
        lax.psum_scatter(grad_heads_w, ("dp", "ctx"), scatter_dimension=1, tiled=True),
        lax.psum_scatter(summed[2], ("dp", "ctx"), scatter_dimension=1, tiled=True),
        lax.psum_scatter(grad_merge_w, ("dp", "ctx"), scatter_dimension=1, tiled=True),
        lax.psum_scatter(summed[3], ("dp", "ctx"), scatter_dimension=0, tiled=True),
        lax.psum_scatter(summed[4], ("dp", "ctx"), scatter_dimension=0, tiled=True),
        lax.psum_scatter(summed[5], ("dp", "ctx"), scatter_dimension=0, tiled=True),
        lax.psum_scatter(grad_up_w, ("dp", "ctx"), scatter_dimension=0, tiled=True),
        lax.psum_scatter(summed[6], ("dp", "ctx"), scatter_dimension=0, tiled=True),
        lax.psum_scatter(grad_down_w, ("dp", "ctx"), scatter_dimension=1, tiled=True),
        lax.psum_scatter(grad_down_bias, ("dp", "ctx"), scatter_dimension=0, tiled=True),
    )
    tokens_grad = jnp.swapaxes(tokens_rows, 0, 1)
    return (
        block_out,
        tokens_grad,
        grads[0],
        grads[1],
        grads[2],
        grads[3],
        grads[4],
        grads[5],
        grads[6],
        grads[7],
        grads[8],
        grads[9],
        grads[10],
        grads[11],
    )


def solution(mesh):
    in_specs = (
        P("dp", ("ctx", "tensor"), None),
        P("dp", "ctx", None),
        P("dp", None),
        P(("dp", "ctx")),
        P(("dp", "ctx")),
        P(None, ("dp", "ctx"), "tensor"),
        P(None, ("dp", "ctx")),
        P("tensor", ("dp", "ctx")),
        P(("dp", "ctx")),
        P(("dp", "ctx")),
        P(("dp", "ctx")),
        P(("dp", "ctx"), "tensor"),
        P(("dp", "ctx")),
        P("tensor", ("dp", "ctx")),
        P(("dp", "ctx")),
    )
    out_specs = (
        P("dp", ("ctx", "tensor"), None),
        P("dp", ("ctx", "tensor"), None),
        P(("dp", "ctx")),
        P(("dp", "ctx")),
        P(None, ("dp", "ctx"), "tensor"),
        P(None, ("dp", "ctx")),
        P("tensor", ("dp", "ctx")),
        P(("dp", "ctx")),
        P(("dp", "ctx")),
        P(("dp", "ctx")),
        P(("dp", "ctx"), "tensor"),
        P(("dp", "ctx")),
        P("tensor", ("dp", "ctx")),
        P(("dp", "ctx")),
    )
    return jax.shard_map(local, mesh=mesh, in_specs=in_specs, out_specs=out_specs, check_vma=False)
```

profile of v0, /device:TPU:0, one launch (start us, length us, event | category | flops | bytes accessed | tf_op | source)
XLA Modules:
  0.0 1073.1 jit_solution(5069692116035231689)
XLA Ops:
  13.8 38.8 %all-reduce.14 = (bf16[768]{0:T(1024)(128)(2,1)}, bf16[768]{0:T(1024)(128)(2,1)}, bf16[768]{0:T(1024)(128)(2,1)}, bf16[768]{0:T(1024)(128)(2,1)S(1)}, bf16[768]{0:T(1024)(128)(2,1)S(1)}, /*index=5*/bf16[768]{0:T(1024)(128)(2,1)}) all-reduce(bf16[768]{0:T(1024)(128)(2,1)S(1)} %dynamic-update-slice, ...), channel_id=1, replica_groups=mesh['dp'=4,'ctx'=2,'tensor'=4] {'dp','ctx'}, use_global_device_ids=true, to_apply=%add.4 | all-reduce | flops 4608 | bytes 18432
  54.6 16.5 %all-gather.1 = bf16[8,96,2]{1,2,0:T(2,128)(2,1)S(1)} all-gather(bf16[1,96,2]{1,2,0:T(2,128)(2,1)S(1)} %bitcast.302), channel_id=1, replica_groups=mesh['dp'=4,'ctx'=2,'tensor'=4] {'dp','ctx'}, dimensions={0}, use_global_device_ids=true | all-gather | bytes 3456 | tf_op jit(solution)/shard_map/all_gather | solution.py:163
  71.3 35.0 %all_gather.54 = bf16[3,768,192]{2,0,1:T(4,128)(2,1)S(1)} all-gather(bf16[3,96,192]{2,0,1:T(4,128)(2,1)S(1)} %copy.62), channel_id=1, replica_groups=mesh['dp'=4,'ctx'=2,'tensor'=4] {'dp','ctx'}, dimensions={1}, use_global_device_ids=true | all-gather | bytes 995328 | tf_op jit(solution)/shard_map/all_gather | solution.py:162
  107.3 3.9 fusion.49
  117.5 33.7 %all_gather.58 = bf16[192,768]{0,1:T(8,128)(2,1)} all-gather(bf16[192,96]{0,1:T(8,128)(2,1)S(1)} %copy.67), channel_id=1, replica_groups=mesh['dp'=4,'ctx'=2,'tensor'=4] {'dp','ctx'}, dimensions={1}, use_global_device_ids=true | all-gather | bytes 331776 | tf_op jit(solution)/shard_map/all_gather | solution.py:164
  154.6 19.0 %all-gather.23.cloned.1.call-done = bf16[1,2048,2,192]{1,3,0,2:T(8,128)(2,1)} async-done(((bf16[1,1024,2,192]{1,3,0,2:T(8,128)(2,1)}), bf16[1,2048,2,192]{1,3,0,2:T(8,128)(2,1)}) %all-gather.23.cloned.1.call-update) | async-done | bytes 1572880 | tf_op jit(solution)/shard_map/all_gather | solution.py:214
  180.5 80.3 %while.42 = (s32[]{:T(128)}, f32[2,3,1024]{2,1,0:T(4,128)S(1)}, f32[2,3,1024]{2,1,0:T(4,128)S(1)}, f32[2,3,1024,64]{2,3,1,0:T(8,128)}, s32[2]{0:T(128)S(1)}, /*i...) while((s32[]{:T(128)}, f32[2,3,1024]{2,1,0:T(4,128)S(1)}, ...), condition=%wide.region_7.8_spmd.clone, body=%wide.region_3.7_spmd.clone.sunk | while | flops 1695756288 | bytes 105603336 | solution.py:120
  184.5 10.9 %fusion.168 = (f32[2,3,1024]{2,1,0:T(4,128)S(1)}, f32[2,3,1024,1024]{3,2,1,0:T(8,128)}) fusion(pred[2,1024,1024]{1,2,0:T(8,128)(4,1)S(1)} %broadcast_compare_fusion.4, bf16[1024,2,3,64]{0,3,2,1:T(8,128)(2,1)S(1)} %bitcast.282, bf16[1024,2,3,64]{0,3,2,1:T(8,128)(2,1)S(1)} %get-tuple-element.971), kind=kOutput, calls=%fused_computation.2.clone.1 | convolution fusion | flops 824174592 | bytes 28860416 | tf_op jit(solution)/shard_map/while/body/eval_jaxpr/qshe,kshe->shqk/dot_general | solution.py:60
  195.4 11.7 %fusion.169 = f32[2,3,1024]{2,1,0:T(4,128)S(1)} fusion(f32[2,3,1024,1024]{3,2,1,0:T(8,128)} %get-tuple-element.918, f32[2,3,1024]{2,1,0:T(4,128)S(1)} %select_maximum_fusion.2, pred[2,1024,1024]{1,2,0:T(8,128)(4,1)S(1)} %broadcast_compare_fusion.4), kind=kLoop, calls=%fused_computation.4.clone.1 | loop fusion | flops 31451136 | bytes 27312128 | tf_op jit(solution)/shard_map/while/body/eval_jaxpr/reduce_sum | solution.py:68
  207.2 12.3 %fusion.171 = f32[2,3,1024,64]{2,3,1,0:T(8,128)S(1)} fusion(f32[2,3,1024,64]{2,3,1,0:T(8,128)S(1)} %copy-done.14, bf16[1024,2,3,64]{0,3,2,1:T(8,128)(2,1)S(1)} %bitcast.283, f32[2,3,1024,1024]{3,2,1,0:T(8,128)} %get-tuple-element.918, f32[2,3,1024]{2,1,0:T(4,128)S(1)} %select_maximum_fusion.2, ...), kind=kOutput, calls=%fused_computation.9.clone.1 | convolution fusion | flops 837943296 | bytes 31244288 | tf_op jit(solution)/shard_map/while/body/eval_jaxpr/shqk,kshe->shqe/dot_general | solution.py:69
  224.7 10.9 %fusion.168 = (f32[2,3,1024]{2,1,0:T(4,128)S(1)}, f32[2,3,1024,1024]{3,2,1,0:T(8,128)}) fusion(pred[2,1024,1024]{1,2,0:T(8,128)(4,1)S(1)} %broadcast_compare_fusion.4, bf16[1024,2,3,64]{0,3,2,1:T(8,128)(2,1)S(1)} %bitcast.282, bf16[1024,2,3,64]{0,3,2,1:T(8,128)(2,1)S(1)} %get-tuple-element.971), kind=kOutput, calls=%fused_computation.2.clone.1 | convolution fusion | flops 824174592 | bytes 28860416 | tf_op jit(solution)/shard_map/while/body/eval_jaxpr/qshe,kshe->shqk/dot_general | solution.py:60
  235.6 11.7 %fusion.169 = f32[2,3,1024]{2,1,0:T(4,128)S(1)} fusion(f32[2,3,1024,1024]{3,2,1,0:T(8,128)} %get-tuple-element.918, f32[2,3,1024]{2,1,0:T(4,128)S(1)} %select_maximum_fusion.2, pred[2,1024,1024]{1,2,0:T(8,128)(4,1)S(1)} %broadcast_compare_fusion.4), kind=kLoop, calls=%fused_computation.4.clone.1 | loop fusion | flops 31451136 | bytes 27312128 | tf_op jit(solution)/shard_map/while/body/eval_jaxpr/reduce_sum | solution.py:68
  247.4 12.3 %fusion.171 = f32[2,3,1024,64]{2,3,1,0:T(8,128)S(1)} fusion(f32[2,3,1024,64]{2,3,1,0:T(8,128)S(1)} %copy-done.14, bf16[1024,2,3,64]{0,3,2,1:T(8,128)(2,1)S(1)} %bitcast.283, f32[2,3,1024,1024]{3,2,1,0:T(8,128)} %get-tuple-element.918, f32[2,3,1024]{2,1,0:T(4,128)S(1)} %select_maximum_fusion.2, ...), kind=kOutput, calls=%fused_computation.9.clone.1 | convolution fusion | flops 837943296 | bytes 31244288 | tf_op jit(solution)/shard_map/while/body/eval_jaxpr/shqk,kshe->shqe/dot_general | solution.py:69
  266.4 36.9 %reduce-scatter.16.cloned.1.call-done = bf16[256,2,768]{2,0,1:T(8,128)(2,1)} async-done(((bf16[1024,2,768]{2,0,1:T(8,128)(2,1)}), bf16[256,2,768]{2,0,1:T(8,128)(2,1)}) %reduce-scatter.16.cloned.1.call-update) | async-done | bytes 786448 | tf_op jit(solution)/shard_map/reduce_scatter | solution.py:228
  307.4 26.0 %all-gather.2 = bf16[8,1,384]{2,1,0:T(2,128)(2,1)S(1)} all-gather(bf16[1,1,384]{2,1,0:T(2,128)(2,1)S(1)} %reshape.353), channel_id=1, replica_groups=mesh['dp'=4,'ctx'=2,'tensor'=4] {'dp','ctx'}, dimensions={0}, use_global_device_ids=true | all-gather | bytes 6912 | tf_op jit(solution)/shard_map/all_gather | solution.py:169
  333.5 4.8 all-gather.15.cloned.1.call-done
  338.4 7.5 fusion.92
  345.8 36.4 %all-gather.19.cloned.1.call-done = bf16[768,768]{0,1:T(8,128)(2,1)} async-done(((bf16[768,96]{0,1:T(8,128)(2,1)}), bf16[768,768]{0,1:T(8,128)(2,1)}) %all-gather.19.cloned.1.call-update) | async-done | bytes 1179664 | tf_op jit(solution)/shard_map/all_gather | solution.py:170
  382.2 9.0 fusion.115
  392.9 4.0 convolution_convert_fusion.1
  397.0 36.3 %reduce-scatter.20.cloned.1.call-done = bf16[256,2,768]{2,0,1:T(8,128)(2,1)} async-done(((bf16[1024,2,768]{2,0,1:T(8,128)(2,1)}), bf16[256,2,768]{2,0,1:T(8,128)(2,1)}) %reduce-scatter.20.cloned.1.call-update) | async-done | bytes 786448 | tf_op jit(solution)/shard_map/reduce_scatter | solution.py:269
  440.7 26.2 %all-gather.21.cloned.1.call-done = bf16[1024,2,768]{2,0,1:T(8,128)(2,1)} async-done(((bf16[256,2,768]{2,0,1:T(8,128)(2,1)}), bf16[1024,2,768]{2,0,1:T(8,128)(2,1)}) %all-gather.21.cloned.1.call-update) | async-done | bytes 3145744 | tf_op jit(solution)/shard_map/all_gather | solution.py:286
  471.0 163.5 %while.43 = (s32[]{:T(128)}, f32[1024,2,3,64]{0,3,2,1:T(8,128)S(1)}, bf16[1024,2,192]{0,2,1:T(8,128)(2,1)}, bf16[1024,2,192]{0,2,1:T(8,128)(2,1)}, f32[1024,2,19...) while((s32[]{:T(128)}, ...), condition=%wide.region_17.18_spmd.clone, body=%wide.region_15.17_spmd.clone.sunk | while | flops 4101814272 | bytes 183927376 | solution.py:320
  478.9 10.1 fusion.182
  489.0 17.4 %multiply_convert_fusion.5 = bf16[2,3,1024,1024]{3,2,1,0:T(8,128)(2,1)} fusion(f32[2,3,1024,1024]{3,2,1,0:T(8,128)} %fusion.182, f32[2,3,1024]{2,1,0:T(4,128)S(1)} %get-tuple-element.1022, f32[2,3,1024]{2,1,0:T(4,128)S(1)} %get-tuple-element.1020, pred[2,1024,1024]{2,1,0:T(8,128)(4,1)} %broadcast_compare_fusion.5, ...), kind=kOutput, calls=%fused_computation.35.clone.1 | convolution fusion | flops 849346560 | bytes 41467904 | tf_op jit(solution)/shard_map/while/body/eval_jaxpr/qshe,kshe->shqk/dot_general | solution.py:96
  506.4 7.0 fusion.184
  516.2 10.7 fusion.186
  528.9 8.7 bitcast_add_fusion.5
  540.0 11.0 %collective-permute-done.3 = bf16[1024,2,192]{0,2,1:T(8,128)(2,1)} collective-permute-done((bf16[1024,2,192]{0,2,1:T(8,128)(2,1)}, bf16[1024,2,192]{0,2,1:T(8,128)(2,1)}, u32[]{:S(2)}, u32[]{:S(2)}) %collective-permute-start.3) | collective-permute-done | bytes 786464 | tf_op jit(solution)/shard_map/while/body/eval_jaxpr/ppermute | solution.py:17
  561.2 10.1 fusion.182
  571.3 17.4 %multiply_convert_fusion.5 = bf16[2,3,1024,1024]{3,2,1,0:T(8,128)(2,1)} fusion(f32[2,3,1024,1024]{3,2,1,0:T(8,128)} %fusion.182, f32[2,3,1024]{2,1,0:T(4,128)S(1)} %get-tuple-element.1022, f32[2,3,1024]{2,1,0:T(4,128)S(1)} %get-tuple-element.1020, pred[2,1024,1024]{2,1,0:T(8,128)(4,1)} %broadcast_compare_fusion.5, ...), kind=kOutput, calls=%fused_computation.35.clone.1 | convolution fusion | flops 849346560 | bytes 41467904 | tf_op jit(solution)/shard_map/while/body/eval_jaxpr/qshe,kshe->shqk/dot_general | solution.py:96
  588.7 7.0 fusion.184
  598.5 10.7 fusion.186
  611.2 8.7 bitcast_add_fusion.5
  622.3 9.5 collective-permute-done.3
  638.9 4.1 bitcast_convert_fusion
  648.3 6.1 fusion.85
  661.8 8.6 convolution_convert_fusion.2
  672.0 9.0 reduce-scatter.22.cloned.1.call-done
  686.1 11.1 %all-reduce.15 = (bf16[768]{0:T(1024)(128)(2,1)}, bf16[768]{0:T(1024)(128)(2,1)}, bf16[2,768]{1,0:T(2,128)(2,1)S(1)}, bf16[768]{0:T(1024)(128)(2,1)}, bf16[768]{...) all-reduce(bf16[768]{0:T(1024)(128)(2,1)S(1)} %get-tuple-element.68, ...), channel_id=1, replica_groups=mesh['dp'=4,'ctx'=2,'tensor'=4] {'tensor'}, use_global_device_ids=true, to_apply=%region_22.23 | all-reduce | flops 8448 | bytes 33792 | tf_op jit(solution)/shard_map/psum | solution.py:350
  698.2 8.6 fusion.58
  706.9 7.0 convolution_bitcast_fusion
  718.8 29.0 %reduce-scatter.32.cloned.1.call-done = f32[96,192]{1,0:T(8,128)} async-done(((f32[768,192]{1,0:T(8,128)}), f32[96,192]{1,0:T(8,128)}) %reduce-scatter.32.cloned.1.call-update) | async-done | bytes 73744
  749.4 67.7 %reduce-scatter.28.cloned.1.call-done = f32[96,576]{1,0:T(8,128)} async-done(((f32[768,576]{1,0:T(8,128)}), f32[96,576]{1,0:T(8,128)}) %reduce-scatter.28.cloned.1.call-update) | async-done | bytes 221200
  819.0 35.9 %all-reduce.13 = (f32[768]{0:T(1024)S(1)}, f32[768]{0:T(1024)S(1)}, f32[768]{0:T(1024)S(1)}, f32[768]{0:T(1024)S(1)}, f32[768]{0:T(1024)S(1)}, /*index=5*/f32[3072]{0:T(1024)S(1)}, f32[768]{0:T(1024)S(1)}) all-reduce(bf16[768]{0:T(1024)(128)(2,1)} %get-tuple-element.744, ...), channel_id=7, replica_groups=mesh['dp'=4,'ctx'=2,'tensor'=4] {'dp','ctx'}, use_global_device_ids=true, to_apply=%region_23.24.clone | all-reduce | flops 7680 | bytes 47616
  864.1 57.0 %reduce-scatter.30.cloned.1.call-done = f32[96,2]{1,0:T(8,128)} async-done(((f32[768,2]{1,0:T(8,128)}), f32[96,2]{1,0:T(8,128)}) %reduce-scatter.30.cloned.1.call-update) | async-done | bytes 784
  922.6 70.7 %reduce-scatter.26.cloned.1.call-done = f32[768,96]{0,1:T(8,128)} async-done(((f32[768,768]{0,1:T(8,128)}), f32[768,96]{0,1:T(8,128)}) %reduce-scatter.26.cloned.1.call-update) | async-done | bytes 294928 | tf_op jit(solution)/shard_map/reduce_scatter | solution.py:369
  993.3 72.0 %reduce-scatter.24.cloned.1.call-done = f32[96,768]{1,0:T(8,128)} async-done(((f32[768,768]{1,0:T(8,128)}), f32[96,768]{1,0:T(8,128)}) %reduce-scatter.24.cloned.1.call-update) | async-done | bytes 294928 | tf_op jit(solution)/shard_map/reduce_scatter | solution.py:367
  (337 shorter events, 133.4 us)
Async XLA Ops:
  8.0 45.2 %copy-start = (bf16[2,256,768]{2,1,0:T(8,128)(2,1)S(1)}, bf16[2,256,768]{2,1,0:T(8,128)(2,1)}, u32[]{:S(2)}) copy-start(bf16[2,256,768]{2,1,0:T(8,128)(2,1)} %param.19) | copy-start | bytes 2359300
  8.1 99.2 %all-gather.11.cloned.1.call-start = ((), (), s32[]{:S(2)}) async-start(), calls=%async_computation.9 | async-start | bytes 3932160 | tf_op jit(solution)/shard_map/all_gather | solution.py:191
  9.5 45.0 %copy-start.38 = (f32[256,2]{0,1:T(2,128)}, f32[256,2]{0,1:T(2,128)S(1)}, u32[]{:S(2)}) copy-start(f32[256,2]{0,1:T(2,128)S(1)} %broadcast_multiply_fusion.5) | copy-start | bytes 6148
  9.6 45.0 %copy-start.56 = (bf16[2,96]{1,0:T(2,128)(2,1)S(1)}, bf16[2,96]{1,0:T(2,128)(2,1)}, u32[]{:S(2)}) copy-start(bf16[2,96]{1,0:T(2,128)(2,1)} %param.25) | copy-start | bytes 1156
  9.6 61.6 %copy-start.30 = (bf16[3,96,192]{2,1,0:T(8,128)(2,1)S(1)}, bf16[3,96,192]{2,1,0:T(8,128)(2,1)}, u32[]{:S(2)}) copy-start(bf16[3,96,192]{2,1,0:T(8,128)(2,1)} %param.24) | copy-start | bytes 331780
  11.1 60.1 %copy-start.41 = (f32[256,2]{0,1:T(2,128)}, f32[256,2]{0,1:T(2,128)S(1)}, u32[]{:S(2)}) copy-start(f32[256,2]{0,1:T(2,128)S(1)} %add_rsqrt_fusion.1) | copy-start | bytes 6148
  54.5 98.3 %all-gather.13.cloned.1.call-start = ((), (), s32[]{:S(2)}) async-start(), calls=%async_computation.10 | async-start | bytes 2359296 | tf_op jit(solution)/shard_map/all_gather | solution.py:215
  114.5 59.1 %all-gather.23.cloned.1.call-start = ((), (), s32[]{:S(2)}) async-start(), calls=%async_computation.21 | async-start | bytes 2359296 | tf_op jit(solution)/shard_map/all_gather | solution.py:214
  117.0 186.3 %reduce-scatter.16.cloned.1.call-start = ((), (), s32[]{:S(2)}) async-start(), calls=%async_computation.11 | async-start | bytes 3932160 | tf_op jit(solution)/shard_map/reduce_scatter | solution.py:228
  265.2 38.2 %copy-start.1 = (bf16[2,256,768]{2,1,0:T(8,128)(2,1)S(1)}, bf16[2,256,768]{2,1,0:T(8,128)(2,1)}, u32[]{:S(2)}) copy-start(bf16[2,256,768]{2,1,0:T(8,128)(2,1)} %param.19) | copy-start | bytes 2359300
  265.2 68.3 %all-gather.17.cloned.1.call-start = ((), (), s32[]{:S(2)}) async-start(), calls=%async_computation.13 | async-start | bytes 1327104 | tf_op jit(solution)/shard_map/all_gather | solution.py:168
  265.8 72.6 %all-gather.15.cloned.1.call-start = ((), (), s32[]{:S(2)}) async-start(), calls=%async_computation.12 | async-start | bytes 3932160 | tf_op jit(solution)/shard_map/all_gather | solution.py:241
  266.3 168.9 %copy-start.26 = (f32[768]{0:T(1024)}, f32[768]{0:T(1024)S(1)}, u32[]{:S(2)}) copy-start(f32[768]{0:T(1024)S(1)} %convert_element_type.268) | copy-start | bytes 9220
  266.4 168.9 %copy-start.28 = (f32[768]{0:T(1024)}, f32[768]{0:T(1024)S(1)}, u32[]{:S(2)}) copy-start(f32[768]{0:T(1024)S(1)} %convert_element_type.269) | copy-start | bytes 9220
  304.9 130.4 %copy-start.32 = (f32[256,2]{0,1:T(2,128)}, f32[256,2]{0,1:T(2,128)S(1)}, u32[]{:S(2)}) copy-start(f32[256,2]{0,1:T(2,128)S(1)} %broadcast_multiply_fusion.4) | copy-start | bytes 6148
  305.3 130.0 %copy-start.34 = (f32[256,2]{0,1:T(2,128)}, f32[256,2]{0,1:T(2,128)S(1)}, u32[]{:S(2)}) copy-start(f32[256,2]{0,1:T(2,128)S(1)} %add_rsqrt_fusion) | copy-start | bytes 6148
  306.7 75.5 %all-gather.19.cloned.1.call-start = ((), (), s32[]{:S(2)}) async-start(), calls=%async_computation.14 | async-start | bytes 1327104 | tf_op jit(solution)/shard_map/all_gather | solution.py:170
  307.3 126.0 %reduce-scatter.20.cloned.1.call-start = ((), (), s32[]{:S(2)}) async-start(), calls=%async_computation.16 | async-start | bytes 3932160 | tf_op jit(solution)/shard_map/reduce_scatter | solution.py:269
  333.5 48.7 %copy-start.47 = (f32[768]{0:T(1024)}, f32[768]{0:T(1024)S(1)}, u32[]{:S(2)}) copy-start(f32[768]{0:T(1024)S(1)} %dynamic-slice_convert_fusion) | copy-start | bytes 9220
  396.9 70.0 %all-gather.21.cloned.1.call-start = ((), (), s32[]{:S(2)}) async-start(), calls=%async_computation.17 | async-start | bytes 3932160 | tf_op jit(solution)/shard_map/all_gather | solution.py:286
  438.2 242.8 %reduce-scatter.22.cloned.1.call-start = ((), (), s32[]{:S(2)}) async-start(), calls=%async_computation.18 | async-start | bytes 3932160 | tf_op jit(solution)/shard_map/reduce_scatter | solution.py:333
  472.3 81.2 %collective-permute-start = (bf16[1024,2,192]{0,2,1:T(8,128)(2,1)S(1)}, bf16[1024,2,192]{0,2,1:T(8,128)(2,1)}, u32[]{:S(2)}, u32[]{:S(2)}) collective-permute-start(bf16[1024,2,192]{0,2,1:T(8,128)(2,1)S(1)} %copy.129), channel_id=1, source_target_pairs={{4,0},{0,4},{5,1},{1,5},{6,2},{2,6},{7,3},{3,7},{12,8},{8,12},{13,... | collective-permute-start | bytes 2359304 | tf_op jit(solution)/shard_map/while/body/eval_jaxpr/ppermute | solution.py:17
  475.8 77.6 %collective-permute-start.1 = (bf16[1024,2,192]{0,2,1:T(8,128)(2,1)}, bf16[1024,2,192]{0,2,1:T(8,128)(2,1)}, u32[]{:S(2)}, u32[]{:S(2)}) collective-permute-start(bf16[1024,2,192]{0,2,1:T(8,128)(2,1)} %copy.130), channel_id=1, source_target_pairs={{4,0},{0,4},{5,1},{1,5},{6,2},{2,6},{7,3},{3,7},{12,8},{8,12},{13,... | collective-permute-start | bytes 2359304 | tf_op jit(solution)/shard_map/while/body/eval_jaxpr/ppermute | solution.py:17
  514.7 12.2 %copy-start.3 = (f32[1024,2,192]{0,2,1:T(8,128)S(1)}, f32[1024,2,192]{0,2,1:T(8,128)}, u32[]{:S(2)}) copy-start(f32[1024,2,192]{0,2,1:T(8,128)} %get-tuple-element.998) | copy-start | bytes 4718596 | tf_op jit(solution)/shard_map/while
  514.7 22.9 %collective-permute-start.2 = (bf16[1024,2,192]{0,2,1:T(8,128)(2,1)}, bf16[1024,2,192]{0,2,1:T(8,128)(2,1)}, u32[]{:S(2)}, u32[]{:S(2)}) collective-permute-start(bf16[1024,2,192]{0,2,1:T(8,128)(2,1)} %fusion.185), channel_id=1, source_target_pairs={{4,0},{0,4},{5,1},{1,5},{6,2},{2,6},{7,3},{3,7},{12,8},{8,12},{13,... | collective-permute-start | bytes 2359304 | tf_op jit(solution)/shard_map/while/body/eval_jaxpr/ppermute | solution.py:17
  528.1 22.9 %collective-permute-start.3 = (bf16[1024,2,192]{0,2,1:T(8,128)(2,1)}, bf16[1024,2,192]{0,2,1:T(8,128)(2,1)}, u32[]{:S(2)}, u32[]{:S(2)}) collective-permute-start(bf16[1024,2,192]{0,2,1:T(8,128)(2,1)} %fusion.187), channel_id=1, source_target_pairs={{4,0},{0,4},{5,1},{1,5},{6,2},{2,6},{7,3},{3,7},{12,8},{8,12},{13,... | collective-permute-start | bytes 2359304 | tf_op jit(solution)/shard_map/while/body/eval_jaxpr/ppermute | solution.py:17
  554.6 79.7 %collective-permute-start = (bf16[1024,2,192]{0,2,1:T(8,128)(2,1)S(1)}, bf16[1024,2,192]{0,2,1:T(8,128)(2,1)}, u32[]{:S(2)}, u32[]{:S(2)}) collective-permute-start(bf16[1024,2,192]{0,2,1:T(8,128)(2,1)S(1)} %copy.129), channel_id=1, source_target_pairs={{4,0},{0,4},{5,1},{1,5},{6,2},{2,6},{7,3},{3,7},{12,8},{8,12},{13,... | collective-permute-start | bytes 2359304 | tf_op jit(solution)/shard_map/while/body/eval_jaxpr/ppermute | solution.py:17
  558.1 76.2 %collective-permute-start.1 = (bf16[1024,2,192]{0,2,1:T(8,128)(2,1)}, bf16[1024,2,192]{0,2,1:T(8,128)(2,1)}, u32[]{:S(2)}, u32[]{:S(2)}) collective-permute-start(bf16[1024,2,192]{0,2,1:T(8,128)(2,1)} %copy.130), channel_id=1, source_target_pairs={{4,0},{0,4},{5,1},{1,5},{6,2},{2,6},{7,3},{3,7},{12,8},{8,12},{13,... | collective-permute-start | bytes 2359304 | tf_op jit(solution)/shard_map/while/body/eval_jaxpr/ppermute | solution.py:17
  597.0 12.2 %copy-start.3 = (f32[1024,2,192]{0,2,1:T(8,128)S(1)}, f32[1024,2,192]{0,2,1:T(8,128)}, u32[]{:S(2)}) copy-start(f32[1024,2,192]{0,2,1:T(8,128)} %get-tuple-element.998) | copy-start | bytes 4718596 | tf_op jit(solution)/shard_map/while
  597.0 22.9 %collective-permute-start.2 = (bf16[1024,2,192]{0,2,1:T(8,128)(2,1)}, bf16[1024,2,192]{0,2,1:T(8,128)(2,1)}, u32[]{:S(2)}, u32[]{:S(2)}) collective-permute-start(bf16[1024,2,192]{0,2,1:T(8,128)(2,1)} %fusion.185), channel_id=1, source_target_pairs={{4,0},{0,4},{5,1},{1,5},{6,2},{2,6},{7,3},{3,7},{12,8},{8,12},{13,... | collective-permute-start | bytes 2359304 | tf_op jit(solution)/shard_map/while/body/eval_jaxpr/ppermute | solution.py:17
  610.4 21.4 %collective-permute-start.3 = (bf16[1024,2,192]{0,2,1:T(8,128)(2,1)}, bf16[1024,2,192]{0,2,1:T(8,128)(2,1)}, u32[]{:S(2)}, u32[]{:S(2)}) collective-permute-start(bf16[1024,2,192]{0,2,1:T(8,128)(2,1)} %fusion.187), channel_id=1, source_target_pairs={{4,0},{0,4},{5,1},{1,5},{6,2},{2,6},{7,3},{3,7},{12,8},{8,12},{13,... | collective-permute-start | bytes 2359304 | tf_op jit(solution)/shard_map/while/body/eval_jaxpr/ppermute | solution.py:17
  643.1 104.8 %reduce-scatter.32.cloned.1.call-start = ((), (), s32[]{:S(2)}) async-start(), calls=%async_computation.24 | async-start | bytes 884736
  648.3 168.8 %reduce-scatter.28.cloned.1.call-start = ((), (), s32[]{:S(2)}) async-start(), calls=%async_computation.22 | async-start | bytes 2211840
  660.2 200.1 %reduce-scatter.18.cloned.1.call-start = ((), (), s32[]{:S(2)}) async-start(), calls=%async_computation.15 | async-start | bytes 3932160 | tf_op jit(solution)/shard_map/reduce_scatter | solution.py:247
  670.5 11.8 %copy-start.2 = (bf16[2,256,768]{2,1,0:T(8,128)(2,1)S(1)}, bf16[2,256,768]{2,1,0:T(8,128)(2,1)}, u32[]{:S(2)}) copy-start(bf16[2,256,768]{2,1,0:T(8,128)(2,1)} %param.19) | copy-start | bytes 2359300
  670.5 11.8 %copy-start.8 = (bf16[256,2,768]{2,0,1:T(8,128)(2,1)S(1)}, bf16[256,2,768]{2,0,1:T(8,128)(2,1)}, u32[]{:S(2)}) copy-start(bf16[256,2,768]{2,0,1:T(8,128)(2,1)} %reduce-scatter.16.cloned.1.call-done) | copy-start | bytes 2359300
  670.5 11.8 %copy-start.27 = (f32[768]{0:T(1024)S(1)}, f32[768]{0:T(1024)}, u32[]{:S(2)}) copy-start(f32[768]{0:T(1024)} %copy-done.26) | copy-start | bytes 9220
  670.5 11.8 %copy-start.29 = (f32[768]{0:T(1024)S(1)}, f32[768]{0:T(1024)}, u32[]{:S(2)}) copy-start(f32[768]{0:T(1024)} %copy-done.28) | copy-start | bytes 9220
  670.5 11.8 %copy-start.33 = (f32[256,2]{0,1:T(2,128)S(1)}, f32[256,2]{0,1:T(2,128)}, u32[]{:S(2)}) copy-start(f32[256,2]{0,1:T(2,128)} %copy-done.32) | copy-start | bytes 6148
  670.5 11.8 %copy-start.35 = (f32[256,2]{0,1:T(2,128)S(1)}, f32[256,2]{0,1:T(2,128)}, u32[]{:S(2)}) copy-start(f32[256,2]{0,1:T(2,128)} %copy-done.34) | copy-start | bytes 6148
  670.5 11.8 %copy-start.37 = (f32[768]{0:T(1024)S(1)}, f32[768]{0:T(1024)}, u32[]{:S(2)}) copy-start(f32[768]{0:T(1024)} %copy-done.36) | copy-start | bytes 9220
  670.5 11.8 %copy-start.39 = (f32[256,2]{0,1:T(2,128)S(1)}, f32[256,2]{0,1:T(2,128)}, u32[]{:S(2)}) copy-start(f32[256,2]{0,1:T(2,128)} %copy-done.38) | copy-start | bytes 6148
  670.5 11.8 %copy-start.42 = (f32[256,2]{0,1:T(2,128)S(1)}, f32[256,2]{0,1:T(2,128)}, u32[]{:S(2)}) copy-start(f32[256,2]{0,1:T(2,128)} %copy-done.41) | copy-start | bytes 6148
  670.6 11.8 %copy-start.44 = (f32[256,2]{0,1:T(2,128)S(1)}, f32[256,2]{0,1:T(2,128)}, u32[]{:S(2)}) copy-start(f32[256,2]{0,1:T(2,128)} %copy-done.43) | copy-start | bytes 6148
  670.6 250.6 %reduce-scatter.30.cloned.1.call-start = ((), (), s32[]{:S(2)}) async-start(), calls=%async_computation.23 | async-start | bytes 442368
  698.2 295.1 %reduce-scatter.26.cloned.1.call-start = ((), (), s32[]{:S(2)}) async-start(), calls=%async_computation.20 | async-start | bytes 2654208 | tf_op jit(solution)/shard_map/reduce_scatter | solution.py:369
  706.8 358.5 %reduce-scatter.24.cloned.1.call-start = ((), (), s32[]{:S(2)}) async-start(), calls=%async_computation.19 | async-start | bytes 2654208 | tf_op jit(solution)/shard_map/reduce_scatter | solution.py:367
  718.8 141.5 %copy-start.11 = (bf16[256,2,768]{2,0,1:T(8,128)(2,1)S(1)}, bf16[256,2,768]{2,0,1:T(8,128)(2,1)}, u32[]{:S(2)}) copy-start(bf16[256,2,768]{2,0,1:T(8,128)(2,1)} %reduce-scatter.22.cloned.1.call-done) | copy-start | bytes 2359300
  (49 other events, 160.3 us)
Sparse Core Ops, SparseCore 0:
  54.7 25.7 all-gather.10
  114.7 29.5 all-gather.12
  146.4 27.2 all-gather.22
  265.3 37.9 reduce-scatter.15
  438.3 28.5 all-gather.20
Sparse Core Ops, SparseCore 1:
  267.9 41.5 all-gather.16
  311.5 26.8 all-gather.14
  340.7 41.5 all-gather.18
  397.0 36.3 reduce-scatter.19
  643.1 37.8 reduce-scatter.21
  685.3 62.5 reduce-scatter.31
  751.2 65.9 reduce-scatter.27
  819.7 36.7 reduce-scatter.17
  859.5 61.6 reduce-scatter.29
  925.2 68.0 reduce-scatter.25
  997.2 68.0 reduce-scatter.23
where the time goes:
time: 1080 us; the launch traced here: 1070 us
  waiting for transfers between devices  487 us (45%)
  matrix products  222 us (21%)
  blocking collectives  197 us (18%)
  other arithmetic  78.5 us (7%)
  local copies, waits for them, and re-layouts  58.1 us (5%)
  between operations  18.9 us (2%)
    unnamed x19, waiting for transfers between devices  155 us
    unnamed x2, blocking collectives  74.7 us
    reduce_scatter x1, waiting for transfers between devices, local(): lax.psum_scatter(grad_up_w, ('dp', 'ctx'), scatter_dimension=0, tiled=True)  72 us
    reduce_scatter x1, waiting for transfers between devices, local(): lax.psum_scatter(grad_down_w, ('dp', 'ctx'), scatter_dimension=1, tiled=T...  70.7 us
    reduce_scatter x1, waiting for transfers between devices, local(): lax.psum_scatter(jnp.einsum('rsh,hd->rsd', member, w_merge, preferred_ele...  36.9 us
    all_gather x1, waiting for transfers between devices, local(): lax.all_gather(down_weight, ('dp', 'ctx'), axis=1, tiled=True)  36.4 us
    reduce_scatter x1, waiting for transfers between devices, local(): lax.psum_scatter(jnp.einsum('rsf,df->rsd', member, w_up, preferred_elemen...  36.3 us
    all_gather x1, blocking collectives, local(): lax.all_gather(heads_weight, ('dp', 'ctx'), axis=1, tiled=True)  35 us
  transfers between devices with their start and end apart: 24, of which 14 were waited for; matrix products, arithmetic and copies ran while one was open for 20% of the time, Pallas kernels for 0%

commit v1 on v0

v1 whole, which is shorter than its diff:
```python
import functools

import jax
import jax.numpy as jnp
from jax import lax
from jax.experimental import pallas as pl
from jax.experimental.pallas import tpu as pltpu
from jax.sharding import PartitionSpec as P

HEAD_DIM = 64
EPS = 1e-05
GELU_C = 0.7978845608028654
NEG = -1e30
TILE = 256
F32 = jnp.float32
BF16 = jnp.bfloat16


def layer_stats(rows):
    centred = rows - jnp.mean(rows, axis=-1, keepdims=True)
    inv_std = lax.rsqrt(jnp.mean(centred * centred, axis=-1, keepdims=True) + EPS)
    return (centred * inv_std, inv_std)


def norm_back(grad_out, normed, inv_std, gain):
    scaled = grad_out * gain
    return inv_std * (
        scaled
        - jnp.mean(scaled, axis=-1, keepdims=True)
        - normed * jnp.mean(scaled * normed, axis=-1, keepdims=True)
    )


def dot(left, right, dims=((1,), (0,))):
    return lax.dot_general(left, right, (dims, ((), ())), preferred_element_type=F32)


def causal_tile(size):
    key_row = lax.broadcasted_iota(jnp.int32, (size, size), 0)
    query_col = lax.broadcasted_iota(jnp.int32, (size, size), 1)
    return key_row <= query_col


def attend_kernel(
    pieces, heads, starts, qkv, q_pos, k_pos, v_pos, out_t, lse, out, q_t, v_t, k_h, o_nat
):
    seq = pl.program_id(0)
    length, width = q_pos.shape
    rows = length // pieces
    blocks = length // TILE
    for p in range(pieces):
        first = pl.multiple_of(starts[seq * pieces + p], rows)
        part = qkv[pl.ds(first, rows), :]
        here = slice(p * rows, (p + 1) * rows)
        q_pos[here, :] = part[:, :width] * jnp.asarray(HEAD_DIM ** (-0.5), BF16)
        k_pos[here, :] = part[:, width : 2 * width]
        v_pos[here, :] = part[:, 2 * width :]
    for b in range(blocks):
        here = slice(b * TILE, (b + 1) * TILE)
        q_t[:, here] = q_pos[here, :].T
        v_t[:, here] = v_pos[here, :].T
        key = k_pos[here, :]
        for h in range(heads):
            k_h[h, here, :] = key[:, h * HEAD_DIM : (h + 1) * HEAD_DIM]
    allowed = causal_tile(TILE)

    def one_head(h, unused):
        hs = pl.ds(pl.multiple_of(h * HEAD_DIM, HEAD_DIM), HEAD_DIM)
        for i in range(blocks):
            here = slice(i * TILE, (i + 1) * TILE)
            query = q_t[hs, here]
            diag = jnp.where(allowed, dot(k_h[h, here, :], query), NEG)
            top = jnp.max(diag, axis=0, keepdims=True)
            if i > 0:
                past = dot(k_h[h, : i * TILE, :], query)
                top = jnp.maximum(top, jnp.max(past, axis=0, keepdims=True))
            diag = jnp.exp(diag - top)
            total = jnp.sum(diag, axis=0, keepdims=True)
            mixed = dot(v_t[hs, here], diag.astype(BF16))
            if i > 0:
                past = jnp.exp(past - top)
                total += jnp.sum(past, axis=0, keepdims=True)
                mixed += dot(v_t[hs, : i * TILE], past.astype(BF16))
            out_t[hs, here] = mixed / total
            lse[h, :, here] = top + jnp.log(total)
        return unused

    lax.fori_loop(0, heads, one_head, 0)
    for b in range(blocks):
        here = slice(b * TILE, (b + 1) * TILE)
        o_nat[here, :] = out_t[:, here].T.astype(BF16)
    for p in range(pieces):
        first = pl.multiple_of(starts[seq * pieces + p], rows)
        out[pl.ds(first, rows), :] = o_nat[p * rows : (p + 1) * rows, :]


def attend(starts, qkv, seqs, pieces):
    total, triple = qkv.shape
    width = triple // 3
    heads = width // HEAD_DIM
    length = total // seqs
    nat = jax.ShapeDtypeStruct((seqs, length, width), BF16)
    nat_spec = pl.BlockSpec((None, length, width), lambda s, t: (s, 0, 0))
    pairs = heads * length * (length + TILE) // 2 * seqs
    return pl.pallas_call(
        functools.partial(attend_kernel, pieces, heads),
        grid_spec=pltpu.PrefetchScalarGridSpec(
            num_scalar_prefetch=1,
            grid=(seqs,),
            in_specs=[pl.BlockSpec((total, triple), lambda s, t: (0, 0))],
            out_specs=[
                nat_spec,
                nat_spec,
                nat_spec,
                pl.BlockSpec((None, width, length), lambda s, t: (s, 0, 0)),
                pl.BlockSpec((None, heads, 1, length), lambda s, t: (s, 0, 0, 0)),
                pl.BlockSpec((total, width), lambda s, t: (0, 0)),
            ],
            scratch_shapes=[
                pltpu.VMEM((width, length), BF16),
                pltpu.VMEM((width, length), BF16),
                pltpu.VMEM((heads, length, HEAD_DIM), BF16),
                pltpu.VMEM((length, width), BF16),
            ],
        ),
        out_shape=[
            nat,
            nat,
            nat,
            jax.ShapeDtypeStruct((seqs, width, length), F32),
            jax.ShapeDtypeStruct((seqs, heads, 1, length), F32),
            jax.ShapeDtypeStruct((total, width), BF16),
        ],
        compiler_params=pltpu.CompilerParams(vmem_limit_bytes=56 * 2**20),
        cost_estimate=pl.CostEstimate(
            flops=16 * HEAD_DIM * pairs, bytes_accessed=12 * total * triple, transcendentals=pairs
        ),
        name="attend",
    )(starts, qkv)


def attend_back_kernel(
    pieces,
    heads,
    starts,
    grad_out,
    q_pos,
    k_pos,
    v_pos,
    out_t,
    lse,
    grad_qkv,
    bias_sum,
    do_nat,
    q_t,
    k_t,
    do_t,
    q_h,
    k_h,
    v_h,
    do_h,
    row_dot,
    dq_t,
    dk_h,
    dv_h,
    g_nat,
):
    seq = pl.program_id(0)
    length, width = q_pos.shape
    rows = length // pieces
    blocks = length // TILE
    for p in range(pieces):
        first = pl.multiple_of(starts[seq * pieces + p], rows)
        do_nat[p * rows : (p + 1) * rows, :] = grad_out[pl.ds(first, rows), :]
    for b in range(blocks):
        here = slice(b * TILE, (b + 1) * TILE)
        query, key, value, grad = q_pos[here, :], k_pos[here, :], v_pos[here, :], do_nat[here, :]
        q_t[:, here] = query.T
        k_t[:, here] = key.T
        grad_t = grad.T
        do_t[:, here] = grad_t
        product = grad_t.astype(F32) * out_t[:, here]
        for h in range(heads):
            cols = slice(h * HEAD_DIM, (h + 1) * HEAD_DIM)
            q_h[h, here, :] = query[:, cols]
            k_h[h, here, :] = key[:, cols]
            v_h[h, here, :] = value[:, cols]
            do_h[h, here, :] = grad[:, cols]
            row_dot[h, :, here] = jnp.sum(product[cols, :], axis=0, keepdims=True)
    allowed = causal_tile(TILE)

    def one_head(h, unused):
        hs = pl.ds(pl.multiple_of(h * HEAD_DIM, HEAD_DIM), HEAD_DIM)
        for j in range(blocks):
            here = slice(j * TILE, (j + 1) * TILE)
            key, value = k_h[h, here, :], v_h[h, here, :]
            key_t = k_t[hs, here]
            scores = jnp.where(allowed, dot(key, q_t[hs, here]), NEG)
            probs = jnp.exp(scores - lse[h, :, here])
            slope = probs * (dot(value, do_t[hs, here]) - row_dot[h, :, here])
            slope_low = slope.astype(BF16)
            grad_v = dot(probs.astype(BF16), do_h[h, here, :])
            grad_k = dot(slope_low, q_h[h, here, :])
            add = dot(key_t, slope_low)
            dq_t[hs, here] = add if j == 0 else dq_t[hs, here] + add
            if j < blocks - 1:
                later = slice((j + 1) * TILE, length)
                probs = jnp.exp(dot(key, q_t[hs, later]) - lse[h, :, later])
                slope = probs * (dot(value, do_t[hs, later]) - row_dot[h, :, later])
                slope_low = slope.astype(BF16)
                grad_v += dot(probs.astype(BF16), do_h[h, later, :])
                grad_k += dot(slope_low, q_h[h, later, :])
                add = dot(key_t, slope_low)
                dq_t[hs, later] = add if j == 0 else dq_t[hs, later] + add
            dk_h[h, here, :] = grad_k
            dv_h[h, here, :] = grad_v
        return unused

    lax.fori_loop(0, heads, one_head, 0)
    sum_q = jnp.zeros((1, width), F32)
    sum_v = jnp.zeros((1, width), F32)
    for b in range(blocks):
        here = slice(b * TILE, (b + 1) * TILE)
        grad_q = dq_t[:, here].T * (HEAD_DIM ** (-0.5))
        grad_k = jnp.concatenate([dk_h[h, here, :] for h in range(heads)], axis=1)
        grad_v = jnp.concatenate([dv_h[h, here, :] for h in range(heads)], axis=1)
        sum_q += jnp.sum(grad_q, axis=0, keepdims=True)
        sum_v += jnp.sum(grad_v, axis=0, keepdims=True)
        g_nat[here, :] = jnp.concatenate([grad_q, grad_k, grad_v], axis=1).astype(BF16)
    for p in range(pieces):
        first = pl.multiple_of(starts[seq * pieces + p], rows)
        grad_qkv[pl.ds(first, rows), :] = g_nat[p * rows : (p + 1) * rows, :]
    bias_sum[...] = jnp.concatenate([sum_q, sum_v], axis=0)


def attend_back(starts, grad_out, q_pos, k_pos, v_pos, out_t, lse, pieces):
    total, width = grad_out.shape
    seqs, length, unused = q_pos.shape
    heads = width // HEAD_DIM
    nat_spec = pl.BlockSpec((None, length, width), lambda s, t: (s, 0, 0))
    pairs = heads * length * (length + TILE) // 2 * seqs
    per_head = pltpu.VMEM((heads, length, HEAD_DIM), BF16)
    across = pltpu.VMEM((width, length), BF16)
    return pl.pallas_call(
        functools.partial(attend_back_kernel, pieces, heads),
        grid_spec=pltpu.PrefetchScalarGridSpec(
            num_scalar_prefetch=1,
            grid=(seqs,),
            in_specs=[
                pl.BlockSpec((total, width), lambda s, t: (0, 0)),
                nat_spec,
                nat_spec,
                nat_spec,
                pl.BlockSpec((None, width, length), lambda s, t: (s, 0, 0)),
                pl.BlockSpec((None, heads, 1, length), lambda s, t: (s, 0, 0, 0)),
            ],
            out_specs=[
                pl.BlockSpec((total, 3 * width), lambda s, t: (0, 0)),
                pl.BlockSpec((None, 2, width), lambda s, t: (s, 0, 0)),
            ],
            scratch_shapes=[
                pltpu.VMEM((length, width), BF16),
                across,
                across,
                across,
                per_head,
                per_head,
                per_head,
                per_head,
                pltpu.VMEM((heads, 1, length), F32),
                pltpu.VMEM((width, length), F32),
                pltpu.VMEM((heads, length, HEAD_DIM), F32),
                pltpu.VMEM((heads, length, HEAD_DIM), F32),
                pltpu.VMEM((length, 3 * width), BF16),
            ],
        ),
        out_shape=[
            jax.ShapeDtypeStruct((total, 3 * width), BF16),
            jax.ShapeDtypeStruct((seqs, 2, width), F32),
        ],
        compiler_params=pltpu.CompilerParams(vmem_limit_bytes=56 * 2**20),
        cost_estimate=pl.CostEstimate(
            flops=40 * HEAD_DIM * pairs, bytes_accessed=20 * total * width, transcendentals=pairs
        ),
        name="attend_back",
    )(starts, grad_out, q_pos, k_pos, v_pos, out_t, lse)


def swap_tensor(block, bit):
    size = lax.axis_size("tensor")
    return lax.ppermute(block, "tensor", [(i, i ^ bit) for i in range(size)])


def rotate(block, axis, distance):
    size = lax.axis_size(axis)
    return lax.ppermute(block, axis, [(i, (i + distance) % size) for i in range(size)])


def tensor_bits():
    return [1 << b for b in range(lax.axis_size("tensor").bit_length() - 1)]


def gather_tensor(own):
    for bit in reversed(tensor_bits()):
        own = jnp.concatenate([own, swap_tensor(own, bit)], axis=0)
    return own


def scatter_tensor(rows, weight_t):
    parts = None
    for bit in tensor_bits():
        half = rows.shape[0] // 2
        away = dot(rows[half:], weight_t)
        if parts is not None:
            away = away + sum(p[half:].astype(F32) for p in parts)
        moved = swap_tensor(away.astype(BF16), bit)
        parts = ([] if parts is None else [p[:half] for p in parts]) + [moved]
        rows = rows[:half]
    own = dot(rows, weight_t)
    return own + sum(p.astype(F32) for p in parts)


def pick(array, index):
    return lax.dynamic_index_in_dim(array, index, 0, keepdims=False)


def scatter_params(blocks):
    dp, ctx = lax.axis_size("dp"), lax.axis_size("ctx")
    dp_pos, ctx_pos = lax.axis_index("dp"), lax.axis_index("ctx")
    by_ctx = jnp.swapaxes(blocks, 0, 1)
    total = pick(by_ctx, ctx_pos).astype(F32)
    for d in range(1, ctx):
        total += rotate(pick(by_ctx, (ctx_pos + d) % ctx), "ctx", d).astype(F32)
    low = total.astype(BF16)
    result = pick(low, dp_pos).astype(F32)
    for d in range(1, dp):
        result += rotate(pick(low, (dp_pos + d) % dp), "dp", d).astype(F32)
    return result


def local(
    tokens,
    cotangent,
    stretch_order,
    attn_gain,
    attn_shift,
    heads_weight,
    heads_bias,
    merge_weight,
    merge_bias,
    feed_gain,
    feed_shift,
    up_weight,
    up_bias,
    down_weight,
    down_bias,
):
    t_size, t_pos = lax.axis_size("tensor"), lax.axis_index("tensor")
    c_size, c_pos = lax.axis_size("ctx"), lax.axis_index("ctx")
    dp_size = lax.axis_size("dp")
    owners = dp_size * c_size
    seqs_in, rows, model = tokens.shape
    seqs = seqs_in // c_size
    shard = heads_weight.shape[1]
    width = heads_weight.shape[2]
    hidden = up_weight.shape[1]
    hidden_all = hidden * t_size
    pieces = c_size * t_size
    rel = [0]
    for bit in reversed(tensor_bits()):
        rel = rel + [r ^ bit for r in rel]

    vectors = jnp.concatenate(
        [
            jnp.stack(
                [
                    attn_gain,
                    attn_shift,
                    heads_bias[0],
                    heads_bias[1],
                    merge_bias,
                    feed_gain,
                    feed_shift,
                    down_bias,
                ],
                axis=1,
            ),
            up_bias.reshape(shard, -1),
        ],
        axis=1,
    )
    first_pack = jnp.concatenate([heads_weight[0], heads_weight[1], heads_weight[2], vectors], axis=1)
    second_pack = jnp.concatenate([up_weight, down_weight.T, merge_weight.T], axis=1)
    first_all = lax.all_gather(first_pack, ("dp", "ctx"), axis=0, tiled=True)
    second_all = lax.all_gather(second_pack, ("dp", "ctx"), axis=0, tiled=True)
    w_heads = first_all[:, : 3 * width]
    vec = first_all[:, 3 * width :].astype(F32)
    vec_t = vec[:, :8].T
    gain_one, shift_one, b_query, b_value, b_merge, gain_two, shift_two, b_down = (
        vec_t[i] for i in range(8)
    )
    b_up = lax.dynamic_slice_in_dim(vec[:, 8:].reshape(-1), t_pos * hidden, hidden, 0)
    b_query = lax.dynamic_slice_in_dim(b_query, t_pos * width, width, 0)
    b_value = lax.dynamic_slice_in_dim(b_value, t_pos * width, width, 0)
    b_heads = jnp.concatenate([b_query, jnp.zeros_like(b_query), b_value])
    w_up = second_all[:, :hidden]
    w_down_t = second_all[:, hidden : 2 * hidden]
    w_merge_t = second_all[:, 2 * hidden :]

    by_owner = tokens.reshape(c_size, seqs, rows, model)
    own = [pick(by_owner, c_pos)] + [
        rotate(pick(by_owner, (c_pos - d) % c_size), "ctx", -d) for d in range(1, c_size)
    ]
    own_rows = jnp.concatenate(own, axis=0).reshape(-1, model)
    tokens_all = gather_tensor(own_rows)

    per_stretch = t_size // 2
    order = lax.dynamic_slice_in_dim(stretch_order, c_pos * seqs, seqs, 0)
    stretches = order.shape[1]
    span = jnp.arange(stretches, dtype=jnp.int32)
    inverse = jnp.sum(
        jnp.where(order[:, :, None] == span[None, None, :], span[None, :, None], 0), axis=1
    )
    stored = inverse[:, :, None]
    part = jnp.arange(per_stretch, dtype=jnp.int32)[None, None, :]
    piece_t = (stored % 2) * per_stretch + part
    piece_c = stored // 2 + 0 * part
    slot = jnp.zeros_like(piece_t)
    for index, offset in enumerate(rel):
        slot = jnp.where((piece_t ^ t_pos) == offset, index, slot)
    away = (piece_c - c_pos) % c_size
    seq_id = jnp.arange(seqs, dtype=jnp.int32)[:, None, None]
    starts = (((slot * c_size + away) * seqs + seq_id) * rows).reshape(-1)

    g_blocks = cotangent.reshape(c_size, seqs, t_size, rows, model)
    bit = t_pos % 2

    def parity(block, which):
        pairs = block.reshape(seqs, t_size // 2, 2, rows, model)
        return lax.dynamic_index_in_dim(pairs, which, 2, keepdims=False)

    g_here = pick(g_blocks, c_pos)
    g_same, g_other = [parity(g_here, bit)], [parity(g_here, 1 - bit)]
    for d in range(1, c_size):
        moved = rotate(parity(pick(g_blocks, (c_pos - d) % c_size), bit), "ctx", -d)
        g_same.append(moved)
        g_other.append(swap_tensor(moved, 1))
    g_parts = []
    for offset in rel:
        source = g_same if offset % 2 == 0 else g_other
        index = (t_pos ^ offset) // 2
        for d in range(c_size):
            g_parts.append(lax.dynamic_index_in_dim(source[d], index, 1, keepdims=False))
    grad_all = jnp.concatenate(g_parts, axis=0).reshape(-1, model)
    span_rows = own_rows.shape[0]

    rows_in = own_rows.astype(F32)
    normed_all, inv_all = layer_stats(tokens_all.astype(F32))
    norm_one = (normed_all * gain_one + shift_one).astype(BF16)
    normed_one, inv_one = layer_stats(rows_in)
    qkv = (dot(norm_one, w_heads) + b_heads).astype(BF16)
    q_pos, k_pos, v_pos, out_t, lse, attn = attend(starts, qkv, seqs, pieces)
    merged = scatter_tensor(attn, w_merge_t.T)
    resid = rows_in + merged + b_merge

    normed_two, inv_two = layer_stats(resid)
    norm_two = gather_tensor((normed_two * gain_two + shift_two).astype(BF16))
    grad_act = dot(grad_all, w_down_t)
    pre = dot(norm_two, w_up) + b_up
    tangent = jnp.tanh(GELU_C * (pre + 0.044715 * pre * pre * pre))
    activ = (0.5 * pre * (1.0 + tangent)).astype(BF16)
    slope = 0.5 * (1.0 + tangent) + 0.5 * pre * (1.0 - tangent * tangent) * GELU_C * (
        1.0 + 3.0 * 0.044715 * pre * pre
    )
    grad_pre = grad_act * slope
    grad_up_bias = jnp.sum(grad_pre, axis=0)
    grad_pre_low = grad_pre.astype(BF16)
    grad_norm_two = scatter_tensor(grad_pre_low, w_up.T)

    own_grad = grad_all[:span_rows].astype(F32)
    grad_resid = own_grad + norm_back(grad_norm_two, normed_two, inv_two, gain_two)
    grad_resid_all = gather_tensor(grad_resid.astype(BF16))
    mixed = scatter_tensor(activ, w_down_t.T)
    block_rows = (resid + mixed + b_down).astype(BF16)

    grad_attn = dot(grad_resid_all, w_merge_t).astype(BF16)
    grad_up = dot(norm_two, grad_pre_low, ((0,), (0,)))
    grad_down_t = dot(grad_all, activ, ((0,), (0,)))
    grad_merge_t = dot(grad_resid_all, attn, ((0,), (0,)))
    second_grad = jnp.concatenate([grad_up, grad_down_t, grad_merge_t], axis=1).astype(BF16)
    second_own = lax.psum_scatter(
        second_grad, ("dp", "ctx"), scatter_dimension=0, tiled=True
    ).astype(F32)

    grad_qkv, bias_sum = attend_back(
        starts, grad_attn, q_pos, k_pos, v_pos, out_t, lse, pieces
    )
    grad_norm_one = scatter_tensor(grad_qkv, w_heads.T)
    grad_heads = dot(norm_one, grad_qkv, ((0,), (0,)))
    tokens_rows = grad_resid + norm_back(grad_norm_one, normed_one, inv_one, gain_one)

    qkv_sum = dot(jnp.ones((8, grad_qkv.shape[0]), BF16), grad_qkv)[0]
    wide = w_heads.astype(F32)
    shift_one_part = jnp.sum(wide * qkv_sum, axis=1)
    gain_one_part = (jnp.sum(wide * grad_heads, axis=1) - shift_one * shift_one_part) / gain_one
    bias_pair = lax.dynamic_update_slice(
        jnp.zeros((2, model), F32), jnp.sum(bias_sum, axis=0), (0, t_pos * width)
    )
    vec_grads = jnp.stack(
        [
            gain_one_part,
            shift_one_part,
            bias_pair[0],
            bias_pair[1],
            jnp.sum(grad_resid, axis=0),
            jnp.sum(grad_norm_two * normed_two, axis=0),
            jnp.sum(grad_norm_two, axis=0),
            jnp.sum(own_grad, axis=0),
        ]
    )
    vec_grads = jnp.swapaxes(vec_grads.reshape(8, owners, shard), 0, 1).reshape(owners, -1)
    up_bias_pad = lax.dynamic_update_slice(
        jnp.zeros((hidden_all,), F32), grad_up_bias, (t_pos * hidden,)
    ).reshape(owners, -1)
    small = jnp.concatenate([vec_grads, up_bias_pad], axis=1)
    count = small.shape[1]
    lines = -(-count // (3 * width))
    small = jnp.pad(small, ((0, 0), (0, lines * 3 * width - count))).reshape(owners, lines, -1)
    first_grad = jnp.concatenate(
        [grad_heads.reshape(owners, shard, 3 * width), small], axis=1
    ).astype(BF16)
    first_own = scatter_params(first_grad.reshape((dp_size, c_size) + first_grad.shape[1:]))
    heads_own = first_own[:shard]
    small_own = first_own[shard:].reshape(-1)[:count]
    small_low = small_own.astype(BF16)
    small_own = small_own + sum(
        rotate(small_low, "tensor", d).astype(F32) for d in range(1, t_size)
    )
    vec_own = small_own[: 8 * shard].reshape(8, shard)
    up_bias_own = small_own[8 * shard :]

    def send_back(array):
        parts = array.reshape(c_size, seqs, rows, model)
        held = jnp.stack(
            [parts[0]] + [rotate(parts[d], "ctx", d) for d in range(1, c_size)]
        )
        return jnp.concatenate(
            [pick(held, (c_pos - s) % c_size) for s in range(c_size)], axis=0
        )

    block_out = send_back(block_rows)
    tokens_grad = send_back(tokens_rows.astype(BF16)).astype(F32)
    return (
        block_out,
        tokens_grad,
        vec_own[0],
        vec_own[1],
        jnp.swapaxes(heads_own.reshape(shard, 3, width), 0, 1),
        vec_own[2:4],
        second_own[:, 2 * hidden :].T,
        vec_own[4],
        vec_own[5],
        vec_own[6],
        second_own[:, :hidden],
        up_bias_own,
        second_own[:, hidden : 2 * hidden].T,
        vec_own[7],
    )


def solution(mesh):
    both = P(("dp", "ctx"))
    in_specs = (
        P("dp", ("ctx", "tensor"), None),
        P("dp", "ctx", None),
        P("dp", None),
        both,
        both,
        P(None, ("dp", "ctx"), "tensor"),
        P(None, ("dp", "ctx")),
        P("tensor", ("dp", "ctx")),
        both,
        both,
        both,
        P(("dp", "ctx"), "tensor"),
        both,
        P("tensor", ("dp", "ctx")),
        both,
    )
    out_specs = (
        P("dp", ("ctx", "tensor"), None),
        P("dp", ("ctx", "tensor"), None),
        both,
        both,
        P(None, ("dp", "ctx"), "tensor"),
        P(None, ("dp", "ctx")),
        P("tensor", ("dp", "ctx")),
        both,
        both,
        both,
        P(("dp", "ctx"), "tensor"),
        both,
        P("tensor", ("dp", "ctx")),
        both,
    )
    return jax.shard_map(local, mesh=mesh, in_specs=in_specs, out_specs=out_specs, check_vma=False)
```

time: 1080 us -> 437 us (0.40)
  waiting for transfers between devices: 487 us -> 153 us
  matrix products: 222 us -> 59.3 us
  blocking collectives: 197 us -> 35.8 us
  Pallas kernels: 0 us -> 52.6 us
  other arithmetic: 78.5 us -> 35.3 us
  starting transfers between devices: 9.68 us -> 21.4 us
    reduce_scatter x6 -> x0, waiting for transfers between devices: 225 us -> none  [the longest x1 72 us: local(): lax.psum_scatter(grad_up_w, ('dp', 'ctx'), scatter_dimension=0, tiled=True)]
    dot_general x26 -> x21, matrix products: 222 us -> 59.3 us  [dot(): lax.dot_general(left, right, (dims, ((), ())), preferred_element_type=F32)]
    unnamed x19 -> x3, waiting for transfers between devices: 155 us -> 14.1 us
    ppermute x8 -> x26, waiting for transfers between devices: 20.5 us -> 139 us  [the longest x15 94.9 us: swap_tensor(): return lax.ppermute(block, 'tensor', [(i, i ^ bit) for i in range(size)])]
    all_gather x7 -> x1, waiting for transfers between devices: 86.5 us -> 0.01 us  [local(): second_all = lax.all_gather(second_pack, ('dp', 'ctx'), axis=0, tiled=True)]
    all_gather x4 -> x1, blocking collectives: 111 us -> 35.8 us  [local(): first_all = lax.all_gather(first_pack, ('dp', 'ctx'), axis=0, tiled=True)]
    unnamed x2 -> x0, blocking collectives: 74.7 us -> none
    pallas_call x0 -> x2, Pallas kernels: none -> 52.6 us  [the longest x1 29.4 us: attend_back(): pl.pallas_call(functools.partial(attend_back_kernel, pieces, heads), grid...]
  transfers between devices with their start and end apart: 24 -> 28, of which waited for: 14 -> 16; matrix products, arithmetic and copies ran while one was open for 20% -> 28% of each run, Pallas kernels for 0% -> 12%
where the time goes in v1:
time: 437 us; the launch traced here: 433 us
  waiting for transfers between devices  153 us (35%)
  local copies, waits for them, and re-layouts  60.3 us (14%)
  matrix products  59.3 us (14%)
  Pallas kernels  52.6 us (12%)
  blocking collectives  35.8 us (8%)
  other arithmetic  35.3 us (8%)
  starting transfers between devices  21.4 us (5%)
  between operations  15.1 us (3%)
    ppermute x15, waiting for transfers between devices, swap_tensor(): return lax.ppermute(block, 'tensor', [(i, i ^ bit) for i in range(size)])  94.9 us
    dot_general x21, matrix products, dot(): lax.dot_general(left, right, (dims, ((), ())), preferred_element_type=F32)  59.3 us
    ppermute x11, waiting for transfers between devices, rotate(): lax.ppermute(block, axis, [(i, (i + distance) % size) for i in range(size)])  44.4 us
    all_gather x1, blocking collectives, local(): first_all = lax.all_gather(first_pack, ('dp', 'ctx'), axis=0, tiled=True)  35.8 us
    pallas_call x1, Pallas kernels, attend_back(): pl.pallas_call(functools.partial(attend_back_kernel, pieces, heads), grid...  29.4 us
    pallas_call x1, Pallas kernels, attend(): pl.pallas_call(functools.partial(attend_kernel, pieces, heads), grid_spec...  23.2 us
    unnamed x99, local copies, waits for them, and re-layouts  20.6 us
    unnamed x3, waiting for transfers between devices  14.1 us
  transfers between devices with their start and end apart: 28, of which 16 were waited for; matrix products, arithmetic and copies ran while one was open for 28% of the time, Pallas kernels for 12%

profile of v1, /device:TPU:0, one launch (start us, length us, event | category | flops | bytes accessed | tf_op | source)
XLA Modules:
  0.0 433.3 jit_solution(11181977067535388233)
XLA Ops:
  8.5 3.0 collective-permute-start
  11.6 9.1 %collective-permute-done = bf16[1,256,768]{2,1,0:T(8,128)(2,1)S(1)} collective-permute-done((bf16[1,256,768]{2,1,0:T(8,128)(2,1)S(1)}, bf16[1,256,768]{2,1,0:T(8,128)(2,1)S(1)}, u32[]{:S(2)}, u32[]{:S(2)}) %collective-permute-start) | collective-permute-done | bytes 393248 | tf_op jit(solution)/shard_map/ppermute | solution.py:296
  21.5 1.7 collective-permute-start.1
  24.8 15.4 %collective-permute-done.1 = bf16[512,768]{1,0:T(8,128)(2,1)S(1)} collective-permute-done((bf16[512,768]{1,0:T(8,128)(2,1)S(1)}, bf16[512,768]{1,0:T(8,128)(2,1)S(1)}, u32[]{:S(2)}, u32[]{:S(2)}) %collective-permute-start.1) | collective-permute-done | bytes 786464 | tf_op jit(solution)/shard_map/ppermute | solution.py:291
  57.7 1.7 concatenate.67
  59.4 35.8 %all_gather.6 = bf16[768,588]{1,0:T(8,128)(2,1)S(1)} all-gather(bf16[96,588]{1,0:T(8,128)(2,1)} %concatenate.67), channel_id=1, replica_groups=mesh['dp'=4,'ctx'=2,'tensor'=4] {'dp','ctx'}, dimensions={0}, use_global_device_ids=true | all-gather | bytes 1016064 | tf_op jit(solution)/shard_map/all_gather | solution.py:394
  97.0 1.7 copy.159
  103.2 3.9 fusion.2
  107.2 3.7 fusion.5
  110.9 6.0 %add_convert_fusion.qkv = bf16[2048,576]{1,0:T(8,128)(2,1)} fusion(bf16[2048,768]{1,0:T(8,128)(2,1)} %fusion.5, f32[576]{0:T(1024)S(1)} %pad_maximum_fusion.18, bf16[768,588]{1,0:T(8,128)(2,1)S(1)} %copy-done.5), kind=kOutput, calls=%fused_computation.17 | convolution fusion | flops 1814298624 | bytes 6410496 | tf_op jit(solution)/shard_map/dot_general | solution.py:35
  117.0 23.2 %attend.1 = (bf16[1,2048,192]{2,1,0:T(8,128)(2,1)}, bf16[1,2048,192]{2,1,0:T(8,128)(2,1)}, bf16[1,2048,192]{2,1,0:T(8,128)(2,1)}, f32[1,192,2048]{2,1,0:T(8,128)...) custom-call(s32[8]{0:T(128)} %fusion.88.starts, bf16[2048,576]{1,0:T(8,128)(2,1)} %add_convert_fusion.qkv), custom_call_target="tpu_custom_call" | custom-call | flops 7247757312 | bytes 14155776 | tf_op jit(solution)/shard_map/attend/pallas_call | solution.py:105
  140.2 1.8 convolution_convert_fusion.4
  142.1 3.4 collective-permute-done.3
  146.9 1.6 collective-permute-start.4
  150.0 16.6 %collective-permute-done.4 = bf16[512,768]{1,0:T(8,128)(2,1)S(1)} collective-permute-done((bf16[512,768]{1,0:T(8,128)(2,1)S(1)}, bf16[512,768]{1,0:T(8,128)(2,1)S(1)}, u32[]{:S(2)}, u32[]{:S(2)}) %collective-permute-start.4) | collective-permute-done | bytes 786464 | tf_op jit(solution)/shard_map/ppermute | solution.py:291
  167.8 1.6 collective-permute-start.5
  169.4 3.3 constant_dynamic-slice_fusion
  173.5 13.2 %collective-permute-done.5 = bf16[512,768]{1,0:T(8,128)(2,1)} collective-permute-done((bf16[512,768]{1,0:T(8,128)(2,1)S(1)}, bf16[512,768]{1,0:T(8,128)(2,1)}, u32[]{:S(2)}, u32[]{:S(2)}) %collective-permute-start.5) | collective-permute-done | bytes 786464 | tf_op jit(solution)/shard_map/ppermute | solution.py:291
  186.7 2.4 pad_maximum_fusion.5
  189.1 2.2 collective-permute-done.10
  192.6 1.6 copy.146
  194.3 1.8 reshape.401
  202.5 6.5 %multiply_convert_fusion = (bf16[2048,768]{1,0:T(8,128)(2,1)S(1)}, f32[2048,768]{1,0:T(8,128)S(1)}) fusion(f32[768]{0:T(1024)S(1)} %dynamic_slice.93, bf16[768,1728]{1,0:T(8,128)(2,1)S(1)} %copy-done.19, bf16[1024,768]{1,0:T(8,128)(2,1)} %collective-permute-done.6, bf16[512,768]{1,0:T(8,128)(2,1)} %collective-permute-done.5, ...), kind=kOutput, calls=%fused_computation.16 | convolution fusion | flops 2441084928 | bytes 13766656 | tf_op jit(solution)/shard_map/dot_general | solution.py:35
  209.1 6.9 %fusion.104 = (bf16[768]{0:T(1024)(128)(2,1)}, bf16[2048,768]{1,0:T(8,128)(2,1)S(1)}) fusion(f32[2048,768]{1,0:T(8,128)S(1)} %get-tuple-element.196, f32[768]{0:T(1024)S(1)} %dynamic_slice.93, bf16[2048,768]{1,0:T(8,128)(2,1)S(1)} %bitcast.143, bf16[768,1728]{1,0:T(8,128)(2,1)S(1)} %copy-done.19), kind=kOutput, calls=%fused_computation.232 | convolution fusion | flops 2448948480 | bytes 13768192 | tf_op jit(solution)/shard_map/dot_general | solution.py:35
  224.9 1.6 collective-permute-start.8
  226.5 15.8 %collective-permute-done.13 = bf16[512,768]{1,0:T(8,128)(2,1)S(1)} collective-permute-done((bf16[512,768]{1,0:T(8,128)(2,1)S(1)}, bf16[512,768]{1,0:T(8,128)(2,1)S(1)}, u32[]{:S(2)}, u32[]{:S(2)}) %collective-permute-start.13) | collective-permute-done | bytes 786464 | tf_op jit(solution)/shard_map/ppermute | solution.py:291
  243.7 14.8 %collective-permute-done.8 = bf16[512,768]{1,0:T(8,128)(2,1)S(1)} collective-permute-done((bf16[512,768]{1,0:T(8,128)(2,1)S(1)}, bf16[512,768]{1,0:T(8,128)(2,1)S(1)}, u32[]{:S(2)}, u32[]{:S(2)}) %collective-permute-start.8) | collective-permute-done | bytes 786464 | tf_op jit(solution)/shard_map/ppermute | solution.py:291
  258.6 2.4 fusion.101
  268.2 14.2 %collective-permute-done.14 = bf16[512,768]{1,0:T(8,128)(2,1)} collective-permute-done((bf16[512,768]{1,0:T(8,128)(2,1)}, bf16[512,768]{1,0:T(8,128)(2,1)}, u32[]{:S(2)}, u32[]{:S(2)}) %collective-permute-start.14) | collective-permute-done | bytes 786464 | tf_op jit(solution)/shard_map/ppermute | solution.py:291
  282.4 2.6 pad_maximum_fusion.6
  285.1 5.4 %convolution_convert_fusion.6 = bf16[768,768]{0,1:T(8,128)(2,1)} fusion(bf16[2048,768]{1,0:T(8,128)(2,1)S(1)} %copy-done.37, bf16[1024,768]{1,0:T(8,128)(2,1)} %collective-permute-done.6, bf16[512,768]{1,0:T(8,128)(2,1)} %collective-permute-done.5, bf16[512,768]{1,0:T(8,128)(2,1)S(1)} %add_convert_fusion.5), kind=kOutput, calls=%fused_computation.64 | convolution fusion | flops 2425946112 | bytes 7471104 | tf_op jit(solution)/shard_map/dot_general | solution.py:35
  290.5 3.7 convolution_convert_fusion.5
  296.2 3.1 convolution_convert_fusion
  300.7 29.4 %attend_back.1 = (bf16[2048,576]{1,0:T(8,128)(2,1)}, f32[1,2,192]{2,1,0:T(2,128)}) custom-call(s32[8]{0:T(128)} %fusion.88.starts, bf16[2048,192]{1,0:T(8,128)(2,1)} %copy.147.grad_out, bf16[1,2048,192]{2,1,0:T(8,128)(2,1)} %get-tuple-element.23.q_pos, bf16[1,2048,192]{2,1,0:T(8,128)(2,1)} %get-tuple-element.24.k_pos, ...), custom_call_target="tpu_custom_call" | custom-call | flops 18119393280 | bytes 7864320 | tf_op jit(solution)/shard_map/attend_back/pallas_call | solution.py:244
  330.0 2.3 convolution_reduce_fusion
  332.5 2.6 convolution_convert_fusion.1
  335.1 2.8 fusion.30
  338.2 4.5 %copy.157 = bf16[768,1728]{1,0:T(8,128)(2,1)} copy(bf16[768,1728]{0,1:T(8,128)(2,1)S(1)} %pad_maximum_fusion.3) | data formatting | bytes 5308416
  342.9 1.6 copy-done.10
  344.4 5.3 %fusion.12 = (f32[768]{0:T(1024)S(1)}, f32[768]{0:T(1024)S(1)}, bf16[768,576]{0,1:T(8,128)(2,1)}) fusion(bf16[768,576]{0,1:T(8,128)(2,1)} %copy.160, f32[576]{0:T(1024)S(1)} %convolution_reduce_fusion, bf16[2048,768]{1,0:T(8,128)(2,1)} %fusion.5, bf16[2048,576]{1,0:T(8,128)(2,1)S(1)} %copy-done.10), kind=kOutput, calls=%fused_computation.29 | convolution fusion | flops 1814592000 | bytes 7282944 | tf_op jit(solution)/shard_map/dot_general | solution.py:35
  356.8 2.8 add_convert_fusion.1
  360.1 10.1 %collective-permute-done.19 = bf16[4,98,576]{2,0,1:T(4,128)(2,1)S(1)} collective-permute-done((bf16[4,98,576]{2,0,1:T(4,128)(2,1)S(1)}, bf16[4,98,576]{2,0,1:T(4,128)(2,1)S(1)}, u32[]{:S(2)}, u32[]{:S(2)}) %collective-permute-start.19) | collective-permute-done | bytes 451616 | tf_op jit(solution)/shard_map/ppermute | solution.py:296
  370.5 3.8 collective-permute-start.22
  375.4 6.0 %collective-permute-done.20 = bf16[98,576]{1,0:T(8,128)(2,1)S(1)} collective-permute-done((bf16[98,576]{1,0:T(8,128)(2,1)S(1)}, bf16[98,576]{1,0:T(8,128)(2,1)S(1)}, u32[]{:S(2)}, u32[]{:S(2)}) %collective-permute-start.20) | collective-permute-done | bytes 112928 | tf_op jit(solution)/shard_map/ppermute | solution.py:296
  382.8 6.5 %collective-permute-done.21 = bf16[98,576]{1,0:T(8,128)(2,1)S(1)} collective-permute-done((bf16[98,576]{1,0:T(8,128)(2,1)S(1)}, bf16[98,576]{1,0:T(8,128)(2,1)S(1)}, u32[]{:S(2)}, u32[]{:S(2)}) %collective-permute-start.21) | collective-permute-done | bytes 112928 | tf_op jit(solution)/shard_map/ppermute | solution.py:296
  392.1 2.3 fusion.100
  397.8 8.9 %collective-permute-done.18 = bf16[1,256,768]{2,1,0:T(8,128)(2,1)S(1)} collective-permute-done((bf16[1,256,768]{2,1,0:T(8,128)(2,1)S(1)}, bf16[1,256,768]{2,1,0:T(8,128)(2,1)S(1)}, u32[]{:S(2)}, u32[]{:S(2)}) %collective-permute-start.18) | collective-permute-done | bytes 393248 | tf_op jit(solution)/shard_map/ppermute | solution.py:296
  408.3 14.1 %reduce-scatter.4.cloned.1.call-done = bf16[96,1728]{1,0:T(8,128)(2,1)} async-done(((bf16[768,1728]{1,0:T(8,128)(2,1)}), bf16[96,1728]{1,0:T(8,128)(2,1)}) %reduce-scatter.4.cloned.1.call-update) | async-done | bytes 331792
  (249 shorter events, 83.1 us)
Async XLA Ops:
  7.2 16.9 %copy-start = (s32[2,4]{1,0:T(2,128)S(1)}, s32[2,4]{1,0:T(2,128)}, u32[]{:S(2)}) copy-start(s32[2,4]{1,0:T(2,128)} %param.17) | copy-start | bytes 100
  7.2 16.0 %copy-start.23 = (bf16[192,96]{1,0:T(8,128)(2,1)S(1)}, bf16[192,96]{1,0:T(8,128)(2,1)}, u32[]{:S(2)}) copy-start(bf16[192,96]{1,0:T(8,128)(2,1)} %param.22) | copy-start | bytes 110596
  7.2 16.1 %copy-start.20 = (bf16[768,96]{0,1:T(8,128)(2,1)S(1)}, bf16[768,96]{0,1:T(8,128)(2,1)}, u32[]{:S(2)}) copy-start(bf16[768,96]{0,1:T(8,128)(2,1)} %param.28) | copy-start | bytes 442372
  7.2 16.1 %copy-start.21 = (bf16[96,768]{1,0:T(8,128)(2,1)S(1)}, bf16[96,768]{1,0:T(8,128)(2,1)}, u32[]{:S(2)}) copy-start(bf16[96,768]{1,0:T(8,128)(2,1)} %param.26) | copy-start | bytes 442372
  7.2 133.0 %all-gather.2.cloned.1.call-start = ((), (), s32[]{:S(2)}) async-start(), calls=%async_computation.1 | async-start | bytes 3096576 | tf_op jit(solution)/shard_map/all_gather | solution.py:395
  8.5 12.1 %collective-permute-start = (bf16[1,256,768]{2,1,0:T(8,128)(2,1)S(1)}, bf16[1,256,768]{2,1,0:T(8,128)(2,1)S(1)}, u32[]{:S(2)}, u32[]{:S(2)}) collective-permute-start(bf16[1,256,768]{2,1,0:T(8,128)(2,1)S(1)} %get-tuple-element.167), channel_id=1, source_target_pairs={{0,4},{4,0},{1,5},{5,1},{2,6},{6,2},{3,7},{7,3},{8,12},{12,8},{9,1... | collective-permute-start | bytes 1179656 | tf_op jit(solution)/shard_map/ppermute | solution.py:296
  20.7 20.7 %copy-start.33 = (bf16[2,96]{1,0:T(2,128)(2,1)S(1)}, bf16[2,96]{1,0:T(2,128)(2,1)}, u32[]{:S(2)}) copy-start(bf16[2,96]{1,0:T(2,128)(2,1)} %param.21) | copy-start | bytes 1156
  21.5 18.7 %collective-permute-start.1 = (bf16[512,768]{1,0:T(8,128)(2,1)S(1)}, bf16[512,768]{1,0:T(8,128)(2,1)S(1)}, u32[]{:S(2)}, u32[]{:S(2)}) collective-permute-start(bf16[512,768]{1,0:T(8,128)(2,1)S(1)} %bitcast.123), channel_id=1, source_target_pairs={{0,2},{1,3},{2,0},{3,1},{4,6},{5,7},{6,4},{7,5},{8,10},{9,11},{10,... | collective-permute-start | bytes 2359304 | tf_op jit(solution)/shard_map/ppermute | solution.py:291
  24.1 398.4 %reduce-scatter.4.cloned.1.call-start = ((), (), s32[]{:S(2)}) async-start(), calls=%async_computation.2 | async-start | bytes 3096576
  41.4 61.3 %collective-permute-start.2 = (bf16[1024,768]{1,0:T(8,128)(2,1)}, bf16[1024,768]{1,0:T(8,128)(2,1)S(1)}, u32[]{:S(2)}, u32[]{:S(2)}) collective-permute-start(bf16[1024,768]{1,0:T(8,128)(2,1)} %pad_maximum_fusion.4), channel_id=1, source_target_pairs={{0,1},{1,0},{2,3},{3,2},{4,5},{5,4},{6,7},{7,6},{8,9},{9,8},{10,11... | collective-permute-start | bytes 4718600 | tf_op jit(solution)/shard_map/ppermute | solution.py:291
  142.0 3.5 collective-permute-start.3
  146.9 19.6 %collective-permute-start.4 = (bf16[512,768]{1,0:T(8,128)(2,1)S(1)}, bf16[512,768]{1,0:T(8,128)(2,1)S(1)}, u32[]{:S(2)}, u32[]{:S(2)}) collective-permute-start(bf16[512,768]{1,0:T(8,128)(2,1)S(1)} %add_convert_fusion.6), channel_id=1, source_target_pairs={{0,2},{1,3},{2,0},{3,1},{4,6},{5,7},{6,4},{7,5},{8,10},{9,11},{10,... | collective-permute-start | bytes 2359304 | tf_op jit(solution)/shard_map/ppermute | solution.py:291
  167.8 18.9 %collective-permute-start.5 = (bf16[512,768]{1,0:T(8,128)(2,1)S(1)}, bf16[512,768]{1,0:T(8,128)(2,1)}, u32[]{:S(2)}, u32[]{:S(2)}) collective-permute-start(bf16[512,768]{1,0:T(8,128)(2,1)S(1)} %add_convert_fusion.5), channel_id=1, source_target_pairs={{0,2},{1,3},{2,0},{3,1},{4,6},{5,7},{6,4},{7,5},{8,10},{9,11},{10,... | collective-permute-start | bytes 2359304 | tf_op jit(solution)/shard_map/ppermute | solution.py:291
  172.7 18.6 %collective-permute-start.10 = (bf16[1,2,256,768]{3,2,1,0:T(8,128)(2,1)S(1)}, bf16[1,2,256,768]{3,2,1,0:T(8,128)(2,1)}, u32[]{:S(2)}, u32[]{:S(2)}) collective-permute-start(bf16[1,2,256,768]{3,2,1,0:T(8,128)(2,1)S(1)} %dynamic-slice_bitcast_fusion), channel_id=1, source_target_pairs={{0,4},{4,0},{1,5},{5,1},{2,6},{6,2},{3,7},{7,3},{8,12},{12,8},{9,1... | collective-permute-start | bytes 2359304 | tf_op jit(solution)/shard_map/ppermute | solution.py:296
  189.1 13.4 %collective-permute-start.6 = (bf16[1024,768]{1,0:T(8,128)(2,1)}, bf16[1024,768]{1,0:T(8,128)(2,1)}, u32[]{:S(2)}, u32[]{:S(2)}) collective-permute-start(bf16[1024,768]{1,0:T(8,128)(2,1)} %pad_maximum_fusion.5), channel_id=1, source_target_pairs={{0,1},{1,0},{2,3},{3,2},{4,5},{5,4},{6,7},{7,6},{8,9},{9,8},{10,11... | collective-permute-start | bytes 4718600 | tf_op jit(solution)/shard_map/ppermute | solution.py:291
  191.3 9.1 %collective-permute-start.11 = (bf16[1,2,256,768]{3,2,1,0:T(8,128)(2,1)}, bf16[1,2,256,768]{3,2,1,0:T(8,128)(2,1)}, u32[]{:S(2)}, u32[]{:S(2)}) collective-permute-start(bf16[1,2,256,768]{3,2,1,0:T(8,128)(2,1)} %collective-permute-done.10), channel_id=1, source_target_pairs={{0,1},{1,0},{2,3},{3,2},{4,5},{5,4},{6,7},{7,6},{8,9},{9,8},{10,11... | collective-permute-start | bytes 2359304 | tf_op jit(solution)/shard_map/ppermute | solution.py:291
  202.5 6.6 %copy-start.24 = (bf16[8,256,768]{2,1,0:T(8,128)(2,1)}, bf16[8,256,768]{2,1,0:T(8,128)(2,1)S(1)}, u32[]{:S(2)}) copy-start(bf16[8,256,768]{2,1,0:T(8,128)(2,1)S(1)} %bitcast_dynamic-update-slice_fusion) | copy-start | bytes 9437188
  209.1 15.0 %copy-start.34 = (bf16[2048,768]{1,0:T(8,128)(2,1)}, bf16[2048,768]{1,0:T(8,128)(2,1)S(1)}, u32[]{:S(2)}) copy-start(bf16[2048,768]{1,0:T(8,128)(2,1)S(1)} %get-tuple-element.195) | copy-start | bytes 9437188
  216.0 6.4 %copy-start.36 = (bf16[2048,768]{1,0:T(8,128)(2,1)}, bf16[2048,768]{1,0:T(8,128)(2,1)S(1)}, u32[]{:S(2)}) copy-start(bf16[2048,768]{1,0:T(8,128)(2,1)S(1)} %get-tuple-element.153) | copy-start | bytes 9437188
  217.4 3.6 collective-permute-start.12
  219.4 4.7 %collective-permute-start.7 = (bf16[1024,768]{1,0:T(8,128)(2,1)S(1)}, bf16[1024,768]{1,0:T(8,128)(2,1)S(1)}, u32[]{:S(2)}, u32[]{:S(2)}) collective-permute-start(bf16[1024,768]{1,0:T(8,128)(2,1)S(1)} %convolution_convert_fusion.3), channel_id=1, source_target_pairs={{0,1},{1,0},{2,3},{3,2},{4,5},{5,4},{6,7},{7,6},{8,9},{9,8},{10,11... | collective-permute-start | bytes 4718600 | tf_op jit(solution)/shard_map/ppermute | solution.py:291
  221.8 20.4 %collective-permute-start.13 = (bf16[512,768]{1,0:T(8,128)(2,1)S(1)}, bf16[512,768]{1,0:T(8,128)(2,1)S(1)}, u32[]{:S(2)}, u32[]{:S(2)}) collective-permute-start(bf16[512,768]{1,0:T(8,128)(2,1)S(1)} %add_convert_fusion.2), channel_id=1, source_target_pairs={{0,2},{1,3},{2,0},{3,1},{4,6},{5,7},{6,4},{7,5},{8,10},{9,11},{10,... | collective-permute-start | bytes 2359304 | tf_op jit(solution)/shard_map/ppermute | solution.py:291
  224.9 33.7 %copy-start.26 = (f32[768]{0:T(1024)S(1)}, f32[768]{0:T(1024)}, u32[]{:S(2)}) copy-start(f32[768]{0:T(1024)} %get-tuple-element.181) | copy-start | bytes 9220
  224.9 33.7 %collective-permute-start.8 = (bf16[512,768]{1,0:T(8,128)(2,1)S(1)}, bf16[512,768]{1,0:T(8,128)(2,1)S(1)}, u32[]{:S(2)}, u32[]{:S(2)}) collective-permute-start(bf16[512,768]{1,0:T(8,128)(2,1)S(1)} %add_convert_fusion.4), channel_id=1, source_target_pairs={{0,2},{1,3},{2,0},{3,1},{4,6},{5,7},{6,4},{7,5},{8,10},{9,11},{10,... | collective-permute-start | bytes 2359304 | tf_op jit(solution)/shard_map/ppermute | solution.py:291
  261.0 5.0 %copy-start.13 = (bf16[1,256,768]{2,1,0:T(8,128)(2,1)S(1)}, bf16[1,256,768]{2,1,0:T(8,128)(2,1)}, u32[]{:S(2)}) copy-start(bf16[1,256,768]{2,1,0:T(8,128)(2,1)} %copy-done.12) | copy-start | bytes 1179652
  263.1 4.7 %copy-start.31 = (bf16[768]{0:T(1024)(128)(2,1)S(1)}, bf16[768]{0:T(1024)(128)(2,1)}, u32[]{:S(2)}) copy-start(bf16[768]{0:T(1024)(128)(2,1)} %get-tuple-element.152) | copy-start | bytes 4612
  263.1 19.3 %collective-permute-start.14 = (bf16[512,768]{1,0:T(8,128)(2,1)}, bf16[512,768]{1,0:T(8,128)(2,1)}, u32[]{:S(2)}, u32[]{:S(2)}) collective-permute-start(bf16[512,768]{1,0:T(8,128)(2,1)} %convert_element_type.187), channel_id=1, source_target_pairs={{0,2},{1,3},{2,0},{3,1},{4,6},{5,7},{6,4},{7,5},{8,10},{9,11},{10,... | collective-permute-start | bytes 2359304 | tf_op jit(solution)/shard_map/ppermute | solution.py:291
  268.2 16.9 %copy-start.37 = (bf16[2048,768]{1,0:T(8,128)(2,1)S(1)}, bf16[2048,768]{1,0:T(8,128)(2,1)}, u32[]{:S(2)}) copy-start(bf16[2048,768]{1,0:T(8,128)(2,1)} %copy-done.36) | copy-start | bytes 9437188
  285.0 5.5 %copy-start.25 = (bf16[8,256,768]{2,1,0:T(8,128)(2,1)S(1)}, bf16[8,256,768]{2,1,0:T(8,128)(2,1)}, u32[]{:S(2)}) copy-start(bf16[8,256,768]{2,1,0:T(8,128)(2,1)} %copy-done.24) | copy-start | bytes 9437188
  285.0 5.5 %copy-start.35 = (bf16[2048,768]{1,0:T(8,128)(2,1)S(1)}, bf16[2048,768]{1,0:T(8,128)(2,1)}, u32[]{:S(2)}) copy-start(bf16[2048,768]{1,0:T(8,128)(2,1)} %copy-done.34) | copy-start | bytes 9437188
  285.0 11.2 %collective-permute-start.15 = (bf16[1024,768]{1,0:T(8,128)(2,1)}, bf16[1024,768]{1,0:T(8,128)(2,1)}, u32[]{:S(2)}, u32[]{:S(2)}) collective-permute-start(bf16[1024,768]{1,0:T(8,128)(2,1)} %pad_maximum_fusion.6), channel_id=1, source_target_pairs={{0,1},{1,0},{2,3},{3,2},{4,5},{5,4},{6,7},{7,6},{8,9},{9,8},{10,11... | collective-permute-start | bytes 4718600 | tf_op jit(solution)/shard_map/ppermute | solution.py:291
  290.5 3.9 copy-start.28
  290.5 4.0 copy-start.14
  295.4 59.1 %collective-permute-start.9 = (bf16[1,256,768]{2,1,0:T(8,128)(2,1)}, bf16[1,256,768]{2,1,0:T(8,128)(2,1)}, u32[]{:S(2)}, u32[]{:S(2)}) collective-permute-start(bf16[1,256,768]{2,1,0:T(8,128)(2,1)} %get-tuple-element.164), channel_id=1, source_target_pairs={{0,4},{4,0},{1,5},{5,1},{2,6},{6,2},{3,7},{7,3},{8,12},{12,8},{9,1... | collective-permute-start | bytes 1179656 | tf_op jit(solution)/shard_map/ppermute | solution.py:296
  342.7 7.1 %copy-start.32 = (f32[1,2,192]{2,1,0:T(2,128)S(1)}, f32[1,2,192]{2,1,0:T(2,128)}, u32[]{:S(2)}) copy-start(f32[1,2,192]{2,1,0:T(2,128)} %get-tuple-element.29) | copy-start | bytes 4612
  342.7 14.0 %collective-permute-start.16 = (bf16[1024,768]{1,0:T(8,128)(2,1)}, bf16[1024,768]{1,0:T(8,128)(2,1)}, u32[]{:S(2)}, u32[]{:S(2)}) collective-permute-start(bf16[1024,768]{1,0:T(8,128)(2,1)} %convolution_convert_fusion.1), channel_id=1, source_target_pairs={{0,1},{1,0},{2,3},{3,2},{4,5},{5,4},{6,7},{7,6},{8,9},{9,8},{10,11... | collective-permute-start | bytes 4718600 | tf_op jit(solution)/shard_map/ppermute | solution.py:291
  349.8 4.7 %copy-start.15 = (bf16[1,1,256,768]{3,2,1,0:T(8,128)(2,1)S(1)}, bf16[1,1,256,768]{3,2,1,0:T(8,128)(2,1)}, u32[]{:S(2)}) copy-start(bf16[1,1,256,768]{3,2,1,0:T(8,128)(2,1)} %get-tuple-element.165) | copy-start | bytes 1179652
  352.9 3.9 copy-start.7
  353.2 17.1 %collective-permute-start.19 = (bf16[4,98,576]{2,0,1:T(4,128)(2,1)S(1)}, bf16[4,98,576]{2,0,1:T(4,128)(2,1)S(1)}, u32[]{:S(2)}, u32[]{:S(2)}) collective-permute-start(bf16[4,98,576]{2,0,1:T(4,128)(2,1)S(1)} %bitcast.139), channel_id=1, source_target_pairs={{0,4},{4,0},{1,5},{5,1},{2,6},{6,2},{3,7},{7,3},{8,12},{12,8},{9,1... | collective-permute-start | bytes 1354760 | tf_op jit(solution)/shard_map/ppermute | solution.py:296
  359.6 32.5 %collective-permute-start.17 = (bf16[512,768]{1,0:T(8,128)(2,1)}, bf16[512,768]{1,0:T(8,128)(2,1)}, u32[]{:S(2)}, u32[]{:S(2)}) collective-permute-start(bf16[512,768]{1,0:T(8,128)(2,1)} %add_convert_fusion.1), channel_id=1, source_target_pairs={{0,2},{1,3},{2,0},{3,1},{4,6},{5,7},{6,4},{7,5},{8,10},{9,11},{10,... | collective-permute-start | bytes 2359304 | tf_op jit(solution)/shard_map/ppermute | solution.py:291
  370.4 10.9 %collective-permute-start.20 = (bf16[98,576]{1,0:T(8,128)(2,1)S(1)}, bf16[98,576]{1,0:T(8,128)(2,1)S(1)}, u32[]{:S(2)}, u32[]{:S(2)}) collective-permute-start(bf16[98,576]{1,0:T(8,128)(2,1)S(1)} %get-tuple-element.168), channel_id=1, source_target_pairs={{0,8},{8,16},{16,24},{24,0},{1,9},{9,17},{17,25},{25,1},{2,10},{10... | collective-permute-start | bytes 338696 | tf_op jit(solution)/shard_map/ppermute | solution.py:296
  370.5 12.3 %collective-permute-start.22 = (bf16[98,576]{1,0:T(8,128)(2,1)S(1)}, bf16[98,576]{1,0:T(8,128)(2,1)S(1)}, u32[]{:S(2)}, u32[]{:S(2)}) collective-permute-start(bf16[98,576]{1,0:T(8,128)(2,1)S(1)} %get-tuple-element.169), channel_id=1, source_target_pairs={{0,24},{8,0},{16,8},{24,16},{1,25},{9,1},{17,9},{25,17},{2,26},{10... | collective-permute-start | bytes 338696 | tf_op jit(solution)/shard_map/ppermute | solution.py:296
  374.3 15.0 %collective-permute-start.21 = (bf16[98,576]{1,0:T(8,128)(2,1)S(1)}, bf16[98,576]{1,0:T(8,128)(2,1)S(1)}, u32[]{:S(2)}, u32[]{:S(2)}) collective-permute-start(bf16[98,576]{1,0:T(8,128)(2,1)S(1)} %get-tuple-element.170), channel_id=1, source_target_pairs={{0,16},{8,24},{16,0},{24,8},{1,17},{9,25},{17,1},{25,9},{2,18},{10... | collective-permute-start | bytes 338696 | tf_op jit(solution)/shard_map/ppermute | solution.py:296
  389.5 6.4 %collective-permute-start.25 = (bf16[1152]{0:T(1024)(128)(2,1)S(1)}, bf16[1152]{0:T(1024)(128)(2,1)S(1)}, u32[]{:S(2)}, u32[]{:S(2)}) collective-permute-start(bf16[1152]{0:T(1024)(128)(2,1)S(1)} %convert_element_type.207), channel_id=1, source_target_pairs={{0,3},{1,0},{2,1},{3,2},{4,7},{5,4},{6,5},{7,6},{8,11},{9,8},{10,9... | collective-permute-start | bytes 6920 | tf_op jit(solution)/shard_map/ppermute | solution.py:296
  390.3 5.6 %collective-permute-start.24 = (bf16[1152]{0:T(1024)(128)(2,1)S(1)}, bf16[1152]{0:T(1024)(128)(2,1)S(1)}, u32[]{:S(2)}, u32[]{:S(2)}) collective-permute-start(bf16[1152]{0:T(1024)(128)(2,1)S(1)} %convert_element_type.207), channel_id=1, source_target_pairs={{0,2},{1,3},{2,0},{3,1},{4,6},{5,7},{6,4},{7,5},{8,10},{9,11},{10,... | collective-permute-start | bytes 6920 | tf_op jit(solution)/shard_map/ppermute | solution.py:296
  391.0 4.9 %collective-permute-start.23 = (bf16[1152]{0:T(1024)(128)(2,1)S(1)}, bf16[1152]{0:T(1024)(128)(2,1)S(1)}, u32[]{:S(2)}, u32[]{:S(2)}) collective-permute-start(bf16[1152]{0:T(1024)(128)(2,1)S(1)} %convert_element_type.207), channel_id=1, source_target_pairs={{0,1},{1,2},{2,3},{3,0},{4,5},{5,6},{6,7},{7,4},{8,9},{9,10},{10,1... | collective-permute-start | bytes 6920 | tf_op jit(solution)/shard_map/ppermute | solution.py:296
  395.1 11.7 %collective-permute-start.18 = (bf16[1,256,768]{2,1,0:T(8,128)(2,1)S(1)}, bf16[1,256,768]{2,1,0:T(8,128)(2,1)S(1)}, u32[]{:S(2)}, u32[]{:S(2)}) collective-permute-start(bf16[1,256,768]{2,1,0:T(8,128)(2,1)S(1)} %get-tuple-element.160), channel_id=1, source_target_pairs={{0,4},{4,0},{1,5},{5,1},{2,6},{6,2},{3,7},{7,3},{8,12},{12,8},{9,1... | collective-permute-start | bytes 1179656 | tf_op jit(solution)/shard_map/ppermute | solution.py:296
  407.1 19.2 %copy-start.1 = (s32[2,4]{1,0:T(2,128)S(1)}, s32[2,4]{1,0:T(2,128)}, u32[]{:S(2)}) copy-start(s32[2,4]{1,0:T(2,128)} %param.17) | copy-start | bytes 100
  (18 other events, 43.6 us)
Sparse Core Ops, SparseCore 0:
  24.2 70.1 all-gather.1
  342.8 79.5 reduce-scatter.3

commit v2 on v1

v2 whole, which is shorter than its diff:
```python
import functools

import jax
import jax.numpy as jnp
from jax import lax
from jax.experimental import pallas as pl
from jax.experimental.pallas import tpu as pltpu
from jax.sharding import PartitionSpec as P

HEAD_DIM = 64
EPS = 1e-05
GELU_C = 0.7978845608028654
NEG = -1e30
TILE = 256
F32 = jnp.float32
BF16 = jnp.bfloat16


def layer_stats(rows):
    centred = rows - jnp.mean(rows, axis=-1, keepdims=True)
    inv_std = lax.rsqrt(jnp.mean(centred * centred, axis=-1, keepdims=True) + EPS)
    return (centred * inv_std, inv_std)


def norm_back(grad_out, normed, inv_std, gain):
    scaled = grad_out * gain
    return inv_std * (
        scaled
        - jnp.mean(scaled, axis=-1, keepdims=True)
        - normed * jnp.mean(scaled * normed, axis=-1, keepdims=True)
    )


def dot(left, right, dims=((1,), (0,))):
    return lax.dot_general(left, right, (dims, ((), ())), preferred_element_type=F32)


def causal_tile(size):
    key_row = lax.broadcasted_iota(jnp.int32, (size, size), 0)
    query_col = lax.broadcasted_iota(jnp.int32, (size, size), 1)
    return key_row <= query_col


def attend_kernel(dims, scalars, *refs):
    pieces, heads, shard, model, n_tokens, n_packed = dims
    token_parts, refs = refs[:n_tokens], refs[n_tokens:]
    packed_parts, refs = refs[:n_packed], refs[n_packed:]
    norm_one, vectors, heads_t, merge_t, q_pos, k_pos, v_pos, out_t, lse, attn = refs[:10]
    outs = refs[10:14]
    q_t, v_t, k_h, o_nat, tokens, packed, w_wide, w_low, merge, out = refs[14:]
    seq = pl.program_id(0)
    length, width = q_pos.shape
    rows = length // pieces
    blocks = length // TILE
    owners = packed.shape[0]
    first_slot = pl.num_programs(0) * pieces
    t_pos = scalars[first_slot + owners]
    place = 0
    for part in token_parts:
        tokens[place : place + part.shape[0], :] = part[...]
        place += part.shape[0]
    place = 0
    for part in packed_parts:
        packed[place : place + part.shape[0]] = part[...]
        place += part.shape[0]

    def tail_of(owner):
        return packed[scalars[first_slot + owner]].astype(F32)[shard:, :]

    def entry(tail, index):
        return tail[index : index + 1, :shard]

    tails = []
    for i in range(owners):
        block = packed[scalars[first_slot + i]].astype(F32)
        w_wide[i * shard : (i + 1) * shard, :] = block[:shard, :]
        tails.append(block[shard:, :])
    w_low[...] = w_wide[:, : 3 * width].astype(BF16)
    heads_t[...] = w_wide[:, : 3 * width].T.astype(BF16)
    merge_low = w_wide[:, 3 * width :]
    merge_t[...] = merge_low.astype(BF16)
    merge[...] = merge_low.T.astype(BF16)
    lines = [jnp.concatenate([entry(t, v) for t in tails], axis=1) for v in range(8)]
    group = width // shard
    mine = [tail_of(t_pos * group + k) for k in range(group)]
    bias_q = jnp.concatenate([entry(t, 2) for t in mine], axis=1)
    bias_v = jnp.concatenate([entry(t, 3) for t in mine], axis=1)
    long = model // width * shard
    bias_up = jnp.concatenate([t[8:9, :long] for t in mine], axis=1)
    lines.append(bias_up)
    lines.append(jnp.zeros((16 - len(lines), model), F32))
    vectors[...] = jnp.concatenate(lines, axis=0)
    bias = jnp.concatenate([bias_q, jnp.zeros((1, width), F32), bias_v], axis=1)
    gain, shift = lines[0], lines[1]
    for p in range(pieces):
        first = pl.multiple_of(scalars[seq * pieces + p], rows)
        normed, unused = layer_stats(tokens[pl.ds(first, rows), :].astype(F32))
        normed = (normed * gain + shift).astype(BF16)
        norm_one[pl.ds(first, rows), :] = normed
        part = (dot(normed, w_low[...]) + bias).astype(BF16)
        here = slice(p * rows, (p + 1) * rows)
        q_pos[here, :] = part[:, :width] * jnp.asarray(HEAD_DIM ** (-0.5), BF16)
        k_pos[here, :] = part[:, width : 2 * width]
        v_pos[here, :] = part[:, 2 * width :]
    for b in range(blocks):
        here = slice(b * TILE, (b + 1) * TILE)
        q_t[:, here] = q_pos[here, :].T
        v_t[:, here] = v_pos[here, :].T
        key = k_pos[here, :]
        for h in range(heads):
            k_h[h, here, :] = key[:, h * HEAD_DIM : (h + 1) * HEAD_DIM]
    allowed = causal_tile(TILE)

    def one_head(h, unused):
        hs = pl.ds(pl.multiple_of(h * HEAD_DIM, HEAD_DIM), HEAD_DIM)
        for i in range(blocks):
            here = slice(i * TILE, (i + 1) * TILE)
            query = q_t[hs, here]
            diag = jnp.where(allowed, dot(k_h[h, here, :], query), NEG)
            top = jnp.max(diag, axis=0, keepdims=True)
            if i > 0:
                past = dot(k_h[h, : i * TILE, :], query)
                top = jnp.maximum(top, jnp.max(past, axis=0, keepdims=True))
            diag = jnp.exp(diag - top)
            total = jnp.sum(diag, axis=0, keepdims=True)
            mixed = dot(v_t[hs, here], diag.astype(BF16))
            if i > 0:
                past = jnp.exp(past - top)
                total += jnp.sum(past, axis=0, keepdims=True)
                mixed += dot(v_t[hs, : i * TILE], past.astype(BF16))
            out_t[hs, here] = mixed / total
            lse[h, :, here] = top + jnp.log(total)
        return unused

    lax.fori_loop(0, heads, one_head, 0)
    for b in range(blocks):
        here = slice(b * TILE, (b + 1) * TILE)
        o_nat[here, :] = out_t[:, here].T.astype(BF16)
    for p in range(pieces):
        first = pl.multiple_of(scalars[seq * pieces + p], rows)
        part = o_nat[p * rows : (p + 1) * rows, :]
        attn[pl.ds(first, rows), :] = part
        out[pl.ds(first, rows), :] = dot(part, merge[...]).astype(BF16)
    size = out.shape[0] // 4
    for j in range(4):
        outs[j][...] = out[j * size : (j + 1) * size, :]


def attend(scalars, token_parts, packed_parts, shard, width, seqs, pieces):
    total = sum(p.shape[0] for p in token_parts)
    model = token_parts[0].shape[1]
    owners = sum(p.shape[0] for p in packed_parts)
    heads = width // HEAD_DIM
    length = total // seqs
    nat = jax.ShapeDtypeStruct((seqs, length, width), BF16)
    nat_spec = pl.BlockSpec((None, length, width), lambda s, t: (s, 0, 0))
    pairs = heads * length * (length + TILE) // 2 * seqs
    whole = lambda *shape: pl.BlockSpec(shape, lambda s, t: (0,) * len(shape))
    return pl.pallas_call(
        functools.partial(
            attend_kernel, (pieces, heads, shard, model, len(token_parts), len(packed_parts))
        ),
        grid_spec=pltpu.PrefetchScalarGridSpec(
            num_scalar_prefetch=1,
            grid=(seqs,),
            in_specs=[whole(*p.shape) for p in token_parts + packed_parts],
            out_specs=[
                whole(total, model),
                whole(16, model),
                whole(3 * width, model),
                whole(model, width),
                nat_spec,
                nat_spec,
                nat_spec,
                pl.BlockSpec((None, width, length), lambda s, t: (s, 0, 0)),
                pl.BlockSpec((None, heads, 1, length), lambda s, t: (s, 0, 0, 0)),
                whole(total, width),
            ]
            + [whole(total // 4, model)] * 4,
            scratch_shapes=[
                pltpu.VMEM((width, length), BF16),
                pltpu.VMEM((width, length), BF16),
                pltpu.VMEM((heads, length, HEAD_DIM), BF16),
                pltpu.VMEM((length, width), BF16),
                pltpu.VMEM((total, model), BF16),
                pltpu.VMEM((owners,) + packed_parts[0].shape[1:], BF16),
                pltpu.VMEM((model, 4 * width), F32),
                pltpu.VMEM((model, 3 * width), BF16),
                pltpu.VMEM((width, model), BF16),
                pltpu.VMEM((total, model), BF16),
            ],
        ),
        out_shape=[
            jax.ShapeDtypeStruct((total, model), BF16),
            jax.ShapeDtypeStruct((16, model), F32),
            jax.ShapeDtypeStruct((3 * width, model), BF16),
            jax.ShapeDtypeStruct((model, width), BF16),
            nat,
            nat,
            nat,
            jax.ShapeDtypeStruct((seqs, width, length), F32),
            jax.ShapeDtypeStruct((seqs, heads, 1, length), F32),
            jax.ShapeDtypeStruct((total, width), BF16),
        ]
        + [jax.ShapeDtypeStruct((total // 4, model), BF16)] * 4,
        compiler_params=pltpu.CompilerParams(vmem_limit_bytes=58 * 2**20),
        cost_estimate=pl.CostEstimate(
            flops=32 * HEAD_DIM * pairs, bytes_accessed=24 * total * model, transcendentals=pairs
        ),
        name="attend",
    )(scalars, *token_parts, *packed_parts)


def attend_back_kernel(dims, starts, *refs):
    pieces, heads, shard, ctx, t_index = dims
    row_parts, refs = refs[:4], refs[4:]
    merge_t, heads_t, norm_one, attn, q_pos, k_pos, v_pos, out_t, lse = refs[:9]
    vectors, resid_sums, up_n, up_2, up_3 = refs[9:14]
    backs, weights = refs[14:18], refs[18]
    grad_rows, do_nat, q_t, k_t, do_t, q_h, k_h, v_h, do_h, row_dot, dq_t, dk_h, dv_h, g_nat = (
        refs[19:33]
    )
    g_t, back, w_full = refs[33:]
    t_pos = starts[t_index]
    seq = pl.program_id(0)
    length, width = q_pos.shape
    model = norm_one.shape[1]
    rows = length // pieces
    blocks = length // TILE
    place = 0
    for part in row_parts:
        grad_rows[place : place + part.shape[0], :] = part[...]
        place += part.shape[0]
    for p in range(pieces):
        first = pl.multiple_of(starts[seq * pieces + p], rows)
        part = dot(grad_rows[pl.ds(first, rows), :], merge_t[...])
        do_nat[p * rows : (p + 1) * rows, :] = part.astype(BF16)
    for b in range(blocks):
        here = slice(b * TILE, (b + 1) * TILE)
        query, key, value, grad = q_pos[here, :], k_pos[here, :], v_pos[here, :], do_nat[here, :]
        q_t[:, here] = query.T
        k_t[:, here] = key.T
        grad_t = grad.T
        do_t[:, here] = grad_t
        product = grad_t.astype(F32) * out_t[:, here]
        for h in range(heads):
            cols = slice(h * HEAD_DIM, (h + 1) * HEAD_DIM)
            q_h[h, here, :] = query[:, cols]
            k_h[h, here, :] = key[:, cols]
            v_h[h, here, :] = value[:, cols]
            do_h[h, here, :] = grad[:, cols]
            row_dot[h, :, here] = jnp.sum(product[cols, :], axis=0, keepdims=True)
    allowed = causal_tile(TILE)

    def one_head(h, unused):
        hs = pl.ds(pl.multiple_of(h * HEAD_DIM, HEAD_DIM), HEAD_DIM)
        for j in range(blocks):
            here = slice(j * TILE, (j + 1) * TILE)
            key, value = k_h[h, here, :], v_h[h, here, :]
            key_t = k_t[hs, here]
            scores = jnp.where(allowed, dot(key, q_t[hs, here]), NEG)
            probs = jnp.exp(scores - lse[h, :, here])
            slope = probs * (dot(value, do_t[hs, here]) - row_dot[h, :, here])
            slope_low = slope.astype(BF16)
            grad_v = dot(probs.astype(BF16), do_h[h, here, :])
            grad_k = dot(slope_low, q_h[h, here, :])
            add = dot(key_t, slope_low)
            dq_t[hs, here] = add if j == 0 else dq_t[hs, here] + add
            if j < blocks - 1:
                later = slice((j + 1) * TILE, length)
                probs = jnp.exp(dot(key, q_t[hs, later]) - lse[h, :, later])
                slope = probs * (dot(value, do_t[hs, later]) - row_dot[h, :, later])
                slope_low = slope.astype(BF16)
                grad_v += dot(probs.astype(BF16), do_h[h, later, :])
                grad_k += dot(slope_low, q_h[h, later, :])
                add = dot(key_t, slope_low)
                dq_t[hs, later] = add if j == 0 else dq_t[hs, later] + add
            dk_h[h, here, :] = grad_k
            dv_h[h, here, :] = grad_v
        return unused

    lax.fori_loop(0, heads, one_head, 0)
    wide = jnp.zeros((1, 3 * width), F32)
    for b in range(blocks):
        here = slice(b * TILE, (b + 1) * TILE)
        grad_q = dq_t[:, here].T * (HEAD_DIM ** (-0.5))
        grad_k = jnp.concatenate([dk_h[h, here, :] for h in range(heads)], axis=1)
        grad_v = jnp.concatenate([dv_h[h, here, :] for h in range(heads)], axis=1)
        grads = jnp.concatenate([grad_q, grad_k, grad_v], axis=1)
        wide += jnp.sum(grads, axis=0, keepdims=True)
        g_nat[here, :] = grads.astype(BF16)
    w_t = jnp.zeros((3 * width, model), F32)
    m_t = jnp.zeros((width, model), F32)
    column = jnp.zeros((3 * width, 1), F32)
    for p in range(pieces):
        first = pl.multiple_of(starts[seq * pieces + p], rows)
        part = g_nat[p * rows : (p + 1) * rows, :]
        back[pl.ds(first, rows), :] = dot(part, heads_t[...]).astype(BF16)
    for p in range(pieces):
        first = pl.multiple_of(starts[seq * pieces + p], rows)
        g_t[:, :] = g_nat[p * rows : (p + 1) * rows, :].astype(F32).T
        turned = g_t[...]
        column += jnp.sum(turned, axis=1, keepdims=True)
        w_t += dot(turned.astype(BF16), norm_one[pl.ds(first, rows), :])
        mine = attn[pl.ds(first, rows), :].astype(F32).T.astype(BF16)
        m_t += dot(mine, grad_rows[pl.ds(first, rows), :])
    w_full[:, : 3 * width] = w_t.T
    w_full[:, 3 * width :] = m_t.T
    size = back.shape[0] // 4
    for j in range(4):
        backs[j][...] = back[j * size : (j + 1) * size, :]
    factor = heads_t[...].astype(F32)
    group = lax.broadcasted_iota(jnp.int32, (1, model), 1) // width
    spread = lambda part: jnp.where(
        group == t_pos, jnp.concatenate([part] * (model // width), axis=1), 0.0
    )
    shift_sum = jnp.sum(factor * column, axis=0, keepdims=True)
    gain_sum = jnp.sum(factor * w_t, axis=0, keepdims=True) - vectors[1:2, :] * shift_sum
    up_sum = up_n[...] + up_2[...] + up_3[...]
    lines = jnp.concatenate(
        [
            gain_sum / vectors[0:1, :],
            shift_sum,
            spread(wide[:, :width]),
            spread(wide[:, 2 * width :]),
            resid_sums[0:4, :],
        ],
        axis=0,
    )
    owners = model // shard
    long = model // width * shard
    for i in range(owners):
        k, lane = i * long // model, i * long % model
        here = slice(i * shard, (i + 1) * shard)
        block = [
            w_full[here, :],
            jnp.concatenate([lines[:, here], jnp.zeros((8, model - shard), F32)], axis=1),
            jnp.concatenate(
                [
                    jnp.where(t_pos == k, up_sum[:, lane : lane + long], 0.0),
                    jnp.zeros((1, model - long), F32),
                ],
                axis=1,
            ),
            jnp.zeros((7, model), F32),
        ]
        weights[i % ctx, i // ctx] = jnp.concatenate(block, axis=0).astype(BF16)


def attend_back(starts, row_parts, merge_t, heads_t, norm_one, attn, kept, lines, shard, ctx, pieces):
    q_pos, k_pos, v_pos, out_t, lse = kept
    total, model = norm_one.shape
    width = merge_t.shape[1]
    seqs, length, unused = q_pos.shape
    heads = width // HEAD_DIM
    nat_spec = pl.BlockSpec((None, length, width), lambda s, t: (s, 0, 0))
    whole = lambda *shape: pl.BlockSpec(shape, lambda s, t: (0,) * len(shape))
    pairs = heads * length * (length + TILE) // 2 * seqs
    per_head = pltpu.VMEM((heads, length, HEAD_DIM), BF16)
    by_owner = (ctx, model // shard // ctx, shard + 16, 4 * width)
    across = pltpu.VMEM((width, length), BF16)
    return pl.pallas_call(
        functools.partial(
            attend_back_kernel, (pieces, heads, shard, ctx, starts.shape[0] - 1)
        ),
        grid_spec=pltpu.PrefetchScalarGridSpec(
            num_scalar_prefetch=1,
            grid=(seqs,),
            in_specs=[whole(*p.shape) for p in row_parts]
            + [
                whole(model, width),
                whole(3 * width, model),
                whole(total, model),
                whole(total, width),
                nat_spec,
                nat_spec,
                nat_spec,
                pl.BlockSpec((None, width, length), lambda s, t: (s, 0, 0)),
                pl.BlockSpec((None, heads, 1, length), lambda s, t: (s, 0, 0, 0)),
            ]
            + [whole(*v.shape) for v in lines],
            out_specs=[whole(total // 4, model)] * 4
            + [
                pl.BlockSpec((None,) + by_owner, lambda s, t: (s, 0, 0, 0, 0)),
            ],
            scratch_shapes=[
                pltpu.VMEM((total, model), BF16),
                pltpu.VMEM((length, width), BF16),
                across,
                across,
                across,
                per_head,
                per_head,
                per_head,
                per_head,
                pltpu.VMEM((heads, 1, length), F32),
                pltpu.VMEM((width, length), F32),
                pltpu.VMEM((heads, length, HEAD_DIM), F32),
                pltpu.VMEM((heads, length, HEAD_DIM), F32),
                pltpu.VMEM((length, 3 * width), BF16),
                pltpu.VMEM((3 * width, length // pieces), F32),
                pltpu.VMEM((total, model), BF16),
                pltpu.VMEM((model, 4 * width), F32),
            ],
        ),
        out_shape=[jax.ShapeDtypeStruct((total // 4, model), BF16)] * 4
        + [
            jax.ShapeDtypeStruct((seqs,) + by_owner, BF16),
        ],
        compiler_params=pltpu.CompilerParams(vmem_limit_bytes=60 * 2**20),
        cost_estimate=pl.CostEstimate(
            flops=60 * HEAD_DIM * pairs, bytes_accessed=24 * total * model, transcendentals=pairs
        ),
        name="attend_back",
    )(starts, *row_parts, merge_t, heads_t, norm_one, attn, q_pos, k_pos, v_pos, out_t, lse, *lines)


def feed_kernel(
    seqs,
    ctx,
    turned,
    table,
    norm,
    g_own,
    g_far,
    up,
    down_t,
    bias,
    *refs,
):
    step = pl.program_id(0)
    if turned:
        up_t, down, act, pre_low, back, mix, g_out, sums = refs
    else:
        act, pre_low, back, mix, g_out, sums, up_t, down = refs

        @pl.when(step == 0)
        def turn_weights():
            up_t[...] = up[...].T
            down[...] = down_t[...].T

    distance = lax.rem(lax.div(step, seqs), ctx)
    grad = jnp.where(distance == 0, g_own[...], g_far[...])
    g_out[...] = grad
    pre = dot(norm[...], up[...]) + bias[...]
    grad_act = dot(grad, down_t[...])
    square = pre * pre
    tangent = jnp.tanh(GELU_C * (pre + 0.044715 * square * pre))
    half = 0.5 * (1.0 + tangent)
    low_act = (pre * half).astype(BF16)
    act[...] = low_act
    mix[...] = dot(low_act, down[...]).astype(BF16)
    slope = half + 0.5 * pre * (1.0 - tangent * tangent) * (
        GELU_C + (GELU_C * 3.0 * 0.044715) * square
    )
    grad_pre = grad_act * slope
    total = jnp.sum(grad_pre, axis=0, keepdims=True)
    sums[...] = jnp.where(step == 0, total, sums[...] + total)
    low = grad_pre.astype(BF16)
    pre_low[...] = low
    back[...] = dot(low, up_t[...]).astype(BF16)


def feed(table, norm, g_own, g_far, second, bias, turned, seqs, ctx):
    total, model = norm.shape
    rows = g_own.shape[1]
    hidden = second.shape[1] // 2
    steps = total // rows
    by_rows = lambda size: pl.BlockSpec((rows, size), lambda i, t: (i, 0))
    return pl.pallas_call(
        functools.partial(feed_kernel, seqs, ctx, len(turned) > 0),
        grid_spec=pltpu.PrefetchScalarGridSpec(
            num_scalar_prefetch=1,
            grid=(steps,),
            in_specs=[
                by_rows(model),
                pl.BlockSpec((None, rows, model), lambda i, t: (t[i], 0, 0)),
                pl.BlockSpec((None, rows, model), lambda i, t: (t[steps + i], 0, 0)),
                pl.BlockSpec((model, hidden), lambda i, t: (0, 0)),
                pl.BlockSpec((model, hidden), lambda i, t: (0, 1)),
                pl.BlockSpec((1, hidden), lambda i, t: (0, 0)),
            ]
            + [pl.BlockSpec((hidden, model), lambda i, t: (0, 0))] * len(turned),
            out_specs=[
                by_rows(hidden),
                by_rows(hidden),
                by_rows(model),
                by_rows(model),
                by_rows(model),
                pl.BlockSpec((1, hidden), lambda i, t: (0, 0)),
            ]
            + [pl.BlockSpec((hidden, model), lambda i, t: (0, 0))] * (2 - len(turned)),
        ),
        out_shape=[
            jax.ShapeDtypeStruct((total, hidden), BF16),
            jax.ShapeDtypeStruct((total, hidden), BF16),
            jax.ShapeDtypeStruct((total, model), BF16),
            jax.ShapeDtypeStruct((total, model), BF16),
            jax.ShapeDtypeStruct((total, model), BF16),
            jax.ShapeDtypeStruct((1, hidden), F32),
        ]
        + [jax.ShapeDtypeStruct((hidden, model), BF16)] * (2 - len(turned)),
        compiler_params=pltpu.CompilerParams(vmem_limit_bytes=60 * 2**20),
        cost_estimate=pl.CostEstimate(
            flops=8 * total * model * hidden,
            bytes_accessed=14 * total * model,
            transcendentals=total * hidden,
        ),
        name="feed",
    )(table, norm, g_own, g_far, second, second, bias, *turned)


def resid_kernel(own, beside, across, resid, grad, vectors, out, low, sums):
    step = pl.program_id(0)
    normed, inv_std = layer_stats(resid[...])
    back = own[...].astype(F32) + beside[...].astype(F32) + across[...].astype(F32)
    given = grad[...].astype(F32)
    total = given + norm_back(back, normed, inv_std, vectors[5:6, :])
    out[...] = total
    low[...] = total.astype(BF16)
    add = lambda rows: jnp.sum(rows, axis=0, keepdims=True)
    lines = jnp.concatenate(
        [add(total), add(back * normed), add(back), add(given), jnp.zeros((4, total.shape[1]), F32)],
        axis=0,
    )
    sums[...] = jnp.where(step == 0, lines, sums[...] + lines)


def first_kernel(own, beside, across, rows, grad, vectors, out, low):
    normed, inv_std = layer_stats(rows[...].astype(F32))
    back = own[...].astype(F32) + beside[...].astype(F32) + across[...].astype(F32)
    total = grad[...] + norm_back(back, normed, inv_std, vectors[0:1, :])
    out[...] = total
    low[...] = total.astype(BF16)


def row_wise(kernel, parts, vectors, with_sums):
    total, model = parts[3].shape
    steps = 4
    by_rows = pl.BlockSpec((total // steps, model), lambda i: (i, 0))
    fixed = lambda rows: pl.BlockSpec((rows, model), lambda i: (0, 0))
    return pl.pallas_call(
        kernel,
        grid=(steps,),
        in_specs=[by_rows] * len(parts) + [fixed(16)],
        out_specs=[by_rows, by_rows] + [fixed(8)] * with_sums,
        out_shape=[
            jax.ShapeDtypeStruct((total, model), F32),
            jax.ShapeDtypeStruct((total, model), BF16),
        ]
        + [jax.ShapeDtypeStruct((8, model), F32)] * with_sums,
        cost_estimate=pl.CostEstimate(
            flops=20 * total * model, bytes_accessed=18 * total * model, transcendentals=total
        ),
        name="row_wise",
    )(*parts, vectors)


def heads_kernel(width, a, b, c, d, heads, merge, small):
    shard = merge.shape[1]
    total = sum(part[...].astype(F32) for part in (a, b, c, d))
    for m in range(3):
        heads[m] = total[:shard, m * width : (m + 1) * width]
    merge[...] = total[:shard, 3 * width :].T
    small[...] = total[shard:, :]


def finish_heads(parts, width):
    shard = parts[0].shape[0] - 16
    if len(parts) != 4:
        low = [sum(p.astype(F32) for p in parts)] + [jnp.zeros(parts[0].shape, F32)] * 3
        parts = low
    return pl.pallas_call(
        functools.partial(heads_kernel, width),
        out_shape=[
            jax.ShapeDtypeStruct((3, shard, width), F32),
            jax.ShapeDtypeStruct((width, shard), F32),
            jax.ShapeDtypeStruct((16, 4 * width), F32),
        ],
        name="finish_heads",
    )(*parts)


def swap_tensor(block, bit):
    size = lax.axis_size("tensor")
    return lax.ppermute(block, "tensor", [(i, i ^ bit) for i in range(size)])


def rotate(block, axis, distance):
    size = lax.axis_size(axis)
    return lax.ppermute(block, axis, [(i, (i + distance) % size) for i in range(size)])


def scatter_tensor(parts):
    far = swap_tensor(parts[3], 1)
    near = (parts[2].astype(F32) + far.astype(F32)).astype(BF16)
    across = swap_tensor(near, 2)
    beside = swap_tensor(parts[1], 1)
    return (parts[0], beside, across)


def quarters(rows):
    size = rows.shape[0] // 4
    return [rows[j * size : (j + 1) * size] for j in range(4)]


def add_all(parts):
    return sum(p.astype(F32) for p in parts)


def pick(array, index):
    return lax.dynamic_index_in_dim(array, index, 0, keepdims=False)


def scatter_ctx(blocks):
    ctx, ctx_pos = lax.axis_size("ctx"), lax.axis_index("ctx")
    take = lambda c: lax.dynamic_index_in_dim(blocks, c, 1, keepdims=False)
    total = take(ctx_pos).astype(F32)
    for d in range(1, ctx):
        total += rotate(take((ctx_pos + d) % ctx), "ctx", d).astype(F32)
    return total.astype(BF16)


def scatter_dp(blocks):
    dp, dp_pos = lax.axis_size("dp"), lax.axis_index("dp")
    return [pick(blocks, dp_pos)] + [
        rotate(pick(blocks, (dp_pos + d) % dp), "dp", d) for d in range(1, dp)
    ]


def local(
    tokens,
    cotangent,
    stretch_order,
    attn_gain,
    attn_shift,
    heads_weight,
    heads_bias,
    merge_weight,
    merge_bias,
    feed_gain,
    feed_shift,
    up_weight,
    up_bias,
    down_weight,
    down_bias,
):
    t_size, t_pos = lax.axis_size("tensor"), lax.axis_index("tensor")
    c_size, c_pos = lax.axis_size("ctx"), lax.axis_index("ctx")
    dp_size, dp_pos = lax.axis_size("dp"), lax.axis_index("dp")
    owners = dp_size * c_size
    seqs_in, rows, model = tokens.shape
    seqs = seqs_in // c_size
    shard = heads_weight.shape[1]
    width = heads_weight.shape[2]
    hidden = up_weight.shape[1]
    hidden_all = hidden * t_size
    pieces = c_size * t_size
    span_rows = c_size * seqs * rows

    by_owner = tokens.reshape(c_size, seqs, rows, model)
    near = pick(by_owner, c_pos).reshape(-1, model)
    far = [rotate(pick(by_owner, (c_pos - d) % c_size), "ctx", -d) for d in range(1, c_size)]
    far = jnp.concatenate(far, axis=0).reshape(-1, model)
    near_x = swap_tensor(near, 2)
    far_x = swap_tensor(far, 2)
    own_rows = jnp.concatenate([near, far], axis=0)

    line = lax.broadcasted_iota(jnp.int32, (16, model), 0)
    small = jnp.zeros((16, model), BF16)
    for index, vector in enumerate(
        [
            attn_gain,
            attn_shift,
            heads_bias[0],
            heads_bias[1],
            merge_bias,
            feed_gain,
            feed_shift,
            down_bias,
            up_bias,
        ]
    ):
        wide = jnp.pad(vector, (0, model - vector.shape[0]))
        small = jnp.where(line == index, wide[None, :], small)
    first_pack = jnp.concatenate(
        [
            jnp.concatenate(
                [heads_weight[0], heads_weight[1], heads_weight[2], merge_weight.T], axis=1
            ),
            small,
        ],
        axis=0,
    )
    by_dp = [first_pack] + [rotate(first_pack, "dp", -d) for d in range(1, dp_size)]
    packed_parts = by_dp + [rotate(p, "ctx", -d) for d in range(1, c_size) for p in by_dp]
    second_pack = jnp.concatenate([up_weight, down_weight.T], axis=1)
    second_pack, by_dp[-1] = lax.optimization_barrier((second_pack, by_dp[-1]))
    packed_parts = [p[None] for p in packed_parts]
    second_all = lax.all_gather(second_pack, ("dp", "ctx"), axis=0, tiled=True)

    near_1, far_1 = swap_tensor(near, 1), swap_tensor(far, 1)
    near_3, far_3 = swap_tensor(near_x, 1), swap_tensor(far_x, 1)
    token_parts = [near, far, near_1, far_1, near_x, far_x, near_3, far_3]

    per_stretch = t_size // 2
    order = lax.dynamic_slice_in_dim(stretch_order, c_pos * seqs, seqs, 0)
    stretches = order.shape[1]
    span = jnp.arange(stretches, dtype=jnp.int32)
    inverse = jnp.sum(
        jnp.where(order[:, :, None] == span[None, None, :], span[None, :, None], 0), axis=1
    )
    stored = inverse[:, :, None]
    part = jnp.arange(per_stretch, dtype=jnp.int32)[None, None, :]
    slot = ((stored % 2) * per_stretch + part) ^ t_pos
    away = (stored // 2 - c_pos) % c_size
    seq_id = jnp.arange(seqs, dtype=jnp.int32)[:, None, None]
    starts = (((slot * c_size + away) * seqs + seq_id) * rows).reshape(-1)
    owner = jnp.arange(owners, dtype=jnp.int32)
    slots = ((owner % c_size - c_pos) % c_size) * dp_size + (owner // c_size - dp_pos) % dp_size
    scalars = jnp.concatenate([starts, slots, t_pos[None].astype(jnp.int32)])

    g_blocks = cotangent.reshape(c_size, seqs, 2, t_size // 2, rows, model)
    bit = t_pos % 2
    g_moved = [
        rotate(
            lax.dynamic_index_in_dim(pick(g_blocks, (c_pos - d) % c_size), bit, 1, keepdims=False),
            "ctx",
            -d,
        )
        for d in range(1, c_size)
    ]
    g_moved = jnp.stack(g_moved)

    norm_one, vec, heads_t, merge_t, q_pos, k_pos, v_pos, out_t, lse, attn, *shares = attend(
        scalars, token_parts, packed_parts, shard, width, seqs, pieces
    )
    shares[3], g_moved = lax.optimization_barrier((shares[3], g_moved))
    merged = add_all(scatter_tensor(shares))
    b_merge, gain_two, shift_two, b_down = vec[4], vec[5], vec[6], vec[7]
    rows_in = own_rows.astype(F32)
    resid = rows_in + merged + b_merge

    normed_two, inv_two = layer_stats(resid)
    norm_0 = (normed_two * gain_two + shift_two).astype(BF16)
    norm_2 = swap_tensor(norm_0, 2)
    norm_near = jnp.concatenate([norm_0, swap_tensor(norm_0, 1)], axis=0)
    g_own = cotangent.reshape(-1, rows, model)
    g_far = jnp.stack([g_moved, swap_tensor(g_moved, 1)], axis=2).reshape(-1, rows, model)
    b_up = vec[8:9, :hidden]

    def feed_part(offsets, norm, turned=()):
        own_table, far_table = [], []
        for j in offsets:
            piece = t_pos ^ j
            for d in range(c_size):
                for q in range(seqs):
                    own_table.append((c_pos * seqs + q) * t_size + piece if d == 0 else 0 * piece)
                    place = (piece // 2) ^ bit
                    far_row = (((d - 1) * seqs + q) * 2 + place) * (t_size // 2) + piece % 2
                    far_table.append(far_row if d > 0 else 0 * piece)
        table = jnp.stack(own_table + far_table).astype(jnp.int32)
        return feed(table, norm, g_own, g_far, second_all, b_up, turned, seqs, c_size)

    act_n, pre_n, back_n, mix_n, g_n, up_sum_n, *turned = feed_part((0, 1), norm_near)
    norm_2, up_sum_n = lax.optimization_barrier((norm_2, up_sum_n))
    norm_3 = swap_tensor(norm_2, 1)
    act_3, pre_3, back_3, mix_3, g_3, up_sum_3 = feed_part((3,), norm_3, turned)
    act_2, pre_2, back_2, mix_2, g_2, up_sum_2 = feed_part((2,), norm_2, turned)
    unused, beside, across = scatter_tensor([back_n, back_n[span_rows:], back_2, back_3])

    together = lambda parts: jnp.concatenate(parts, axis=0)
    grad_down_t = dot(together([g_n, g_2, g_3]), together([act_n, act_2, act_3]), ((0,), (0,)))
    grad_up = dot(together([norm_near, norm_2, norm_3]), together([pre_n, pre_2, pre_3]), ((0,), (0,)))
    feed_grad = jnp.concatenate([grad_up, grad_down_t], axis=1).astype(BF16)
    across, feed_grad = lax.optimization_barrier((across, feed_grad))
    feed_half = scatter_ctx(feed_grad.reshape(dp_size, c_size, shard, 2 * hidden))
    grad_resid, resid_0, resid_sums = row_wise(
        resid_kernel, [back_n, beside, across, resid, g_n], vec, True
    )
    resid_2 = swap_tensor(resid_0, 2)
    resid_1 = swap_tensor(resid_0, 1)
    mix_beside = swap_tensor(mix_n[span_rows:], 1)
    mix_near = (mix_2.astype(F32) + swap_tensor(mix_3, 1).astype(F32)).astype(BF16)
    resid_2, mix_near, feed_half = lax.optimization_barrier((resid_2, mix_near, feed_half))
    mix_across = swap_tensor(mix_near, 2)
    feed_parts = scatter_dp(feed_half)

    *backs, weights = attend_back(
        scalars,
        [resid_0, resid_1, resid_2, swap_tensor(resid_2, 1)],
        merge_t,
        heads_t,
        norm_one,
        attn,
        (q_pos, k_pos, v_pos, out_t, lse),
        [vec, resid_sums, up_sum_n, up_sum_2, up_sum_3],
        shard,
        c_size,
        pieces,
    )
    weights, feed_parts, mix_across = lax.optimization_barrier((weights, feed_parts, mix_across))
    unused, beside, across = scatter_tensor(backs)
    tokens_rows, tokens_low = row_wise(
        first_kernel, [backs[0], beside, across, own_rows, grad_resid], vec, False
    )
    if seqs == 1:
        weights = weights[0]
    else:
        weights = jnp.sum(weights.astype(F32), axis=0).astype(BF16)
    heads_half = pick(weights, c_pos).astype(F32)
    for d in range(1, c_size):
        heads_half += rotate(pick(weights, (c_pos + d) % c_size), "ctx", d).astype(F32)
    heads_half = heads_half.astype(BF16)
    heads_own, merge_own, sums = finish_heads(scatter_dp(heads_half), width)
    feed_own = add_all(feed_parts)
    up_own, down_own = feed_own[:, :hidden], feed_own[:, hidden:]
    mixed = add_all([mix_n[:span_rows], mix_beside, mix_across])
    block_rows = (resid + mixed + b_down).astype(BF16)
    block_rows, heads_half = lax.optimization_barrier((block_rows, heads_half))

    sums = add_all([sums] + [rotate(sums, "tensor", d) for d in range(1, t_size)])
    vec_own = sums[:8, :shard]
    up_bias_own = sums[8, : hidden_all // owners]

    def send_back(low, own):
        parts = low.reshape(c_size, seqs, rows, model)
        held = jnp.stack(
            [own.reshape(c_size, seqs, rows, model)[0]]
            + [rotate(parts[d], "ctx", d).astype(own.dtype) for d in range(1, c_size)]
        )
        return jnp.concatenate(
            [pick(held, (c_pos - s) % c_size) for s in range(c_size)], axis=0
        )

    block_out = send_back(block_rows, block_rows)
    tokens_grad = send_back(tokens_low, tokens_rows)
    return (
        block_out,
        tokens_grad,
        vec_own[0],
        vec_own[1],
        heads_own,
        vec_own[2:4],
        merge_own,
        vec_own[4],
        vec_own[5],
        vec_own[6],
        up_own,
        up_bias_own,
        down_own.T,
        vec_own[7],
    )


def solution(mesh):
    both = P(("dp", "ctx"))
    in_specs = (
        P("dp", ("ctx", "tensor"), None),
        P("dp", "ctx", None),
        P("dp", None),
        both,
        both,
        P(None, ("dp", "ctx"), "tensor"),
        P(None, ("dp", "ctx")),
        P("tensor", ("dp", "ctx")),
        both,
        both,
        both,
        P(("dp", "ctx"), "tensor"),
        both,
        P("tensor", ("dp", "ctx")),
        both,
    )
    out_specs = (
        P("dp", ("ctx", "tensor"), None),
        P("dp", ("ctx", "tensor"), None),
        both,
        both,
        P(None, ("dp", "ctx"), "tensor"),
        P(None, ("dp", "ctx")),
        P("tensor", ("dp", "ctx")),
        both,
        both,
        both,
        P(("dp", "ctx"), "tensor"),
        both,
        P("tensor", ("dp", "ctx")),
        both,
    )
    return jax.shard_map(local, mesh=mesh, in_specs=in_specs, out_specs=out_specs, check_vma=False)
```

time: 437 us -> 326 us (0.75)
  Pallas kernels: 52.6 us -> 107 us
  matrix products: 59.3 us -> 7.81 us
  waiting for transfers between devices: 153 us -> 102 us
  local copies, waits for them, and re-layouts: 60.3 us -> 20.4 us
  blocking collectives: 35.8 us -> 0 us
  starting transfers between devices: 21.4 us -> 42.7 us
  other arithmetic: 35.3 us -> 23.6 us
    pallas_call x2 -> x8, Pallas kernels: 52.6 us -> 107 us  [the longest x1 37.3 us: attend_back(): pl.pallas_call(functools.partial(attend_back_kernel, (pieces, heads, shar...]
    ppermute x15 -> x25, waiting for transfers between devices: 94.9 us -> 41.1 us  [swap_tensor(): return lax.ppermute(block, 'tensor', [(i, i ^ bit) for i in range(size)])]
    dot_general x21 -> x2, matrix products: 59.3 us -> 7.81 us  [dot(): lax.dot_general(left, right, (dims, ((), ())), preferred_element_type=F32)]
    all_gather x1 -> x0, blocking collectives: 35.8 us -> none  [local(): first_all = lax.all_gather(first_pack, ('dp', 'ctx'), axis=0, tiled=True)]
    ppermute x11 -> x22, waiting for transfers between devices: 44.4 us -> 61.4 us  [rotate(): lax.ppermute(block, axis, [(i, (i + distance) % size) for i in range(size)])]
    unnamed x99 -> x103, local copies, waits for them, and re-layouts: 20.6 us -> 4.42 us
    ppermute x11 -> x22, starting transfers between devices: 12.4 us -> 28.4 us  [rotate(): lax.ppermute(block, axis, [(i, (i + distance) % size) for i in range(size)])]
    unnamed x3 -> x1, waiting for transfers between devices: 14.1 us -> 0.02 us
  transfers between devices with their start and end apart: 28 -> 48, of which waited for: 16 -> 19; matrix products, arithmetic and copies ran while one was open for 28% -> 13% of each run, Pallas kernels for 12% -> 29%
where the time goes in v2:
time: 326 us; the launch traced here: 319 us
  Pallas kernels  107 us (33%)
  waiting for transfers between devices  102 us (31%)
  starting transfers between devices  42.7 us (13%)
  other arithmetic  23.6 us (7%)
  local copies, waits for them, and re-layouts  20.4 us (6%)
  between operations  15.4 us (5%)
  matrix products  7.81 us (2%)
    ppermute x22, waiting for transfers between devices, rotate(): lax.ppermute(block, axis, [(i, (i + distance) % size) for i in range(size)])  61.4 us
    ppermute x25, waiting for transfers between devices, swap_tensor(): return lax.ppermute(block, 'tensor', [(i, i ^ bit) for i in range(size)])  41.1 us
    pallas_call x1, Pallas kernels, attend_back(): pl.pallas_call(functools.partial(attend_back_kernel, (pieces, heads, shar...  37.3 us
    pallas_call x1, Pallas kernels, attend(): pl.pallas_call(functools.partial(attend_kernel, (pieces, heads, shard, mo...  30.7 us
    ppermute x22, starting transfers between devices, rotate(): lax.ppermute(block, axis, [(i, (i + distance) % size) for i in range(size)])  28.4 us
    pallas_call x3, Pallas kernels, feed(): pl.pallas_call(functools.partial(feed_kernel, seqs, ctx, len(turned) > 0)...  26.2 us
    ppermute x25, starting transfers between devices, swap_tensor(): return lax.ppermute(block, 'tensor', [(i, i ^ bit) for i in range(size)])  14.3 us
    pallas_call x2, Pallas kernels, row_wise(): pl.pallas_call(kernel, grid=(steps,), in_specs=[by_rows] * len(parts) + [...  10.5 us
  transfers between devices with their start and end apart: 48, of which 19 were waited for; matrix products, arithmetic and copies ran while one was open for 13% of the time, Pallas kernels for 29%

profile of v2, /device:TPU:0, one launch (start us, length us, event | category | flops | bytes accessed | tf_op | source)
XLA Modules:
  0.0 319.1 jit_solution(18379785339301656694)
XLA Ops:
  8.7 3.0 collective-permute-start
  12.4 1.6 collective-permute-start.9
  14.0 2.2 collective-permute-start.7
  18.6 2.2 collective-permute-done
  20.9 1.7 collective-permute-start.4
  23.0 1.6 collective-permute-start.10
  25.9 5.5 %collective-permute-done.8 = bf16[112,768]{1,0:T(8,128)(2,1)} collective-permute-done((bf16[112,768]{1,0:T(8,128)(2,1)S(1)}, bf16[112,768]{1,0:T(8,128)(2,1)}, u32[]{:S(2)}, u32[]{:S(2)}) %collective-permute-start.8) | collective-permute-done | bytes 172064 | tf_op jit(solution)/shard_map/ppermute | solution.py:591
  32.4 2.8 collective-permute-done.4.refs_5_
  36.0 2.1 collective-permute-done.11
  40.4 3.9 %collective-permute-done.12 = bf16[112,768]{1,0:T(8,128)(2,1)} collective-permute-done((bf16[112,768]{1,0:T(8,128)(2,1)}, bf16[112,768]{1,0:T(8,128)(2,1)}, u32[]{:S(2)}, u32[]{:S(2)}) %collective-permute-start.12) | collective-permute-done | bytes 172064 | tf_op jit(solution)/shard_map/ppermute | solution.py:591
  45.6 30.7 %attend.1 = (bf16[2048,768]{1,0:T(8,128)(2,1)}, f32[16,768]{1,0:T(8,128)}, bf16[576,768]{1,0:T(8,128)(2,1)}, bf16[768,192]{1,0:T(8,128)(2,1)}, bf16[1,2048,192]{...) custom-call(s32[17]{0:T(128)} %pad_add_fusion.2.scalars.starts, ...), custom_call_target="tpu_custom_call" | custom-call | flops 14495514624 | bytes 37748736 | tf_op jit(solution)/shard_map/attend/pallas_call | solution.py:159
  77.0 2.0 collective-permute-done.16
  80.3 1.5 collective-permute-start.17
  81.8 1.5 slice_reduce_fusion
  83.3 16.6 %collective-permute-done.17 = bf16[512,768]{1,0:T(8,128)(2,1)S(1)} collective-permute-done((bf16[512,768]{1,0:T(8,128)(2,1)S(1)}, bf16[512,768]{1,0:T(8,128)(2,1)S(1)}, u32[]{:S(2)}, u32[]{:S(2)}) %collective-permute-start.17) | collective-permute-done | bytes 786464 | tf_op jit(solution)/shard_map/ppermute | solution.py:586
  103.8 2.4 pad_maximum_fusion.2
  107.4 11.1 %feed.3 = (bf16[1024,768]{1,0:T(8,128)(2,1)}, bf16[1024,768]{1,0:T(8,128)(2,1)}, bf16[1024,768]{1,0:T(8,128)(2,1)}, bf16[1024,768]{1,0:T(8,128)(2,1)}, bf16[1024...) custom-call(s32[8]{0:T(128)} %stack.65.table, ...), custom_call_target="tpu_custom_call" | custom-call | flops 4831838208 | bytes 11010048 | tf_op jit(solution)/shard_map/feed/pallas_call | solution.py:470
  118.6 3.1 collective-permute-done.22.norm
  122.5 7.4 %feed.4 = (bf16[512,768]{1,0:T(8,128)(2,1)}, bf16[512,768]{1,0:T(8,128)(2,1)}, bf16[512,768]{1,0:T(8,128)(2,1)}, bf16[512,768]{1,0:T(8,128)(2,1)}, bf16[512,768]{1,0:T(8,128)(2,1)}, /*index=5*/f32[1,768]{1,0:T(1,128)}) custom-call(s32[4]{0:T(128)} %get-tuple-element.176.table, bf16[512,768]{1,0:T(8,128)(2,1)} %copy-done.12, bf16[8,256,768]{2,1,0:T(8,128)(2,1)} %bitcast.110, ...), custom_call_target="tpu_custom_call" | custom-call | flops 2415919104 | bytes 5505024 | tf_op jit(solution)/shard_map/feed/pallas_call | solution.py:470
  130.8 7.7 %feed.5 = (bf16[512,768]{1,0:T(8,128)(2,1)}, bf16[512,768]{1,0:T(8,128)(2,1)}, bf16[512,768]{1,0:T(8,128)(2,1)}, bf16[512,768]{1,0:T(8,128)(2,1)}, bf16[512,768]{1,0:T(8,128)(2,1)}, /*index=5*/f32[1,768]{1,0:T(1,128)}) custom-call(s32[4]{0:T(128)} %get-tuple-element.177.table, bf16[512,768]{1,0:T(8,128)(2,1)} %copy-done.14, bf16[8,256,768]{2,1,0:T(8,128)(2,1)} %bitcast.111, ...), custom_call_target="tpu_custom_call" | custom-call | flops 2415919104 | bytes 5505024 | tf_op jit(solution)/shard_map/feed/pallas_call | solution.py:470
  138.8 5.0 %fusion.30 = bf16[768,768]{0,1:T(8,128)(2,1)S(1)} fusion(bf16[512,768]{1,0:T(8,128)(2,1)} %get-tuple-element.96, bf16[512,768]{1,0:T(8,128)(2,1)} %get-tuple-element.95, bf16[1024,768]{1,0:T(8,128)(2,1)} %get-tuple-element.94, bf16[512,768]{1,0:T(8,128)(2,1)} %copy-done.14, bf16[512,768]{1,0:T(8,128)(2,1)S(1)} %copy-done.13, ...), kind=kOutput, calls=%fused_computation.43 | convolution fusion | flops 2438529024 | bytes 7471104 | tf_op jit(solution)/shard_map/dot_general | solution.py:35
  144.0 1.5 collective-permute-start.25
  145.6 2.8 fusion.25
  148.4 1.6 pad_maximum_fusion
  150.0 13.9 %collective-permute-done.25.across = bf16[512,768]{1,0:T(8,128)(2,1)} collective-permute-done((bf16[512,768]{1,0:T(8,128)(2,1)S(1)}, bf16[512,768]{1,0:T(8,128)(2,1)}, u32[]{:S(2)}, u32[]{:S(2)}) %collective-permute-start.25) | collective-permute-done | bytes 786464 | tf_op jit(solution)/shard_map/ppermute | solution.py:586
  163.9 2.8 copy.37
  166.9 1.5 collective-permute-start.29
  169.1 2.2 collective-permute-done.21.beside
  171.3 5.3 %row_wise.2 = (f32[512,768]{1,0:T(8,128)}, bf16[512,768]{1,0:T(8,128)(2,1)}, f32[8,768]{1,0:T(8,128)}) custom-call(bf16[1024,768]{1,0:T(8,128)(2,1)} %get-tuple-element.87.own, bf16[512,768]{1,0:T(8,128)(2,1)} %collective-permute-done.21.beside, bf16[512,768]{1,0:T(8,128)(2,1)} %collective-permute-done.25.across, f32[512,768]{1,0:T(8,128)} %copy-done.2, ...), custom_call_target="tpu_custom_call" | custom-call | flops 7864320 | bytes 7077888 | tf_op jit(solution)/shard_map/row_wise/pallas_call | solution.py:542
  176.6 1.6 collective-permute-start.27
  178.1 2.4 add_convert_fusion.2
  180.6 13.9 %collective-permute-done.29 = bf16[4,96,1536]{2,1,0:T(8,128)(2,1)} collective-permute-done((bf16[4,96,1536]{2,1,0:T(8,128)(2,1)S(1)}, bf16[4,96,1536]{2,1,0:T(8,128)(2,1)}, u32[]{:S(2)}, u32[]{:S(2)}) %collective-permute-start.29) | collective-permute-done | bytes 1179680 | tf_op jit(solution)/shard_map/ppermute | solution.py:591
  194.4 1.6 fusion.24
  196.5 2.1 pad_maximum_fusion.4.rows
  201.3 2.0 collective-permute-start.32
  203.3 3.1 collective-permute-start.33
  208.0 37.3 %attend_back.1 = (bf16[512,768]{1,0:T(8,128)(2,1)}, bf16[512,768]{1,0:T(8,128)(2,1)}, bf16[512,768]{1,0:T(8,128)(2,1)}, bf16[512,768]{1,0:T(8,128)(2,1)}, bf16[1,2,4,112,768]{4,3,2,1,0:T(8,128)(2,1)}) custom-call(s32[17]{0:T(128)} %pad_add_fusion.2.scalars.starts, bf16[512,768]{1,0:T(8,128)(2,1)} %get-tuple-element.104.refs_0_, ...), custom_call_target="tpu_custom_call" | custom-call | flops 27179089920 | bytes 37748736 | tf_op jit(solution)/shard_map/attend_back/pallas_call | solution.py:362
  250.5 1.9 add_convert_fusion.1
  252.5 10.5 %collective-permute-done.35 = bf16[4,112,768]{2,1,0:T(8,128)(2,1)S(1)} collective-permute-done((bf16[4,112,768]{2,1,0:T(8,128)(2,1)S(1)}, bf16[4,112,768]{2,1,0:T(8,128)(2,1)S(1)}, u32[]{:S(2)}, u32[]{:S(2)}) %collective-permute-start.35) | collective-permute-done | bytes 688160 | tf_op jit(solution)/shard_map/ppermute | solution.py:591
  264.9 2.9 collective-permute-start.43
  268.6 4.5 %collective-permute-done.41.b = bf16[112,768]{1,0:T(8,128)(2,1)S(1)} collective-permute-done((bf16[112,768]{1,0:T(8,128)(2,1)S(1)}, bf16[112,768]{1,0:T(8,128)(2,1)S(1)}, u32[]{:S(2)}, u32[]{:S(2)}) %collective-permute-start.41) | collective-permute-done | bytes 172064 | tf_op jit(solution)/shard_map/ppermute | solution.py:591
  273.1 4.5 %collective-permute-done.42.c = bf16[112,768]{1,0:T(8,128)(2,1)S(1)} collective-permute-done((bf16[112,768]{1,0:T(8,128)(2,1)S(1)}, bf16[112,768]{1,0:T(8,128)(2,1)S(1)}, u32[]{:S(2)}, u32[]{:S(2)}) %collective-permute-start.42) | collective-permute-done | bytes 172064 | tf_op jit(solution)/shard_map/ppermute | solution.py:591
  278.2 2.0 finish_heads.1
  282.4 2.3 collective-permute-done.44
  288.2 5.7 %collective-permute-done.36 = bf16[1,256,768]{2,1,0:T(8,128)(2,1)S(1)} collective-permute-done((bf16[1,256,768]{2,1,0:T(8,128)(2,1)S(1)}, bf16[1,256,768]{2,1,0:T(8,128)(2,1)S(1)}, u32[]{:S(2)}, u32[]{:S(2)}) %collective-permute-start.36) | collective-permute-done | bytes 393248 | tf_op jit(solution)/shard_map/ppermute | solution.py:591
  295.4 5.2 %row_wise.3 = (f32[512,768]{1,0:T(8,128)}, bf16[512,768]{1,0:T(8,128)(2,1)}) custom-call(bf16[512,768]{1,0:T(8,128)(2,1)} %get-tuple-element.128.own, bf16[512,768]{1,0:T(8,128)(2,1)} %copy-done.15, bf16[512,768]{1,0:T(8,128)(2,1)} %copy-done.16, bf16[512,768]{1,0:T(8,128)(2,1)} %pad_maximum_fusion.4.rows, f32[512,768]{1,0:T(8,128)} %get-tuple-element.132.grad, ...), custom_call_target="tpu_custom_call" | custom-call | flops 7864320 | bytes 7077888 | tf_op jit(solution)/shard_map/row_wise/pallas_call | solution.py:542
  301.7 1.5 collective-permute-start.40
  304.3 5.9 %collective-permute-done.40 = bf16[1,256,768]{2,1,0:T(8,128)(2,1)S(1)} collective-permute-done((bf16[1,256,768]{2,1,0:T(8,128)(2,1)S(1)}, bf16[1,256,768]{2,1,0:T(8,128)(2,1)S(1)}, u32[]{:S(2)}, u32[]{:S(2)}) %collective-permute-start.40) | collective-permute-done | bytes 393248 | tf_op jit(solution)/shard_map/ppermute | solution.py:591
  (236 shorter events, 45.3 us)
Async XLA Ops:
  7.3 100.1 %all-gather.2.cloned.1.call-start = ((), (), s32[]{:S(2)}) async-start(), calls=%async_computation | async-start | bytes 2654208 | tf_op jit(solution)/shard_map/all_gather | solution.py:700
  8.7 12.1 %collective-permute-start = (bf16[1,256,768]{2,1,0:T(8,128)(2,1)S(1)}, bf16[1,256,768]{2,1,0:T(8,128)(2,1)S(1)}, u32[]{:S(2)}, u32[]{:S(2)}) collective-permute-start(bf16[1,256,768]{2,1,0:T(8,128)(2,1)S(1)} %get-tuple-element.158), channel_id=1, source_target_pairs={{0,4},{4,0},{1,5},{5,1},{2,6},{6,2},{3,7},{7,3},{8,12},{12,8},{9,1... | collective-permute-start | bytes 1179656 | tf_op jit(solution)/shard_map/ppermute | solution.py:591
  12.4 10.6 %collective-permute-start.9 = (bf16[112,768]{1,0:T(8,128)(2,1)S(1)}, bf16[112,768]{1,0:T(8,128)(2,1)S(1)}, u32[]{:S(2)}, u32[]{:S(2)}) collective-permute-start(bf16[112,768]{1,0:T(8,128)(2,1)S(1)} %pad_maximum_fusion.7), channel_id=1, source_target_pairs={{0,8},{8,16},{16,24},{24,0},{1,9},{9,17},{17,25},{25,1},{2,10},{10... | collective-permute-start | bytes 516104 | tf_op jit(solution)/shard_map/ppermute | solution.py:591
  14.0 10.6 %collective-permute-start.7 = (bf16[112,768]{1,0:T(8,128)(2,1)S(1)}, bf16[112,768]{1,0:T(8,128)(2,1)S(1)}, u32[]{:S(2)}, u32[]{:S(2)}) collective-permute-start(bf16[112,768]{1,0:T(8,128)(2,1)S(1)} %pad_maximum_fusion.7), channel_id=1, source_target_pairs={{0,24},{8,0},{16,8},{24,16},{1,25},{9,1},{17,9},{25,17},{2,26},{10... | collective-permute-start | bytes 516104 | tf_op jit(solution)/shard_map/ppermute | solution.py:591
  16.3 15.0 %collective-permute-start.8 = (bf16[112,768]{1,0:T(8,128)(2,1)S(1)}, bf16[112,768]{1,0:T(8,128)(2,1)}, u32[]{:S(2)}, u32[]{:S(2)}) collective-permute-start(bf16[112,768]{1,0:T(8,128)(2,1)S(1)} %pad_maximum_fusion.7), channel_id=1, source_target_pairs={{0,16},{8,24},{16,0},{24,8},{1,17},{9,25},{17,1},{25,9},{2,18},{10... | collective-permute-start | bytes 516104 | tf_op jit(solution)/shard_map/ppermute | solution.py:591
  17.1 15.0 %collective-permute-start.3 = (bf16[256,768]{1,0:T(8,128)(2,1)S(1)}, bf16[256,768]{1,0:T(8,128)(2,1)S(1)}, u32[]{:S(2)}, u32[]{:S(2)}) collective-permute-start(bf16[256,768]{1,0:T(8,128)(2,1)S(1)} %get-tuple-element.159.refs_0_), channel_id=1, source_target_pairs={{0,2},{1,3},{2,0},{3,1},{4,6},{5,7},{6,4},{7,5},{8,10},{9,11},{10,... | collective-permute-start | bytes 1179656 | tf_op jit(solution)/shard_map/ppermute | solution.py:586
  20.9 14.3 %collective-permute-start.4 = (bf16[256,768]{1,0:T(8,128)(2,1)S(1)}, bf16[256,768]{1,0:T(8,128)(2,1)S(1)}, u32[]{:S(2)}, u32[]{:S(2)}) collective-permute-start(bf16[256,768]{1,0:T(8,128)(2,1)S(1)} %bitcast.117), channel_id=1, source_target_pairs={{0,2},{1,3},{2,0},{3,1},{4,6},{5,7},{6,4},{7,5},{8,10},{9,11},{10,... | collective-permute-start | bytes 1179656 | tf_op jit(solution)/shard_map/ppermute | solution.py:586
  23.0 8.3 %collective-permute-start.10 = (bf16[112,768]{1,0:T(8,128)(2,1)S(1)}, bf16[112,768]{1,0:T(8,128)(2,1)S(1)}, u32[]{:S(2)}, u32[]{:S(2)}) collective-permute-start(bf16[112,768]{1,0:T(8,128)(2,1)S(1)} %pad_maximum_fusion.7), channel_id=1, source_target_pairs={{0,4},{4,0},{1,5},{5,1},{2,6},{6,2},{3,7},{7,3},{8,12},{12,8},{9,1... | collective-permute-start | bytes 516104 | tf_op jit(solution)/shard_map/ppermute | solution.py:591
  24.6 7.3 %collective-permute-start.13 = (bf16[112,768]{1,0:T(8,128)(2,1)S(1)}, bf16[112,768]{1,0:T(8,128)(2,1)S(1)}, u32[]{:S(2)}, u32[]{:S(2)}) collective-permute-start(bf16[112,768]{1,0:T(8,128)(2,1)S(1)} %collective-permute-done.9), channel_id=1, source_target_pairs={{0,4},{4,0},{1,5},{5,1},{2,6},{6,2},{3,7},{7,3},{8,12},{12,8},{9,1... | collective-permute-start | bytes 516104 | tf_op jit(solution)/shard_map/ppermute | solution.py:591
  31.3 13.6 %collective-permute-start.1 = (bf16[256,768]{1,0:T(8,128)(2,1)S(1)}, bf16[256,768]{1,0:T(8,128)(2,1)S(1)}, u32[]{:S(2)}, u32[]{:S(2)}) collective-permute-start(bf16[256,768]{1,0:T(8,128)(2,1)S(1)} %get-tuple-element.159.refs_0_), channel_id=1, source_target_pairs={{0,1},{1,0},{2,3},{3,2},{4,5},{5,4},{6,7},{7,6},{8,9},{9,8},{10,11... | collective-permute-start | bytes 1179656 | tf_op jit(solution)/shard_map/ppermute | solution.py:586
  31.3 6.8 %collective-permute-start.11 = (bf16[112,768]{1,0:T(8,128)(2,1)S(1)}, bf16[112,768]{1,0:T(8,128)(2,1)S(1)}, u32[]{:S(2)}, u32[]{:S(2)}) collective-permute-start(bf16[112,768]{1,0:T(8,128)(2,1)S(1)} %collective-permute-done.7), channel_id=1, source_target_pairs={{0,4},{4,0},{1,5},{5,1},{2,6},{6,2},{3,7},{7,3},{8,12},{12,8},{9,1... | collective-permute-start | bytes 516104 | tf_op jit(solution)/shard_map/ppermute | solution.py:591
  31.9 13.0 %collective-permute-start.2 = (bf16[256,768]{1,0:T(8,128)(2,1)S(1)}, bf16[256,768]{1,0:T(8,128)(2,1)}, u32[]{:S(2)}, u32[]{:S(2)}) collective-permute-start(bf16[256,768]{1,0:T(8,128)(2,1)S(1)} %bitcast.118), channel_id=1, source_target_pairs={{0,1},{1,0},{2,3},{3,2},{4,5},{5,4},{6,7},{7,6},{8,9},{9,8},{10,11... | collective-permute-start | bytes 1179656 | tf_op jit(solution)/shard_map/ppermute | solution.py:586
  32.1 12.8 %collective-permute-start.5 = (bf16[256,768]{1,0:T(8,128)(2,1)S(1)}, bf16[256,768]{1,0:T(8,128)(2,1)}, u32[]{:S(2)}, u32[]{:S(2)}) collective-permute-start(bf16[256,768]{1,0:T(8,128)(2,1)S(1)} %collective-permute-done.3.refs_4_), channel_id=1, source_target_pairs={{0,1},{1,0},{2,3},{3,2},{4,5},{5,4},{6,7},{7,6},{8,9},{9,8},{10,11... | collective-permute-start | bytes 1179656 | tf_op jit(solution)/shard_map/ppermute | solution.py:586
  35.2 9.7 %collective-permute-start.6 = (bf16[256,768]{1,0:T(8,128)(2,1)S(1)}, bf16[256,768]{1,0:T(8,128)(2,1)}, u32[]{:S(2)}, u32[]{:S(2)}) collective-permute-start(bf16[256,768]{1,0:T(8,128)(2,1)S(1)} %collective-permute-done.4.refs_5_), channel_id=1, source_target_pairs={{0,1},{1,0},{2,3},{3,2},{4,5},{5,4},{6,7},{7,6},{8,9},{9,8},{10,11... | collective-permute-start | bytes 1179656 | tf_op jit(solution)/shard_map/ppermute | solution.py:586
  38.1 6.2 %collective-permute-start.12 = (bf16[112,768]{1,0:T(8,128)(2,1)}, bf16[112,768]{1,0:T(8,128)(2,1)}, u32[]{:S(2)}, u32[]{:S(2)}) collective-permute-start(bf16[112,768]{1,0:T(8,128)(2,1)} %collective-permute-done.8), channel_id=1, source_target_pairs={{0,4},{4,0},{1,5},{5,1},{2,6},{6,2},{3,7},{7,3},{8,12},{12,8},{9,1... | collective-permute-start | bytes 516104 | tf_op jit(solution)/shard_map/ppermute | solution.py:591
  44.3 32.0 %collective-permute-start.15 = (bf16[1,2,256,768]{3,2,1,0:T(8,128)(2,1)S(1)}, bf16[1,2,256,768]{3,2,1,0:T(8,128)(2,1)S(1)}, u32[]{:S(2)}, u32[]{:S(2)}) collective-permute-start(bf16[1,2,256,768]{3,2,1,0:T(8,128)(2,1)S(1)} %dynamic-slice_bitcast_fusion.1), channel_id=1, source_target_pairs={{0,4},{4,0},{1,5},{5,1},{2,6},{6,2},{3,7},{7,3},{8,12},{12,8},{9,1... | collective-permute-start | bytes 2359304 | tf_op jit(solution)/shard_map/ppermute | solution.py:591
  76.4 2.6 collective-permute-start.16
  76.5 6.8 %collective-permute-start.14 = (bf16[512,768]{1,0:T(8,128)(2,1)}, bf16[512,768]{1,0:T(8,128)(2,1)S(1)}, u32[]{:S(2)}, u32[]{:S(2)}) collective-permute-start(bf16[512,768]{1,0:T(8,128)(2,1)} %get-tuple-element.79), channel_id=1, source_target_pairs={{0,1},{1,0},{2,3},{3,2},{4,5},{5,4},{6,7},{7,6},{8,9},{9,8},{10,11... | collective-permute-start | bytes 2359304 | tf_op jit(solution)/shard_map/ppermute | solution.py:586
  80.3 19.6 %collective-permute-start.17 = (bf16[512,768]{1,0:T(8,128)(2,1)S(1)}, bf16[512,768]{1,0:T(8,128)(2,1)S(1)}, u32[]{:S(2)}, u32[]{:S(2)}) collective-permute-start(bf16[512,768]{1,0:T(8,128)(2,1)S(1)} %add_convert_fusion.5), channel_id=1, source_target_pairs={{0,2},{1,3},{2,0},{3,1},{4,6},{5,7},{6,4},{7,5},{8,10},{9,11},{10,... | collective-permute-start | bytes 2359304 | tf_op jit(solution)/shard_map/ppermute | solution.py:586
  81.8 22.0 %collective-permute-start.19 = (bf16[1,1,2,256,768]{4,3,2,1,0:T(8,128)(2,1)S(1)}, bf16[1,1,2,256,768]{4,3,2,1,0:T(8,128)(2,1)}, u32[]{:S(2)}, u32[]{:S(2)}) collective-permute-start(bf16[1,1,2,256,768]{4,3,2,1,0:T(8,128)(2,1)S(1)} %bitcast.122), channel_id=1, source_target_pairs={{0,1},{1,0},{2,3},{3,2},{4,5},{5,4},{6,7},{7,6},{8,9},{9,8},{10,11... | collective-permute-start | bytes 2359304 | tf_op jit(solution)/shard_map/ppermute | solution.py:586
  101.7 4.5 %collective-permute-start.18 = (bf16[512,768]{1,0:T(8,128)(2,1)S(1)}, bf16[512,768]{1,0:T(8,128)(2,1)S(1)}, u32[]{:S(2)}, u32[]{:S(2)}) collective-permute-start(bf16[512,768]{1,0:T(8,128)(2,1)S(1)} %add_convert_fusion.4), channel_id=1, source_target_pairs={{0,1},{1,0},{2,3},{3,2},{4,5},{5,4},{6,7},{7,6},{8,9},{9,8},{10,11... | collective-permute-start | bytes 2359304 | tf_op jit(solution)/shard_map/ppermute | solution.py:586
  101.7 20.0 %collective-permute-start.22 = (bf16[512,768]{1,0:T(8,128)(2,1)S(1)}, bf16[512,768]{1,0:T(8,128)(2,1)S(1)}, u32[]{:S(2)}, u32[]{:S(2)}) collective-permute-start(bf16[512,768]{1,0:T(8,128)(2,1)S(1)} %add_convert_fusion.4), channel_id=1, source_target_pairs={{0,2},{1,3},{2,0},{3,1},{4,6},{5,7},{6,4},{7,5},{8,10},{9,11},{10,... | collective-permute-start | bytes 2359304 | tf_op jit(solution)/shard_map/ppermute | solution.py:586
  121.7 8.3 %collective-permute-start.23 = (bf16[512,768]{1,0:T(8,128)(2,1)S(1)}, bf16[512,768]{1,0:T(8,128)(2,1)S(1)}, u32[]{:S(2)}, u32[]{:S(2)}) collective-permute-start(bf16[512,768]{1,0:T(8,128)(2,1)S(1)} %collective-permute-done.22.norm), channel_id=1, source_target_pairs={{0,1},{1,0},{2,3},{3,2},{4,5},{5,4},{6,7},{7,6},{8,9},{9,8},{10,11... | collective-permute-start | bytes 2359304 | tf_op jit(solution)/shard_map/ppermute | solution.py:586
  138.5 5.3 %collective-permute-start.24 = (bf16[512,768]{1,0:T(8,128)(2,1)}, bf16[512,768]{1,0:T(8,128)(2,1)S(1)}, u32[]{:S(2)}, u32[]{:S(2)}) collective-permute-start(bf16[512,768]{1,0:T(8,128)(2,1)} %get-tuple-element.93), channel_id=1, source_target_pairs={{0,1},{1,0},{2,3},{3,2},{4,5},{5,4},{6,7},{7,6},{8,9},{9,8},{10,11... | collective-permute-start | bytes 2359304 | tf_op jit(solution)/shard_map/ppermute | solution.py:586
  144.0 19.9 %collective-permute-start.25 = (bf16[512,768]{1,0:T(8,128)(2,1)S(1)}, bf16[512,768]{1,0:T(8,128)(2,1)}, u32[]{:S(2)}, u32[]{:S(2)}) collective-permute-start(bf16[512,768]{1,0:T(8,128)(2,1)S(1)} %add_convert_fusion.3), channel_id=1, source_target_pairs={{0,2},{1,3},{2,0},{3,1},{4,6},{5,7},{6,4},{7,5},{8,10},{9,11},{10,... | collective-permute-start | bytes 2359304 | tf_op jit(solution)/shard_map/ppermute | solution.py:586
  166.9 27.5 %collective-permute-start.29 = (bf16[4,96,1536]{2,1,0:T(8,128)(2,1)S(1)}, bf16[4,96,1536]{2,1,0:T(8,128)(2,1)}, u32[]{:S(2)}, u32[]{:S(2)}) collective-permute-start(bf16[4,96,1536]{2,1,0:T(8,128)(2,1)S(1)} %dynamic-slice_bitcast_fusion), channel_id=1, source_target_pairs={{0,4},{4,0},{1,5},{5,1},{2,6},{6,2},{3,7},{7,3},{8,12},{12,8},{9,1... | collective-permute-start | bytes 3538952 | tf_op jit(solution)/shard_map/ppermute | solution.py:591
  168.5 2.8 collective-permute-start.21
  168.6 9.6 %collective-permute-start.28 = (bf16[512,768]{1,0:T(8,128)(2,1)}, bf16[512,768]{1,0:T(8,128)(2,1)}, u32[]{:S(2)}, u32[]{:S(2)}) collective-permute-start(bf16[512,768]{1,0:T(8,128)(2,1)} %get-tuple-element.106), channel_id=1, source_target_pairs={{0,1},{1,0},{2,3},{3,2},{4,5},{5,4},{6,7},{7,6},{8,9},{9,8},{10,11... | collective-permute-start | bytes 2359304 | tf_op jit(solution)/shard_map/ppermute | solution.py:586
  176.6 20.0 %collective-permute-start.27 = (bf16[512,768]{1,0:T(8,128)(2,1)}, bf16[512,768]{1,0:T(8,128)(2,1)}, u32[]{:S(2)}, u32[]{:S(2)}) collective-permute-start(bf16[512,768]{1,0:T(8,128)(2,1)} %get-tuple-element.104.refs_0_), channel_id=1, source_target_pairs={{0,2},{1,3},{2,0},{3,1},{4,6},{5,7},{6,4},{7,5},{8,10},{9,11},{10,... | collective-permute-start | bytes 2359304 | tf_op jit(solution)/shard_map/ppermute | solution.py:586
  180.6 22.8 %collective-permute-start.26 = (bf16[512,768]{1,0:T(8,128)(2,1)}, bf16[512,768]{1,0:T(8,128)(2,1)}, u32[]{:S(2)}, u32[]{:S(2)}) collective-permute-start(bf16[512,768]{1,0:T(8,128)(2,1)} %get-tuple-element.104.refs_0_), channel_id=1, source_target_pairs={{0,1},{1,0},{2,3},{3,2},{4,5},{5,4},{6,7},{7,6},{8,9},{9,8},{10,11... | collective-permute-start | bytes 2359304 | tf_op jit(solution)/shard_map/ppermute | solution.py:586
  196.5 9.9 %collective-permute-start.30 = (bf16[512,768]{1,0:T(8,128)(2,1)}, bf16[512,768]{1,0:T(8,128)(2,1)}, u32[]{:S(2)}, u32[]{:S(2)}) collective-permute-start(bf16[512,768]{1,0:T(8,128)(2,1)} %collective-permute-done.27.refs_2_), channel_id=1, source_target_pairs={{0,1},{1,0},{2,3},{3,2},{4,5},{5,4},{6,7},{7,6},{8,9},{9,8},{10,11... | collective-permute-start | bytes 2359304 | tf_op jit(solution)/shard_map/ppermute | solution.py:586
  199.6 50.9 %collective-permute-start.20 = (bf16[512,768]{1,0:T(8,128)(2,1)}, bf16[512,768]{1,0:T(8,128)(2,1)}, u32[]{:S(2)}, u32[]{:S(2)}) collective-permute-start(bf16[512,768]{1,0:T(8,128)(2,1)} %slice.107), channel_id=1, source_target_pairs={{0,1},{1,0},{2,3},{3,2},{4,5},{5,4},{6,7},{7,6},{8,9},{9,8},{10,11... | collective-permute-start | bytes 2359304 | tf_op jit(solution)/shard_map/ppermute | solution.py:586
  201.0 44.2 %collective-permute-start.31 = (bf16[96,1536]{1,0:T(8,128)(2,1)}, bf16[96,1536]{1,0:T(8,128)(2,1)S(1)}, u32[]{:S(2)}, u32[]{:S(2)}) collective-permute-start(bf16[96,1536]{1,0:T(8,128)(2,1)} %get-tuple-element.152), channel_id=1, source_target_pairs={{0,8},{8,16},{16,24},{24,0},{1,9},{9,17},{17,25},{25,1},{2,10},{10... | collective-permute-start | bytes 884744 | tf_op jit(solution)/shard_map/ppermute | solution.py:591
  201.3 43.9 %collective-permute-start.32 = (bf16[96,1536]{1,0:T(8,128)(2,1)}, bf16[96,1536]{1,0:T(8,128)(2,1)S(1)}, u32[]{:S(2)}, u32[]{:S(2)}) collective-permute-start(bf16[96,1536]{1,0:T(8,128)(2,1)} %get-tuple-element.151), channel_id=1, source_target_pairs={{0,16},{8,24},{16,0},{24,8},{1,17},{9,25},{17,1},{25,9},{2,18},{10... | collective-permute-start | bytes 884744 | tf_op jit(solution)/shard_map/ppermute | solution.py:591
  203.3 41.9 %collective-permute-start.33 = (bf16[96,1536]{1,0:T(8,128)(2,1)}, bf16[96,1536]{1,0:T(8,128)(2,1)}, u32[]{:S(2)}, u32[]{:S(2)}) collective-permute-start(bf16[96,1536]{1,0:T(8,128)(2,1)} %get-tuple-element.150), channel_id=1, source_target_pairs={{0,24},{8,0},{16,8},{24,16},{1,25},{9,1},{17,9},{25,17},{2,26},{10... | collective-permute-start | bytes 884744 | tf_op jit(solution)/shard_map/ppermute | solution.py:591
  206.5 38.8 %collective-permute-start.34 = (bf16[512,768]{1,0:T(8,128)(2,1)S(1)}, bf16[512,768]{1,0:T(8,128)(2,1)S(1)}, u32[]{:S(2)}, u32[]{:S(2)}) collective-permute-start(bf16[512,768]{1,0:T(8,128)(2,1)S(1)} %copy-done.18), channel_id=1, source_target_pairs={{0,2},{1,3},{2,0},{3,1},{4,6},{5,7},{6,4},{7,5},{8,10},{9,11},{10,... | collective-permute-start | bytes 2359304 | tf_op jit(solution)/shard_map/ppermute | solution.py:586
  246.7 16.3 %collective-permute-start.35 = (bf16[4,112,768]{2,1,0:T(8,128)(2,1)S(1)}, bf16[4,112,768]{2,1,0:T(8,128)(2,1)S(1)}, u32[]{:S(2)}, u32[]{:S(2)}) collective-permute-start(bf16[4,112,768]{2,1,0:T(8,128)(2,1)S(1)} %dynamic-slice_bitcast_fusion.2), channel_id=1, source_target_pairs={{0,4},{4,0},{1,5},{5,1},{2,6},{6,2},{3,7},{7,3},{8,12},{12,8},{9,1... | collective-permute-start | bytes 2064392 | tf_op jit(solution)/shard_map/ppermute | solution.py:591
  248.0 19.7 %collective-permute-start.38 = (bf16[512,768]{1,0:T(8,128)(2,1)}, bf16[512,768]{1,0:T(8,128)(2,1)S(1)}, u32[]{:S(2)}, u32[]{:S(2)}) collective-permute-start(bf16[512,768]{1,0:T(8,128)(2,1)} %get-tuple-element.131), channel_id=1, source_target_pairs={{0,1},{1,0},{2,3},{3,2},{4,5},{5,4},{6,7},{7,6},{8,9},{9,8},{10,11... | collective-permute-start | bytes 2359304 | tf_op jit(solution)/shard_map/ppermute | solution.py:586
  250.0 44.2 %collective-permute-start.37 = (bf16[512,768]{1,0:T(8,128)(2,1)}, bf16[512,768]{1,0:T(8,128)(2,1)S(1)}, u32[]{:S(2)}, u32[]{:S(2)}) collective-permute-start(bf16[512,768]{1,0:T(8,128)(2,1)} %get-tuple-element.129), channel_id=1, source_target_pairs={{0,1},{1,0},{2,3},{3,2},{4,5},{5,4},{6,7},{7,6},{8,9},{9,8},{10,11... | collective-permute-start | bytes 2359304 | tf_op jit(solution)/shard_map/ppermute | solution.py:586
  263.9 9.2 %collective-permute-start.41 = (bf16[112,768]{1,0:T(8,128)(2,1)S(1)}, bf16[112,768]{1,0:T(8,128)(2,1)S(1)}, u32[]{:S(2)}, u32[]{:S(2)}) collective-permute-start(bf16[112,768]{1,0:T(8,128)(2,1)S(1)} %get-tuple-element.162), channel_id=1, source_target_pairs={{0,8},{8,16},{16,24},{24,0},{1,9},{9,17},{17,25},{25,1},{2,10},{10... | collective-permute-start | bytes 516104 | tf_op jit(solution)/shard_map/ppermute | solution.py:591
  263.9 13.6 %collective-permute-start.42 = (bf16[112,768]{1,0:T(8,128)(2,1)S(1)}, bf16[112,768]{1,0:T(8,128)(2,1)S(1)}, u32[]{:S(2)}, u32[]{:S(2)}) collective-permute-start(bf16[112,768]{1,0:T(8,128)(2,1)S(1)} %get-tuple-element.161), channel_id=1, source_target_pairs={{0,16},{8,24},{16,0},{24,8},{1,17},{9,25},{17,1},{25,9},{2,18},{10... | collective-permute-start | bytes 516104 | tf_op jit(solution)/shard_map/ppermute | solution.py:591
  264.9 12.7 %collective-permute-start.43 = (bf16[112,768]{1,0:T(8,128)(2,1)S(1)}, bf16[112,768]{1,0:T(8,128)(2,1)}, u32[]{:S(2)}, u32[]{:S(2)}) collective-permute-start(bf16[112,768]{1,0:T(8,128)(2,1)S(1)} %get-tuple-element.160), channel_id=1, source_target_pairs={{0,24},{8,0},{16,8},{24,16},{1,25},{9,1},{17,9},{25,17},{2,26},{10... | collective-permute-start | bytes 516104 | tf_op jit(solution)/shard_map/ppermute | solution.py:591
  268.0 26.2 %collective-permute-start.39 = (bf16[512,768]{1,0:T(8,128)(2,1)S(1)}, bf16[512,768]{1,0:T(8,128)(2,1)S(1)}, u32[]{:S(2)}, u32[]{:S(2)}) collective-permute-start(bf16[512,768]{1,0:T(8,128)(2,1)S(1)} %add_convert_fusion), channel_id=1, source_target_pairs={{0,2},{1,3},{2,0},{3,1},{4,6},{5,7},{6,4},{7,5},{8,10},{9,11},{10,... | collective-permute-start | bytes 2359304 | tf_op jit(solution)/shard_map/ppermute | solution.py:586
  280.3 4.3 %collective-permute-start.44 = (f32[16,768]{1,0:T(8,128)}, f32[16,768]{1,0:T(8,128)S(1)}, u32[]{:S(2)}, u32[]{:S(2)}) collective-permute-start(f32[16,768]{1,0:T(8,128)} %get-tuple-element.135), channel_id=1, source_target_pairs={{0,1},{1,2},{2,3},{3,0},{4,5},{5,6},{6,7},{7,4},{8,9},{9,10},{10,1... | collective-permute-start | bytes 147464 | tf_op jit(solution)/shard_map/ppermute | solution.py:591
  280.3 6.2 %collective-permute-start.45 = (f32[16,768]{1,0:T(8,128)}, f32[16,768]{1,0:T(8,128)S(1)}, u32[]{:S(2)}, u32[]{:S(2)}) collective-permute-start(f32[16,768]{1,0:T(8,128)} %get-tuple-element.135), channel_id=1, source_target_pairs={{0,2},{1,3},{2,0},{3,1},{4,6},{5,7},{6,4},{7,5},{8,10},{9,11},{10,... | collective-permute-start | bytes 147464 | tf_op jit(solution)/shard_map/ppermute | solution.py:591
  280.9 5.6 %collective-permute-start.46 = (f32[16,768]{1,0:T(8,128)}, f32[16,768]{1,0:T(8,128)S(1)}, u32[]{:S(2)}, u32[]{:S(2)}) collective-permute-start(f32[16,768]{1,0:T(8,128)} %get-tuple-element.135), channel_id=1, source_target_pairs={{0,3},{1,0},{2,1},{3,2},{4,7},{5,4},{6,5},{7,6},{8,11},{9,8},{10,9... | collective-permute-start | bytes 147464 | tf_op jit(solution)/shard_map/ppermute | solution.py:591
  284.6 9.3 %collective-permute-start.36 = (bf16[1,256,768]{2,1,0:T(8,128)(2,1)S(1)}, bf16[1,256,768]{2,1,0:T(8,128)(2,1)S(1)}, u32[]{:S(2)}, u32[]{:S(2)}) collective-permute-start(bf16[1,256,768]{2,1,0:T(8,128)(2,1)S(1)} %get-tuple-element.156), channel_id=1, source_target_pairs={{0,4},{4,0},{1,5},{5,1},{2,6},{6,2},{3,7},{7,3},{8,12},{12,8},{9,1... | collective-permute-start | bytes 1179656 | tf_op jit(solution)/shard_map/ppermute | solution.py:591
  301.7 8.4 %collective-permute-start.40 = (bf16[1,256,768]{2,1,0:T(8,128)(2,1)S(1)}, bf16[1,256,768]{2,1,0:T(8,128)(2,1)S(1)}, u32[]{:S(2)}, u32[]{:S(2)}) collective-permute-start(bf16[1,256,768]{2,1,0:T(8,128)(2,1)S(1)} %slice_bitcast_fusion.1), channel_id=1, source_target_pairs={{0,4},{4,0},{1,5},{5,1},{2,6},{6,2},{3,7},{7,3},{8,12},{12,8},{9,1... | collective-permute-start | bytes 1179656 | tf_op jit(solution)/shard_map/ppermute | solution.py:591
  (51 other events, 400.8 us)
Sparse Core Ops, SparseCore 0:
  40.5 54.8 all-gather.1
